TPU v7x, 256 devices: a whole 4x4x8 slice. The times are simulated.
256 devices in a mesh: dp: 8 (over y, core), ctx: 16 (over z, x_hi), tp: 2 (over x_lo).
Axes of the slice: x: 4 (x_hi: 2, x_lo: 2; x = x_hi * 2 + x_lo), y: 4, z: 8, core: 2. Of those that a mesh axis runs over, the one named last changes fastest.
Arguments:
- queries: bfloat16 [32, 1024, 2048], P('dp', 'ctx', 'tp'), may hold values from -8 to 8
- key_states: bfloat16 [32, 1024, 1024], P('dp', 'ctx', 'tp'), may hold values from -8 to 8
- value_state_rows: bfloat16 [32, 1024, 1024], P('dp', 'ctx', 'tp'), may hold values from -6 to 6
- segment_ids: int32 [32, 1024], P('dp', 'ctx'), may hold values from 0 to 3, never falling along the last dimension, each value on 1 to 512 neighbouring positions
- output_grad: bfloat16 [32, 1024, 3584], P('dp', 'ctx', 'tp'), may hold values from -6 to 6
- out_weight: bfloat16 [2048, 3584], P('tp'), may hold values from -0.09375 to 0.09375
- destination: int32 [32], replicated, may hold values from 0 to 31, as said below
Outputs:
- query_out: bfloat16 [32, 1024, 2048], P('dp', 'ctx', 'tp')
- key_out: bfloat16 [32, 1024, 1024], P('dp', 'ctx', 'tp')
- value_out: bfloat16 [32, 1024, 1024], P('dp', 'ctx', 'tp')
Inputs may be any that keep to these rules, and one draw needn't show every extreme that they name: `segment_ids`: ids never fall along a row; each document holds 1 to 512 positions, some document exactly 512. `destination`: a permutation of the rows; rows r // 4 == g form data group g, and the 4 rows of one group go to 4 different groups.
All inputs are finite; a program needn't handle non-finite values.
Results may differ from a plain program's by a relative error of at most 0.015.
Values may be sent and summed in bfloat16 or wider, within the bound.
No kernel may reach another device: no remote copies, remote signals or barrier semaphores. Data moves between devices by JAX's collectives and lax.ppermute only.
A program may use at most 128 MiB of HBM per device.

v0:
```python
import jax
import jax.numpy as jnp
from jax import lax
from jax.sharding import PartitionSpec as P

HEAD_SIZE = 256


logit_cap = 50.0
score_scale = 0.0625


def as_bf16(values_f32):
    return lax.optimization_barrier(values_f32.astype(jnp.bfloat16))


def pick(onehot, source_data):
    flattened = source_data.reshape(source_data.shape[0], -1)
    chosen = lax.dot_general(
        onehot.astype(source_data.dtype),
        flattened,
        (((1,), (0,)), ((), ())),
        preferred_element_type=jnp.float32,
    )
    return chosen.astype(source_data.dtype).reshape((onehot.shape[0],) + source_data.shape[1:])


def local_gradients(queries, key_states, value_state_rows, segment_ids, output_grad, out_weight):
    row_count, block_len, query_width = queries.shape
    kv_width = key_states.shape[2]
    kv_heads = kv_width // HEAD_SIZE
    query_group_size = query_width // HEAD_SIZE // kv_heads
    attention_gradient = lax.dot_general(
        lax.all_gather(output_grad, "tp", axis=2, tiled=True),
        out_weight,
        (((2,), (1,)), ((), ())),
        preferred_element_type=jnp.float32,
    ).astype(jnp.bfloat16)
    all_keys, all_values, all_segments = (
        lax.all_gather(key_states, "ctx", axis=1, tiled=True),
        lax.all_gather(value_state_rows, "ctx", axis=1, tiled=True),
        lax.all_gather(segment_ids, "ctx", axis=1, tiled=True),
    )
    length = all_keys.shape[1]
    ctx_place = lax.axis_index("ctx")
    positions = ctx_place * block_len + jnp.arange(block_len, dtype=jnp.int32)
    key_index = jnp.arange(length, dtype=jnp.int32)
    allowed = (segment_ids[:, :, None] == all_segments[:, None, :]) & (
        key_index[None, None, :] <= positions[None, :, None]
    )
    allowed = allowed[:, None, None]
    query_head_rows = queries.reshape(row_count, block_len, kv_heads, query_group_size, HEAD_SIZE)
    head_gradients = attention_gradient.reshape(
        row_count, block_len, kv_heads, query_group_size, HEAD_SIZE
    )
    key_head_rows = all_keys.reshape(row_count, length, kv_heads, HEAD_SIZE)
    value_head_rows = all_values.reshape(row_count, length, kv_heads, HEAD_SIZE)
    raw_scores = (
        jnp.einsum(
            "rckgd,rlkd->rkgcl", query_head_rows, key_head_rows, preferred_element_type=jnp.float32
        )
        * score_scale
    )
    capped = logit_cap * jnp.tanh(raw_scores / logit_cap)
    exponent_terms = jnp.where(allowed, jnp.exp(capped), 0.0)
    exp_total = jnp.sum(exponent_terms, axis=-1)
    unnorm = jnp.einsum(
        "rkgcl,rlkd->rckgd",
        as_bf16(exponent_terms),
        value_head_rows,
        preferred_element_type=jnp.float32,
    )
    attn_out = unnorm / jnp.transpose(exp_total, (0, 3, 1, 2))[..., None]
    row_delta = jnp.sum(head_gradients.astype(jnp.float32) * attn_out, axis=-1)
    attn_prob = jnp.where(allowed, jnp.exp(capped - jnp.log(exp_total)[..., None]), 0.0)
    prob_grad = jnp.einsum(
        "rckgd,rlkd->rkgcl", head_gradients, value_head_rows, preferred_element_type=jnp.float32
    )
    score_grad = attn_prob * (prob_grad - jnp.transpose(row_delta, (0, 2, 3, 1))[..., None])
    raw_grad = as_bf16(score_grad * (1.0 - (capped / logit_cap) ** 2) * score_scale)
    prob_low = as_bf16(attn_prob)
    query_grad = jnp.einsum(
        "rkgcl,rlkd->rckgd", raw_grad, key_head_rows, preferred_element_type=jnp.float32
    )
    query_grad = query_grad.astype(jnp.bfloat16).reshape(row_count, block_len, query_width)
    key_part = jnp.einsum(
        "rkgcl,rckgd->rlkd", raw_grad, query_head_rows, preferred_element_type=jnp.float32
    ).reshape(row_count, length, kv_width)
    value_part = jnp.einsum(
        "rkgcl,rckgd->rlkd", prob_low, head_gradients, preferred_element_type=jnp.float32
    ).reshape(row_count, length, kv_width)
    key_sum, value_sum = (
        lax.psum_scatter(
            key_part.astype(jnp.bfloat16), "ctx", scatter_dimension=1, tiled=True
        ).astype(jnp.float32),
        lax.psum_scatter(
            value_part.astype(jnp.bfloat16), "ctx", scatter_dimension=1, tiled=True
        ).astype(jnp.float32),
    )
    key_grad = key_sum.astype(jnp.bfloat16)
    value_grad = value_sum.astype(jnp.bfloat16)
    return (query_grad, key_grad, value_grad)


def on_device(
    queries, key_states, value_state_rows, segment_ids, output_grad, out_weight, destination
):
    row_count = queries.shape[0]
    group_count = lax.axis_size("dp")
    my_group = lax.axis_index("dp")
    own_targets = lax.dynamic_slice_in_dim(destination, my_group * row_count, row_count, 0)
    group_index = jnp.arange(group_count, dtype=jnp.int32)
    send_onehot = (own_targets[None, :] // row_count == group_index[:, None]).astype(jnp.int32)
    wanted = my_group * row_count + jnp.arange(row_count, dtype=jnp.int32)
    all_index = jnp.arange(destination.shape[0], dtype=jnp.int32)
    sources = jnp.sum(
        jnp.where(destination[None, :] == wanted[:, None], all_index[None, :], 0), axis=1
    )
    recv_onehot = (sources[:, None] // row_count == group_index[None, :]).astype(jnp.int32)
    query_grad, key_grad, value_grad = local_gradients(
        queries, key_states, value_state_rows, segment_ids, output_grad, out_weight
    )
    arrived = (
        lax.all_to_all(
            pick(send_onehot, query_grad), "dp", split_axis=0, concat_axis=0, tiled=True
        ),
        lax.all_to_all(pick(send_onehot, key_grad), "dp", split_axis=0, concat_axis=0, tiled=True),
        lax.all_to_all(
            pick(send_onehot, value_grad), "dp", split_axis=0, concat_axis=0, tiled=True
        ),
    )
    query_out = pick(recv_onehot, arrived[0])
    key_out = pick(recv_onehot, arrived[1])
    value_out = pick(recv_onehot, arrived[2])
    return (query_out, key_out, value_out)


def solution(mesh):
    in_specs = (
        P("dp", "ctx", "tp"),
        P("dp", "ctx", "tp"),
        P("dp", "ctx", "tp"),
        P("dp", "ctx"),
        P("dp", "ctx", "tp"),
        P("tp", None),
        P(),
    )
    out_specs = (P("dp", "ctx", "tp"), P("dp", "ctx", "tp"), P("dp", "ctx", "tp"))
    return jax.shard_map(
        on_device, mesh=mesh, in_specs=in_specs, out_specs=out_specs, check_vma=False
    )
```

profile of v0, /device:TPU:1, one launch (start us, length us, event | category | flops | bytes accessed | tf_op | source)
XLA Modules:
  0.0 728.6 jit_solution(1827405901905526770)
XLA Ops:
  7.2 0.0 all-gather.7.cloned.1.call-start
  7.2 0.7 all-gather.7.cloned.1.call-update
  7.9 0.0 all-gather.5.cloned.1.call-start
  7.9 1.9 copy.51
  9.8 0.0 all-gather.5.cloned.1.call-update
  9.8 0.0 all-gather.9.cloned.1.call-start
  9.9 1.9 copy.55
  11.7 0.0 all-gather.9.cloned.1.call-update
  11.8 0.0 reduce-scatter.3.cloned.1.call-start
  11.8 38.4 %all-gather = s32[16,64,4]{1,2,0:T(4,128)S(1)} all-gather(s32[1,64,4]{1,2,0:T(4,128)} %bitcast.138), channel_id=1, replica_groups=mesh['dp'=8,'ctx'=16,'tp'=2] {'ctx'}, dimensions={0}, use_global_device_ids=true | all-gather | bytes 17408 | tf_op jit(solution)/shard_map/all_gather | solution.py:42
  50.2 0.1 reshape.166
  50.3 1.4 reshape.151
  51.7 0.1 iota_compare_fusion
  51.8 0.9 compare_and_fusion
  52.7 0.0 all-gather.7.cloned.1.call-done
  52.8 5.7 fusion.11
  58.5 0.4 reshape.152
  58.9 91.3 %all-gather.5.cloned.1.call-done = bf16[4,1024,512]{2,0,1:T(4,128)(2,1)} async-done(((bf16[4,64,512]{2,0,1:T(4,128)(2,1)}), bf16[4,1024,512]{2,0,1:T(4,128)(2,1)}) %all-gather.5.cloned.1.call-update) | async-done | bytes 4194320 | tf_op jit(solution)/shard_map/all_gather | solution.py:40
  150.2 7.5 %copy.52 = bf16[4,1024,512]{1,2,0:T(8,128)(2,1)} copy(bf16[4,1024,512]{2,0,1:T(4,128)(2,1)} %all-gather.5.cloned.1.call-done) | data formatting | bytes 8388608 | tf_op jit(solution)/shard_map/all_gather | solution.py:40
  157.7 4.0 fusion.10
  161.8 0.0 copy-start.2
  161.8 2.7 fusion.8
  164.5 85.4 %all-gather.9.cloned.1.call-done = bf16[4,1024,512]{2,0,1:T(4,128)(2,1)} async-done(((bf16[4,64,512]{2,0,1:T(4,128)(2,1)}), bf16[4,1024,512]{2,0,1:T(4,128)(2,1)}) %all-gather.9.cloned.1.call-update) | async-done | bytes 4194320 | tf_op jit(solution)/shard_map/all_gather | solution.py:41
  249.9 7.5 %copy.56 = bf16[4,1024,512]{1,2,0:T(8,128)(2,1)} copy(bf16[4,1024,512]{2,0,1:T(4,128)(2,1)} %all-gather.9.cloned.1.call-done) | data formatting | bytes 8388608 | tf_op jit(solution)/shard_map/all_gather | solution.py:41
  257.5 4.6 fusion.17
  262.1 0.7 copy-done.4
  262.8 2.7 fusion.3
  265.5 1.3 copy-done
  266.8 3.2 bitcast_convert_fusion.1
  270.1 6.2 copy.65
  276.3 0.0 reduce-scatter.3.cloned.1.call-update
  276.3 0.2 reduce-scatter.5.cloned.1.call-start
  276.5 3.2 bitcast_convert_fusion
  279.8 6.2 copy.68
  286.0 0.0 reduce-scatter.5.cloned.1.call-update
  286.0 0.6 copy-done.5
  286.6 0.1 and_select_fusion
  286.7 0.9 copy-done.1
  287.6 3.9 fusion.16
  291.5 0.5 copy.62
  292.0 0.3 reshape_reshape.3
  292.4 0.4 convolution_convert_fusion
  292.8 1.6 copy.63
  294.3 8.1 %all-to-all-start = ((bf16[8,64,1024]{2,1,0:T(8,128)(2,1)}), bf16[8,64,1024]{2,1,0:T(8,128)(2,1)S(1)}, u32[]{:S(2)}, u32[]{:S(2)}) async-start(bf16[8,64,1024]{2,1,0:T(8,128)(2,1)} %copy.63), calls=%async_computation | async-start | bytes 2097152 | tf_op jit(solution)/shard_map/all_to_all | solution.py:124
  302.4 0.2 select_reduce_fusion
  302.6 181.7 %reduce-scatter.3.cloned.1.call-done = bf16[4,64,512]{2,1,0:T(8,128)(2,1)} async-done(((bf16[4,1024,512]{2,1,0:T(8,128)(2,1)}), bf16[4,64,512]{2,1,0:T(8,128)(2,1)}) %reduce-scatter.3.cloned.1.call-update) | async-done | bytes 262160 | tf_op jit(solution)/shard_map/reduce_scatter | solution.py:93
  484.3 1.2 copy.86
  485.4 0.3 convolution_convert_fusion.3
  485.7 0.9 copy.66
  486.7 9.4 %all-to-all-start.1 = ((bf16[8,64,512]{2,1,0:T(8,128)(2,1)}), bf16[8,64,512]{2,1,0:T(8,128)(2,1)S(1)}, u32[]{:S(2)}, u32[]{:S(2)}) async-start(bf16[8,64,512]{2,1,0:T(8,128)(2,1)} %copy.66), calls=%async_computation.2 | async-start | bytes 1048576 | tf_op jit(solution)/shard_map/all_to_all | solution.py:127
  496.1 0.6 copy.84
  496.7 202.4 %reduce-scatter.5.cloned.1.call-done = bf16[4,64,512]{2,1,0:T(8,128)(2,1)} async-done(((bf16[4,1024,512]{2,1,0:T(8,128)(2,1)}), bf16[4,64,512]{2,1,0:T(8,128)(2,1)}) %reduce-scatter.5.cloned.1.call-update) | async-done | bytes 262160 | tf_op jit(solution)/shard_map/reduce_scatter | solution.py:96
  699.1 1.2 copy.89
  700.3 0.3 convolution_convert_fusion.2
  700.5 0.9 copy.69
  701.5 9.5 %all-to-all-start.2 = ((bf16[8,64,512]{2,1,0:T(8,128)(2,1)}), bf16[8,64,512]{2,1,0:T(8,128)(2,1)S(1)}, u32[]{:S(2)}, u32[]{:S(2)}) async-start(bf16[8,64,512]{2,1,0:T(8,128)(2,1)} %copy.69), calls=%async_computation.4 | async-start | bytes 1048576 | tf_op jit(solution)/shard_map/all_to_all | solution.py:128
  711.0 0.5 convolution_convert_fusion.1
  711.5 1.0 copy.106
  712.5 0.3 copy.87
  712.8 0.3 convolution_convert_fusion.5
  713.1 7.4 %all-to-all-done.2 = bf16[8,64,512]{2,1,0:T(8,128)(2,1)S(1)} async-done(((bf16[8,64,512]{2,1,0:T(8,128)(2,1)}), bf16[8,64,512]{2,1,0:T(8,128)(2,1)S(1)}, u32[]{:S(2)}, u32[]{:S(2)}) %all-to-all-start.2) | async-done | bytes 524320 | tf_op jit(solution)/shard_map/all_to_all | solution.py:128
  720.5 0.3 copy.90
  720.8 0.3 convolution_convert_fusion.4
  721.1 0.9 copy_bitcast_fusion.1
  (14 shorter events, 0.0 us)
Async XLA Ops:
  7.2 45.6 %all-gather.7.cloned.1.call-start = ((), (), s32[]{:S(2)}) async-start(), calls=%async_computation.6 | async-start | bytes 2752512 | tf_op jit(solution)/shard_map/all_gather | solution.py:34
  7.9 142.3 %all-gather.5.cloned.1.call-start = ((), (), s32[]{:S(2)}) async-start(), calls=%async_computation.5 | async-start | bytes 4456448 | tf_op jit(solution)/shard_map/all_gather | solution.py:40
  9.8 240.1 %all-gather.9.cloned.1.call-start = ((), (), s32[]{:S(2)}) async-start(), calls=%async_computation.7 | async-start | bytes 4456448 | tf_op jit(solution)/shard_map/all_gather | solution.py:41
  11.8 472.5 %reduce-scatter.3.cloned.1.call-start = ((), (), s32[]{:S(2)}) async-start(), calls=%async_computation.8 | async-start | bytes 4456448 | tf_op jit(solution)/shard_map/reduce_scatter | solution.py:93
  161.8 2.8 copy-start.2
  257.5 4.6 copy-start.3
  257.5 5.3 copy-start.4
  265.5 1.3 copy-start
  276.3 422.8 %reduce-scatter.5.cloned.1.call-start = ((), (), s32[]{:S(2)}) async-start(), calls=%async_computation.9 | async-start | bytes 4456448 | tf_op jit(solution)/shard_map/reduce_scatter | solution.py:96
  286.0 0.7 copy-start.5
  286.0 1.6 copy-start.1
  294.3 192.3 %all-to-all-start = ((bf16[8,64,1024]{2,1,0:T(8,128)(2,1)}), bf16[8,64,1024]{2,1,0:T(8,128)(2,1)S(1)}, u32[]{:S(2)}, u32[]{:S(2)}) async-start(bf16[8,64,1024]{2,1,0:T(8,128)(2,1)} %copy.63), calls=%async_computation | async-start | bytes 2097152 | tf_op jit(solution)/shard_map/all_to_all | solution.py:124
  486.7 214.8 %all-to-all-start.1 = ((bf16[8,64,512]{2,1,0:T(8,128)(2,1)}), bf16[8,64,512]{2,1,0:T(8,128)(2,1)S(1)}, u32[]{:S(2)}, u32[]{:S(2)}) async-start(bf16[8,64,512]{2,1,0:T(8,128)(2,1)} %copy.66), calls=%async_computation.2 | async-start | bytes 1048576 | tf_op jit(solution)/shard_map/all_to_all | solution.py:127
  701.5 19.0 %all-to-all-start.2 = ((bf16[8,64,512]{2,1,0:T(8,128)(2,1)}), bf16[8,64,512]{2,1,0:T(8,128)(2,1)S(1)}, u32[]{:S(2)}, u32[]{:S(2)}) async-start(bf16[8,64,512]{2,1,0:T(8,128)(2,1)} %copy.69), calls=%async_computation.4 | async-start | bytes 1048576 | tf_op jit(solution)/shard_map/all_to_all | solution.py:128
Sparse Core Ops, SparseCore 0:
  9.8 39.4 all-gather.6
  52.4 97.7 all-gather.4
  153.4 96.5 all-gather.8
  276.4 207.7 reduce-scatter.2
  488.7 210.3 reduce-scatter.4
where the time goes:
time: 730 us; the launch traced here: 729 us
  waiting for transfers between devices  569 us (78%)
  local copies, waits for them, and re-layouts  46.2 us (6%)
  blocking collectives  38.4 us (5%)
  matrix products  29.6 us (4%)
  starting transfers between devices  27.4 us (4%)
  between operations  14 us (2%)
    reduce_scatter x1, waiting for transfers between devices, local_gradients(): lax.psum_scatter(value_part.astype(jnp.bfloat16), 'ctx', scatter_dimensio...  202 us
    reduce_scatter x1, waiting for transfers between devices, local_gradients(): lax.psum_scatter(key_part.astype(jnp.bfloat16), 'ctx', scatter_dimension=...  182 us
    all_gather x1, waiting for transfers between devices, local_gradients(): lax.all_gather(key_states, 'ctx', axis=1, tiled=True)  91.3 us
    all_gather x1, waiting for transfers between devices, local_gradients(): lax.all_gather(value_state_rows, 'ctx', axis=1, tiled=True)  85.4 us
    all_gather x1, blocking collectives, local_gradients(): lax.all_gather(segment_ids, 'ctx', axis=1, tiled=True)  38.4 us
  transfers between devices with their start and end apart: 8, of which 5 were waited for; matrix products, arithmetic and copies ran while one was open for 7% of the time, Pallas kernels for 0%

commit v1 on v0

v1 whole, which is shorter than its diff:
```python
import functools

import jax
import jax.numpy as jnp
from jax import lax
from jax.experimental import pallas as pl
from jax.experimental.pallas import tpu as pltpu
from jax.sharding import PartitionSpec as P

HEAD = 256
CAP = 50.0
SCALE = 0.0625
LOG2E = 1.4426950408889634
F32 = jnp.float32
BF16 = jnp.bfloat16
VMEM_LIMIT = 48 * 1024 * 1024


def dot(a, b, ca, cb):
    return lax.dot_general(a, b, (((ca,), (cb,)), ((), ())), preferred_element_type=F32)


def projection_kernel(tp_ref, own_ref, other_ref, weight_ref, out_ref):
    rows, block, half = own_ref.shape
    tp = tp_ref[0]
    own_at = pl.multiple_of(tp * half, 128)
    other_at = pl.multiple_of((1 - tp) * half, 128)
    own = own_ref[...].reshape(rows * block, half)
    other = other_ref[...].reshape(rows * block, half)
    total = dot(own, weight_ref[:, pl.ds(own_at, half)], 1, 1)
    total += dot(other, weight_ref[:, pl.ds(other_at, half)], 1, 1)
    out_ref[...] = total.astype(BF16).reshape(out_ref.shape)


def project(own, other, weight, tp):
    rows, block, half = own.shape
    heads = weight.shape[0] // HEAD
    whole = pl.BlockSpec((rows, block, half), lambda h, tp: (0, 0, 0))
    return pl.pallas_call(
        projection_kernel,
        grid_spec=pltpu.PrefetchScalarGridSpec(
            num_scalar_prefetch=1,
            grid=(heads,),
            in_specs=[
                whole,
                whole,
                pl.BlockSpec((HEAD, 2 * half), lambda h, tp: (h, 0)),
            ],
            out_specs=pl.BlockSpec(
                (rows, 1, block, HEAD), lambda h, tp: (0, h // 2, 0, h % 2)
            ),
        ),
        out_shape=jax.ShapeDtypeStruct((rows, heads // 2, block, 2 * HEAD), BF16),
        compiler_params=pltpu.CompilerParams(vmem_limit_bytes=VMEM_LIMIT),
        cost_estimate=pl.CostEstimate(
            flops=2 * rows * block * 2 * half * heads * HEAD,
            bytes_accessed=2 * heads * HEAD * 2 * half,
            transcendentals=0,
        ),
        name="project",
    )(tp, own, other, weight)


def attention_kernel(
    q_ref, kv_own, kv_other, do_ref, qinfo, kinfo, dq_ref, dkv_own, dkv_other, acc
):
    steps, block, _ = q_ref.shape
    per = 2
    lanes = per * block
    acc[...] = jnp.zeros_like(acc)

    def heads_on_rows(ref, z):
        both = ref[z : z + per].reshape(lanes, 2 * HEAD)
        return jnp.concatenate([both[:, :HEAD], both[:, HEAD:]], axis=0)

    for z in range(0, steps, per):
        low, high = max(0, z - 4), z + per
        q = heads_on_rows(q_ref, z)
        do = heads_on_rows(do_ref, z)
        seg_q = qinfo[0:1, z * block : z * block + lanes]
        pos_q = qinfo[1:2, z * block : z * block + lanes]
        parts = []
        total = 0.0
        weighted = 0.0
        for side, kv_ref in ((0, kv_own), (1, kv_other)):
            kv = kv_ref[low:high].reshape((high - low) * block, 2 * HEAD)
            k, v = kv[:, :HEAD], kv[:, HEAD:]
            seg_k = kinfo[side, low * block : high * block, 0:1]
            pos_k = kinfo[side, low * block : high * block, 1:2]
            allowed = (seg_k == seg_q) & (pos_k <= pos_q)
            allowed = jnp.concatenate([allowed, allowed], axis=1)
            t = jnp.tanh(dot(k, q, 1, 1) * (SCALE / CAP))
            e = jnp.where(allowed, jnp.exp2(t * (CAP * LOG2E)), 0.0)
            dp = dot(v, do, 1, 1)
            total += jnp.sum(e, axis=0, keepdims=True)
            weighted += jnp.sum(e.astype(BF16).astype(F32) * dp, axis=0, keepdims=True)
            parts.append((k, t, e, dp))
        inverse = 1.0 / total
        delta = weighted * inverse
        scaled = inverse * SCALE
        dq = 0.0
        for side, (k, t, e, dp) in enumerate(parts):
            prob = (e * inverse).astype(BF16)
            ds = ((e * scaled) * (dp - delta) * (1.0 - t * t)).astype(BF16)
            acc[side, low * block : high * block, :HEAD] += dot(ds, q, 1, 0)
            acc[side, low * block : high * block, HEAD:] += dot(prob, do, 1, 0)
            dq += dot(ds, k, 0, 0)
        dq = dq.astype(BF16)
        dq_ref[z : z + per, :, :HEAD] = dq[:lanes].reshape(per, block, HEAD)
        dq_ref[z : z + per, :, HEAD:] = dq[lanes:].reshape(per, block, HEAD)
    dkv_own[...] = acc[0].reshape(dkv_own.shape)
    dkv_other[...] = acc[1].astype(BF16).reshape(dkv_other.shape)


def attention(q, kv_own, kv_other, do, qinfo, kinfo):
    steps, block, width = q.shape
    vmem = pl.BlockSpec(memory_space=pltpu.VMEM)
    return pl.pallas_call(
        attention_kernel,
        in_specs=[vmem] * 6,
        out_specs=[vmem] * 3,
        out_shape=[
            jax.ShapeDtypeStruct((steps, block, width), BF16),
            jax.ShapeDtypeStruct((steps, block, width), F32),
            jax.ShapeDtypeStruct((steps, block, width), BF16),
        ],
        scratch_shapes=[pltpu.VMEM((2, steps * block, width), F32)],
        compiler_params=pltpu.CompilerParams(vmem_limit_bytes=VMEM_LIMIT),
        cost_estimate=pl.CostEstimate(
            flops=3 * 10**9, bytes_accessed=6 * 2**20, transcendentals=1200000
        ),
        name="attend",
    )(q, kv_own, kv_other, do, qinfo, kinfo)


def copy_kernel(index_ref, in_ref, out_ref):
    out_ref[...] = in_ref[...]


def pick_rows(index, source):
    count, rest = index.shape[0], source.shape[1:]
    zeros = (0,) * len(rest)
    return pl.pallas_call(
        copy_kernel,
        grid_spec=pltpu.PrefetchScalarGridSpec(
            num_scalar_prefetch=1,
            grid=(count,),
            in_specs=[pl.BlockSpec((1,) + rest, lambda i, index: (index[i],) + zeros)],
            out_specs=pl.BlockSpec((1,) + rest, lambda i, index: (i,) + zeros),
        ),
        out_shape=jax.ShapeDtypeStruct((count,) + rest, source.dtype),
        name="pick",
    )(index, source)


def place_q_kernel(index_ref, in_ref, out_ref):
    width = in_ref.shape[-1]
    for h in range(in_ref.shape[1]):
        out_ref[0, :, h * width : (h + 1) * width] = in_ref[0, h]


def place_kv_kernel(index_ref, in_ref, key_ref, value_ref):
    for h in range(in_ref.shape[1]):
        key_ref[0, :, h * HEAD : (h + 1) * HEAD] = in_ref[0, h, :, :HEAD]
        value_ref[0, :, h * HEAD : (h + 1) * HEAD] = in_ref[0, h, :, HEAD:]


def place_rows(kernel, index, source, out_widths, name):
    count = index.shape[0]
    rest = source.shape[1:]
    block = source.shape[2]
    return pl.pallas_call(
        kernel,
        grid_spec=pltpu.PrefetchScalarGridSpec(
            num_scalar_prefetch=1,
            grid=(count,),
            in_specs=[pl.BlockSpec((1,) + rest, lambda i, index: (index[i], 0, 0, 0))],
            out_specs=[
                pl.BlockSpec((1, block, w), lambda i, index: (i, 0, 0))
                for w in out_widths
            ],
        ),
        out_shape=[
            jax.ShapeDtypeStruct((count, block, w), source.dtype) for w in out_widths
        ],
        name=name,
    )(index, source)


def exchange(x, axis, groups=None):
    return lax.all_to_all(
        x, axis, split_axis=0, concat_axis=0, tiled=True, axis_index_groups=groups
    )


def on_device(
    queries, key_states, value_state_rows, segment_ids, output_grad, out_weight, destination
):
    rows, block, q_width = queries.shape
    kv_heads = key_states.shape[2] // HEAD
    units = rows * kv_heads
    n_ctx = lax.axis_size("ctx")
    groups = lax.axis_size("dp")
    pair = n_ctx // units
    ctx = lax.axis_index("ctx")
    tp = lax.axis_index("tp")
    group = lax.axis_index("dp")
    side = ctx % pair
    unit = ctx // pair
    columns = [[z * pair + h for z in range(units)] for h in range(pair)]
    swap = [(z * pair + h, z * pair + 1 - h) for z in range(units) for h in range(pair)]

    dest = destination.reshape(groups, rows)
    own_targets = lax.dynamic_slice_in_dim(dest, group, 1, 0) // rows
    send_index = jnp.sum(
        jnp.where(
            own_targets == jnp.arange(groups, dtype=jnp.int32)[:, None],
            jnp.arange(rows, dtype=jnp.int32)[None, :],
            0,
        ),
        axis=1,
    )
    wanted = group * rows + jnp.arange(rows, dtype=jnp.int32)
    recv_index = jnp.sum(
        jnp.where(
            destination[None, :] == wanted[:, None],
            jnp.arange(groups * rows, dtype=jnp.int32)[None, :] // rows,
            0,
        ),
        axis=1,
    )

    other_grad = lax.ppermute(output_grad, "tp", [(0, 1), (1, 0)])

    def per_unit(x):
        x = x.reshape(rows, block, kv_heads, x.shape[2] // kv_heads)
        return jnp.transpose(x, (0, 2, 1, 3)).reshape(units, block, x.shape[3])

    kv = jnp.concatenate([per_unit(key_states), per_unit(value_state_rows)], axis=2)
    kv_own = exchange(kv, "ctx", columns)
    q = exchange(per_unit(queries), "ctx", columns)
    kv_other = lax.ppermute(kv_own, "ctx", swap)

    seg_send = jnp.repeat(segment_ids, kv_heads * pair, axis=0)
    seg_all = exchange(seg_send, "ctx").reshape(units, pair, block)
    pos_all = jnp.arange(n_ctx * block, dtype=jnp.int32).reshape(units, pair, block)

    def of_side(x, which):
        return lax.dynamic_slice_in_dim(x, which, 1, 1).reshape(units * block)

    info = [
        jnp.stack([of_side(seg_all, which), of_side(pos_all, which)])
        for which in (side, 1 - side)
    ]
    qinfo = info[0]
    kinfo = jnp.stack([jnp.transpose(info[0]), jnp.transpose(info[1])])

    do = project(output_grad, other_grad, out_weight, tp[None].astype(jnp.int32))
    do = exchange(do.reshape(units, block, q_width // kv_heads), "ctx", columns)

    dq, dkv_mine, dkv_theirs = attention(q, kv_own, kv_other, do, qinfo, kinfo)

    dq = exchange(dq, "ctx", columns)
    dkv_back = lax.ppermute(dkv_theirs, "ctx", swap)
    dkv = (dkv_mine + dkv_back.astype(F32)).astype(BF16)
    dkv = exchange(dkv, "ctx", columns)

    def by_row(x):
        return x.reshape(rows, kv_heads, block, x.shape[2])

    dq = exchange(pick_rows(send_index, by_row(dq)), "dp")
    (query_out,) = place_rows(place_q_kernel, recv_index, dq, [q_width], "place_q")
    dkv = exchange(pick_rows(send_index, by_row(dkv)), "dp")
    key_out, value_out = place_rows(
        place_kv_kernel, recv_index, dkv, [kv_heads * HEAD] * 2, "place_kv"
    )
    return query_out, key_out, value_out


def solution(mesh):
    in_specs = (
        P("dp", "ctx", "tp"),
        P("dp", "ctx", "tp"),
        P("dp", "ctx", "tp"),
        P("dp", "ctx"),
        P("dp", "ctx", "tp"),
        P("tp", None),
        P(),
    )
    out_specs = (P("dp", "ctx", "tp"), P("dp", "ctx", "tp"), P("dp", "ctx", "tp"))
    return jax.shard_map(
        on_device, mesh=mesh, in_specs=in_specs, out_specs=out_specs, check_vma=False
    )
```

time: 730 us -> 170 us (0.23)
  waiting for transfers between devices: 569 us -> 76.6 us
  blocking collectives: 38.4 us -> 0 us
  local copies, waits for them, and re-layouts: 46.2 us -> 8.7 us
  matrix products: 29.6 us -> 0 us
  Pallas kernels: 0 us -> 28.8 us
  starting transfers between devices: 27.4 us -> 49.6 us
  between operations: 14 us -> 0.79 us
    reduce_scatter x2 -> x0, waiting for transfers between devices: 384 us -> none  [the longest x1 202 us: local_gradients(): lax.psum_scatter(value_part.astype(jnp.bfloat16), 'ctx', scatter_dimensio...]
    all_gather x3 -> x0, waiting for transfers between devices: 177 us -> none  [the longest x1 91.3 us: local_gradients(): lax.all_gather(key_states, 'ctx', axis=1, tiled=True)]
    all_to_all x3 -> x8, waiting for transfers between devices: 7.39 us -> 56 us  [exchange(): lax.all_to_all(x, axis, split_axis=0, concat_axis=0, tiled=True, axis_ind...]
    all_gather x1 -> x0, blocking collectives: 38.4 us -> none  [local_gradients(): lax.all_gather(segment_ids, 'ctx', axis=1, tiled=True)]
    dot_general x13 -> x0, matrix products: 29.6 us -> none  [the longest x1 5.73 us: local_gradients(): lax.dot_general(lax.all_gather(output_grad, 'tp', axis=2, tiled=True), ou...]
    pallas_call x0 -> x6, Pallas kernels: none -> 28.8 us  [the longest x2 11 us: pick_rows(): pl.pallas_call(copy_kernel, grid_spec=pltpu.PrefetchScalarGridSpec(num_sc...]
    all_to_all x3 -> x8, starting transfers between devices: 27 us -> 48.6 us  [exchange(): lax.all_to_all(x, axis, split_axis=0, concat_axis=0, tiled=True, axis_ind...]
    ppermute x0 -> x3, waiting for transfers between devices: none -> 20.6 us  [the longest x1 10.2 us: on_device(): kv_other = lax.ppermute(kv_own, 'ctx', swap)]
  transfers between devices with their start and end apart: 8 -> 11, of which waited for: 5 -> 11; matrix products, arithmetic and copies ran while one was open for 7% -> 5% of each run, Pallas kernels for 0% -> 12%
where the time goes in v1:
time: 170 us; the launch traced here: 169 us
  waiting for transfers between devices  76.6 us (45%)
  starting transfers between devices  49.6 us (29%)
  Pallas kernels  28.8 us (17%)
  local copies, waits for them, and re-layouts  8.7 us (5%)
  other arithmetic  4.12 us (2%)
    all_to_all x8, waiting for transfers between devices, exchange(): lax.all_to_all(x, axis, split_axis=0, concat_axis=0, tiled=True, axis_ind...  56 us
    all_to_all x8, starting transfers between devices, exchange(): lax.all_to_all(x, axis, split_axis=0, concat_axis=0, tiled=True, axis_ind...  48.6 us
    pallas_call x2, Pallas kernels, pick_rows(): pl.pallas_call(copy_kernel, grid_spec=pltpu.PrefetchScalarGridSpec(num_sc...  11 us
    ppermute x1, waiting for transfers between devices, on_device(): kv_other = lax.ppermute(kv_own, 'ctx', swap)  10.2 us
    ppermute x1, waiting for transfers between devices, on_device(): dkv_back = lax.ppermute(dkv_theirs, 'ctx', swap)  9.46 us
    pallas_call x2, Pallas kernels, place_rows(): pl.pallas_call(kernel, grid_spec=pltpu.PrefetchScalarGridSpec(num_scalar_...  7.65 us
    pallas_call x1, Pallas kernels, project(): pl.pallas_call(projection_kernel, grid_spec=pltpu.PrefetchScalarGridSpec(...  5.94 us
    pallas_call x1, Pallas kernels, attention(): pl.pallas_call(attention_kernel, in_specs=[vmem] * 6, out_specs=[vmem] *...  4.14 us
  transfers between devices with their start and end apart: 11, of which 11 were waited for; matrix products, arithmetic and copies ran while one was open for 5% of the time, Pallas kernels for 12%

profile of v1, /device:TPU:1, one launch (start us, length us, event | category | flops | bytes accessed | tf_op | source)
XLA Modules:
  0.0 168.6 jit_solution(9346524558240610386)
XLA Ops:
  0.6 0.0 copy-start
  0.6 1.4 broadcast_in_dim.40
  2.0 11.6 %all-to-all-start.3 = ((s32[16,1,64]{2,1,0:T(1,128)}), s32[16,1,64]{2,1,0:T(1,128)S(1)}, u32[]{:S(2)}, u32[]{:S(2)}) async-start(s32[16,1,64]{2,1,0:T(1,128)} %bitcast.6), calls=%async_computation.3 | async-start | bytes 16384 | tf_op jit(solution)/shard_map/all_to_all | solution.py:191
  13.6 1.0 fusion.3
  14.6 1.0 fusion.4
  15.6 0.9 pad_maximum_fusion.1
  16.5 5.9 %all-to-all-done.3 = s32[16,1,64]{2,1,0:T(1,128)S(1)} async-done(((s32[16,1,64]{2,1,0:T(1,128)}), s32[16,1,64]{2,1,0:T(1,128)S(1)}, u32[]{:S(2)}, u32[]{:S(2)}) %all-to-all-start.3) | async-done | bytes 4128 | tf_op jit(solution)/shard_map/all_to_all | solution.py:191
  22.4 3.5 %all-to-all-start.1 = ((bf16[8,64,512]{2,1,0:T(8,128)(2,1)}), bf16[8,64,512]{2,1,0:T(8,128)(2,1)S(1)}, u32[]{:S(2)}, u32[]{:S(2)}) async-start(bf16[8,64,512]{2,1,0:T(8,128)(2,1)} %pad_maximum_fusion.1), calls=%async_computation.1 | async-start | bytes 1048576 | tf_op jit(solution)/shard_map/all_to_all | solution.py:191
  25.9 0.4 collective-permute-start.1
  26.3 1.1 fusion.2
  27.4 0.8 pad_maximum_fusion
  28.2 13.2 %all-to-all-done.1.kv_own = bf16[8,64,512]{2,1,0:T(8,128)(2,1)S(1)} async-done(((bf16[8,64,512]{2,1,0:T(8,128)(2,1)}), bf16[8,64,512]{2,1,0:T(8,128)(2,1)S(1)}, u32[]{:S(2)}, u32[]{:S(2)}) %all-to-all-start.1) | async-done | bytes 524320 | tf_op jit(solution)/shard_map/all_to_all | solution.py:191
  41.4 3.5 %all-to-all-start = ((bf16[8,64,512]{2,1,0:T(8,128)(2,1)}), bf16[8,64,512]{2,1,0:T(8,128)(2,1)S(1)}, u32[]{:S(2)}, u32[]{:S(2)}) async-start(bf16[8,64,512]{2,1,0:T(8,128)(2,1)} %bitcast.1), calls=%async_computation | async-start | bytes 1048576 | tf_op jit(solution)/shard_map/all_to_all | solution.py:191
  44.9 1.0 collective-permute-done.1.other_ref
  45.9 0.0 copy-done
  45.9 5.9 %project.1 = bf16[4,2,64,512]{3,2,1,0:T(8,128)(2,1)} custom-call(s32[1]{0:T(128)} %bitcast.4.tp_ref, bf16[4,64,1792]{2,1,0:T(8,128)(2,1)S(1)} %copy-done, bf16[4,64,1792]{2,1,0:T(8,128)(2,1)S(1)} %collective-permute-done.1.other_ref, bf16[1024,3584]{1,0:T(8,128)(2,1)} %weight_ref.1), custom_call_target="tpu_custom_call" | custom-call | flops 1879048192 | bytes 7340032 | tf_op jit(solution)/shard_map/project/pallas_call | solution.py:39
  51.9 7.6 %all-to-all-done.q_ref = bf16[8,64,512]{2,1,0:T(8,128)(2,1)S(1)} async-done(((bf16[8,64,512]{2,1,0:T(8,128)(2,1)}), bf16[8,64,512]{2,1,0:T(8,128)(2,1)S(1)}, u32[]{:S(2)}, u32[]{:S(2)}) %all-to-all-start) | async-done | bytes 524320 | tf_op jit(solution)/shard_map/all_to_all | solution.py:191
  59.4 3.5 %all-to-all-start.2 = ((bf16[8,64,512]{2,1,0:T(8,128)(2,1)}), bf16[8,64,512]{2,1,0:T(8,128)(2,1)S(1)}, u32[]{:S(2)}, u32[]{:S(2)}) async-start(bf16[8,64,512]{2,1,0:T(8,128)(2,1)} %bitcast.5), calls=%async_computation.2 | async-start | bytes 1048576 | tf_op jit(solution)/shard_map/all_to_all | solution.py:191
  63.0 0.4 collective-permute-start
  63.3 0.1 stack_reshape.13
  63.4 0.1 stack_reshape.15
  63.5 0.1 stack_reshape.12
  63.6 0.1 stack_reshape.14
  63.7 0.2 copy.17.kinfo
  64.0 10.2 %collective-permute-done.kv_other = bf16[8,64,512]{2,1,0:T(8,128)(2,1)S(1)} collective-permute-done((bf16[8,64,512]{2,1,0:T(8,128)(2,1)S(1)}, bf16[8,64,512]{2,1,0:T(8,128)(2,1)S(1)}, u32[]{:S(2)}, u32[]{:S(2)}) %collective-permute-start) | collective-permute-done | bytes 524320 | tf_op jit(solution)/shard_map/ppermute | solution.py:242
  74.1 0.0 copy-start.1
  74.1 0.8 copy-done.1
  74.9 1.7 all-to-all-done.2.do_ref
  76.6 0.0 copy-start.2
  76.6 1.0 copy-done.2
  77.6 0.0 copy-start.8
  77.6 4.1 %attend.1 = (bf16[8,64,512]{2,1,0:T(8,128)(2,1)}, f32[8,64,512]{2,1,0:T(8,128)S(1)}, bf16[8,64,512]{2,1,0:T(8,128)(2,1)S(1)}) custom-call(bf16[8,64,512]{2,1,0:T(8,128)(2,1)S(1)} %all-to-all-done.q_ref, bf16[8,64,512]{2,1,0:T(8,128)(2,1)S(1)} %all-to-all-done.1.kv_own, bf16[8,64,512]{2,1,0:T(8,128)(2,1)S(1)} %copy-done.2, ...), custom_call_target="tpu_custom_call" | custom-call | flops 3000000000 | bytes 6291456 | tf_op jit(solution)/shard_map/attend/pallas_call | solution.py:118
  81.8 0.0 copy-start.3
  81.8 0.8 copy-done.3
  82.6 4.5 %all-to-all-start.4 = ((bf16[8,64,512]{2,1,0:T(8,128)(2,1)}), bf16[8,64,512]{2,1,0:T(8,128)(2,1)S(1)}, u32[]{:S(2)}, u32[]{:S(2)}) async-start(bf16[8,64,512]{2,1,0:T(8,128)(2,1)} %get-tuple-element.8), calls=%async_computation.4 | async-start | bytes 1048576 | tf_op jit(solution)/shard_map/all_to_all | solution.py:191
  87.1 0.3 collective-permute-start.2
  87.4 9.5 %collective-permute-done.2 = bf16[8,64,512]{2,1,0:T(8,128)(2,1)S(1)} collective-permute-done((bf16[8,64,512]{2,1,0:T(8,128)(2,1)}, bf16[8,64,512]{2,1,0:T(8,128)(2,1)S(1)}, u32[]{:S(2)}, u32[]{:S(2)}) %collective-permute-start.2) | collective-permute-done | bytes 524320 | tf_op jit(solution)/shard_map/ppermute | solution.py:264
  96.8 1.0 add_convert_fusion
  97.8 1.5 all-to-all-done.4
  99.3 0.0 copy-start.6
  99.3 5.4 %all-to-all-start.6 = ((bf16[8,64,512]{2,1,0:T(8,128)(2,1)}), bf16[8,64,512]{2,1,0:T(8,128)(2,1)S(1)}, u32[]{:S(2)}, u32[]{:S(2)}) async-start(bf16[8,64,512]{2,1,0:T(8,128)(2,1)} %add_convert_fusion), calls=%async_computation.6 | async-start | bytes 1048576 | tf_op jit(solution)/shard_map/all_to_all | solution.py:191
  104.7 0.0 copy-done.8
  104.8 0.1 reshape.101
  104.9 0.6 select_reduce_fusion.index_ref
  105.5 0.0 copy-done.6
  105.5 5.5 %pick.2 = bf16[8,2,64,512]{3,2,1,0:T(8,128)(2,1)} custom-call(s32[8]{0:T(128)} %select_reduce_fusion.index_ref, bf16[4,2,64,512]{3,2,1,0:T(8,128)(2,1)} %bitcast.23), custom_call_target="tpu_custom_call" | custom-call | tf_op jit(solution)/shard_map/pick/pallas_call | solution.py:143
  111.0 6.0 %all-to-all-done.6 = bf16[8,64,512]{2,1,0:T(8,128)(2,1)S(1)} async-done(((bf16[8,64,512]{2,1,0:T(8,128)(2,1)}), bf16[8,64,512]{2,1,0:T(8,128)(2,1)S(1)}, u32[]{:S(2)}, u32[]{:S(2)}) %all-to-all-start.6) | async-done | bytes 524320 | tf_op jit(solution)/shard_map/all_to_all | solution.py:191
  117.0 0.0 copy-start.7
  117.0 12.3 %all-to-all-start.5 = ((bf16[8,2,64,512]{3,2,1,0:T(8,128)(2,1)}), bf16[8,2,64,512]{3,2,1,0:T(8,128)(2,1)S(1)}, u32[]{:S(2)}, u32[]{:S(2)}) async-start(bf16[8,2,64,512]{3,2,1,0:T(8,128)(2,1)} %pick.2), calls=%async_computation.5 | async-start | bytes 2097152 | tf_op jit(solution)/shard_map/all_to_all | solution.py:191
  129.3 0.0 copy-done.7
  129.3 5.5 %pick.3 = bf16[8,2,64,512]{3,2,1,0:T(8,128)(2,1)} custom-call(s32[8]{0:T(128)} %select_reduce_fusion.index_ref, bf16[4,2,64,512]{3,2,1,0:T(8,128)(2,1)} %bitcast.24), custom_call_target="tpu_custom_call" | custom-call | tf_op jit(solution)/shard_map/pick/pallas_call | solution.py:143
  134.8 9.6 %all-to-all-done.5.in_ref = bf16[8,2,64,512]{3,2,1,0:T(8,128)(2,1)S(1)} async-done(((bf16[8,2,64,512]{3,2,1,0:T(8,128)(2,1)}), bf16[8,2,64,512]{3,2,1,0:T(8,128)(2,1)S(1)}, u32[]{:S(2)}, u32[]{:S(2)}) %all-to-all-start.5) | async-done | bytes 1048608 | tf_op jit(solution)/shard_map/all_to_all | solution.py:191
  144.4 0.0 copy-start.4
  144.4 4.3 %all-to-all-start.7 = ((bf16[8,2,64,512]{3,2,1,0:T(8,128)(2,1)}), bf16[8,2,64,512]{3,2,1,0:T(8,128)(2,1)S(1)}, u32[]{:S(2)}, u32[]{:S(2)}) async-start(bf16[8,2,64,512]{3,2,1,0:T(8,128)(2,1)} %pick.3), calls=%async_computation.7 | async-start | bytes 2097152 | tf_op jit(solution)/shard_map/all_to_all | solution.py:191
  148.7 0.8 select_reduce_fusion.1.index_ref
  149.5 0.0 copy-done.4
  149.5 3.8 %place_q.1 = bf16[4,64,1024]{2,1,0:T(8,128)(2,1)} custom-call(s32[4]{0:T(128)} %select_reduce_fusion.1.index_ref, bf16[8,2,64,512]{3,2,1,0:T(8,128)(2,1)} %copy-done.4), custom_call_target="tpu_custom_call" | custom-call | tf_op jit(solution)/shard_map/place_q/pallas_call | solution.py:172
  153.3 10.5 %all-to-all-done.7.in_ref = bf16[8,2,64,512]{3,2,1,0:T(8,128)(2,1)S(1)} async-done(((bf16[8,2,64,512]{3,2,1,0:T(8,128)(2,1)}), bf16[8,2,64,512]{3,2,1,0:T(8,128)(2,1)S(1)}, u32[]{:S(2)}, u32[]{:S(2)}) %all-to-all-start.7) | async-done | bytes 1048608 | tf_op jit(solution)/shard_map/all_to_all | solution.py:191
  163.8 0.0 copy-start.5
  163.8 1.0 copy-done.5
  164.8 3.8 %place_kv.1 = (bf16[4,64,512]{2,1,0:T(8,128)(2,1)}, bf16[4,64,512]{2,1,0:T(8,128)(2,1)}) custom-call(s32[4]{0:T(128)} %select_reduce_fusion.1.index_ref, bf16[8,2,64,512]{3,2,1,0:T(8,128)(2,1)} %copy-done.5), custom_call_target="tpu_custom_call" | custom-call | tf_op jit(solution)/shard_map/place_kv/pallas_call | solution.py:172
  (11 shorter events, 0.1 us)
Async XLA Ops:
  0.6 45.3 %copy-start = (bf16[4,64,1792]{2,1,0:T(8,128)(2,1)S(1)}, bf16[4,64,1792]{2,1,0:T(8,128)(2,1)}, u32[]{:S(2)}) copy-start(bf16[4,64,1792]{2,1,0:T(8,128)(2,1)} %own_ref.1) | copy-start | bytes 2752516
  2.0 20.4 %all-to-all-start.3 = ((s32[16,1,64]{2,1,0:T(1,128)}), s32[16,1,64]{2,1,0:T(1,128)S(1)}, u32[]{:S(2)}, u32[]{:S(2)}) async-start(s32[16,1,64]{2,1,0:T(1,128)} %bitcast.6), calls=%async_computation.3 | async-start | bytes 16384 | tf_op jit(solution)/shard_map/all_to_all | solution.py:191
  22.4 19.1 %all-to-all-start.1 = ((bf16[8,64,512]{2,1,0:T(8,128)(2,1)}), bf16[8,64,512]{2,1,0:T(8,128)(2,1)S(1)}, u32[]{:S(2)}, u32[]{:S(2)}) async-start(bf16[8,64,512]{2,1,0:T(8,128)(2,1)} %pad_maximum_fusion.1), calls=%async_computation.1 | async-start | bytes 1048576 | tf_op jit(solution)/shard_map/all_to_all | solution.py:191
  25.9 20.0 %collective-permute-start.1 = (bf16[4,64,1792]{2,1,0:T(8,128)(2,1)}, bf16[4,64,1792]{2,1,0:T(8,128)(2,1)S(1)}, u32[]{:S(2)}, u32[]{:S(2)}) collective-permute-start(bf16[4,64,1792]{2,1,0:T(8,128)(2,1)} %own_ref.1), channel_id=1, source_target_pairs={{0,1},{1,0},{2,3},{3,2},{4,5},{5,4},{6,7},{7,6},{8,9},{9,8},{10,11... | collective-permute-start | bytes 2752520 | tf_op jit(solution)/shard_map/ppermute | solution.py:233
  41.4 18.0 %all-to-all-start = ((bf16[8,64,512]{2,1,0:T(8,128)(2,1)}), bf16[8,64,512]{2,1,0:T(8,128)(2,1)S(1)}, u32[]{:S(2)}, u32[]{:S(2)}) async-start(bf16[8,64,512]{2,1,0:T(8,128)(2,1)} %bitcast.1), calls=%async_computation | async-start | bytes 1048576 | tf_op jit(solution)/shard_map/all_to_all | solution.py:191
  59.4 17.1 %all-to-all-start.2 = ((bf16[8,64,512]{2,1,0:T(8,128)(2,1)}), bf16[8,64,512]{2,1,0:T(8,128)(2,1)S(1)}, u32[]{:S(2)}, u32[]{:S(2)}) async-start(bf16[8,64,512]{2,1,0:T(8,128)(2,1)} %bitcast.5), calls=%async_computation.2 | async-start | bytes 1048576 | tf_op jit(solution)/shard_map/all_to_all | solution.py:191
  63.0 11.2 %collective-permute-start = (bf16[8,64,512]{2,1,0:T(8,128)(2,1)S(1)}, bf16[8,64,512]{2,1,0:T(8,128)(2,1)S(1)}, u32[]{:S(2)}, u32[]{:S(2)}) collective-permute-start(bf16[8,64,512]{2,1,0:T(8,128)(2,1)S(1)} %all-to-all-done.1.kv_own), channel_id=1, source_target_pairs={{0,2},{2,0},{4,6},{6,4},{8,10},{10,8},{12,14},{14,12},{16,18},{18,... | collective-permute-start | bytes 1572872 | tf_op jit(solution)/shard_map/ppermute | solution.py:242
  74.1 0.8 copy-start.1
  76.6 1.0 copy-start.2
  77.6 27.1 %copy-start.8 = (s32[32]{0:T(128)S(1)}, s32[32]{0:T(128)}, u32[]{:S(2)}) copy-start(s32[32]{0:T(128)} %param.13) | copy-start | bytes 388
  81.8 0.8 copy-start.3
  82.6 16.7 %all-to-all-start.4 = ((bf16[8,64,512]{2,1,0:T(8,128)(2,1)}), bf16[8,64,512]{2,1,0:T(8,128)(2,1)S(1)}, u32[]{:S(2)}, u32[]{:S(2)}) async-start(bf16[8,64,512]{2,1,0:T(8,128)(2,1)} %get-tuple-element.8), calls=%async_computation.4 | async-start | bytes 1048576 | tf_op jit(solution)/shard_map/all_to_all | solution.py:191
  87.1 9.7 %collective-permute-start.2 = (bf16[8,64,512]{2,1,0:T(8,128)(2,1)}, bf16[8,64,512]{2,1,0:T(8,128)(2,1)S(1)}, u32[]{:S(2)}, u32[]{:S(2)}) collective-permute-start(bf16[8,64,512]{2,1,0:T(8,128)(2,1)} %copy-done.3), channel_id=1, source_target_pairs={{0,2},{2,0},{4,6},{6,4},{8,10},{10,8},{12,14},{14,12},{16,18},{18,... | collective-permute-start | bytes 1572872 | tf_op jit(solution)/shard_map/ppermute | solution.py:264
  99.3 6.1 %copy-start.6 = (bf16[8,64,512]{2,1,0:T(8,128)(2,1)}, bf16[8,64,512]{2,1,0:T(8,128)(2,1)S(1)}, u32[]{:S(2)}) copy-start(bf16[8,64,512]{2,1,0:T(8,128)(2,1)S(1)} %all-to-all-done.4) | copy-start | bytes 1572868
  99.3 17.7 %all-to-all-start.6 = ((bf16[8,64,512]{2,1,0:T(8,128)(2,1)}), bf16[8,64,512]{2,1,0:T(8,128)(2,1)S(1)}, u32[]{:S(2)}, u32[]{:S(2)}) async-start(bf16[8,64,512]{2,1,0:T(8,128)(2,1)} %add_convert_fusion), calls=%async_computation.6 | async-start | bytes 1048576 | tf_op jit(solution)/shard_map/all_to_all | solution.py:191
  117.0 12.3 %copy-start.7 = (bf16[8,64,512]{2,1,0:T(8,128)(2,1)}, bf16[8,64,512]{2,1,0:T(8,128)(2,1)S(1)}, u32[]{:S(2)}) copy-start(bf16[8,64,512]{2,1,0:T(8,128)(2,1)S(1)} %all-to-all-done.6) | copy-start | bytes 1572868
  117.0 27.4 %all-to-all-start.5 = ((bf16[8,2,64,512]{3,2,1,0:T(8,128)(2,1)}), bf16[8,2,64,512]{3,2,1,0:T(8,128)(2,1)S(1)}, u32[]{:S(2)}, u32[]{:S(2)}) async-start(bf16[8,2,64,512]{3,2,1,0:T(8,128)(2,1)} %pick.2), calls=%async_computation.5 | async-start | bytes 2097152 | tf_op jit(solution)/shard_map/all_to_all | solution.py:191
  144.4 5.1 %copy-start.4 = (bf16[8,2,64,512]{3,2,1,0:T(8,128)(2,1)}, bf16[8,2,64,512]{3,2,1,0:T(8,128)(2,1)S(1)}, u32[]{:S(2)}) copy-start(bf16[8,2,64,512]{3,2,1,0:T(8,128)(2,1)S(1)} %all-to-all-done.5.in_ref) | copy-start | bytes 3145732
  144.4 19.4 %all-to-all-start.7 = ((bf16[8,2,64,512]{3,2,1,0:T(8,128)(2,1)}), bf16[8,2,64,512]{3,2,1,0:T(8,128)(2,1)S(1)}, u32[]{:S(2)}, u32[]{:S(2)}) async-start(bf16[8,2,64,512]{3,2,1,0:T(8,128)(2,1)} %pick.3), calls=%async_computation.7 | async-start | bytes 2097152 | tf_op jit(solution)/shard_map/all_to_all | solution.py:191
  163.8 1.0 copy-start.5

commit v2 on v1

v2 whole, which is shorter than its diff:
```python
import jax
import jax.numpy as jnp
from jax import lax
from jax.experimental import pallas as pl
from jax.experimental.pallas import tpu as pltpu
from jax.sharding import PartitionSpec as P

HEAD = 256
CAP = 50.0
SCALE = 0.0625
LOG2E = 1.4426950408889634
F32 = jnp.float32
BF16 = jnp.bfloat16
TILE = 16
SMALL_VMEM = 8 * 1024 * 1024
WHOLE_VMEM = 60 * 1024 * 1024
LARGE_VMEM = 28 * 1024 * 1024


def dot(a, b, ca, cb):
    return lax.dot_general(a, b, (((ca,), (cb,)), ((), ())), preferred_element_type=F32)


VMEM = pl.BlockSpec(memory_space=pltpu.VMEM)
SMEM = pl.BlockSpec(memory_space=pltpu.SMEM)
ANY = pl.BlockSpec(memory_space=pl.ANY)


def pack_kernel(seg_ref, q_hbm, k_hbm, v_hbm, out_ref, q_ref, k_ref, v_ref, sems):
    rows, block, q_width = q_ref.shape
    kv_heads = k_ref.shape[2] // HEAD
    width = q_width // kv_heads
    pieces = block // TILE
    copies = [
        pltpu.make_async_copy(source, target, sems.at[i])
        for i, (source, target) in enumerate(
            ((q_hbm, q_ref), (k_hbm, k_ref), (v_hbm, v_ref))
        )
    ]
    for copy in copies:
        copy.start()
    place = lax.broadcasted_iota(jnp.int32, (TILE, block), 1)
    row = lax.broadcasted_iota(jnp.int32, (TILE, block), 0)
    lane = lax.broadcasted_iota(jnp.int32, (TILE, 128), 1)
    ids = []
    for r in range(rows):
        spread = jnp.broadcast_to(seg_ref[r : r + 1], (TILE, block)).astype(F32)
        columns = jnp.zeros((TILE, 128), F32)
        for j in range(pieces):
            column = jnp.sum(
                jnp.where(place == row + j * TILE, spread, 0.0), axis=1, keepdims=True
            )
            columns = jnp.where(lane == j, column, columns)
        ids.append(columns.astype(BF16))
    for copy in copies:
        copy.wait()
    for r in range(rows):
        for h in range(kv_heads):
            u = r * kv_heads + h
            heads = slice(h * HEAD, (h + 1) * HEAD)
            for j in range(pieces):
                at = slice(j * TILE, (j + 1) * TILE)
                k_at = pieces * HEAD + j * 2 * HEAD
                out_ref[u, :, j * HEAD : (j + 1) * HEAD] = q_ref[
                    r, at, h * width : h * width + HEAD
                ]
                out_ref[u, :, k_at : k_at + HEAD] = k_ref[r, at, heads]
                out_ref[u, :, k_at + HEAD : k_at + 2 * HEAD] = v_ref[r, at, heads]
            out_ref[u, :, pieces * 3 * HEAD :] = ids[r]


def pack(seg, q, k, v):
    rows, block, _ = q.shape
    kv_heads = k.shape[2] // HEAD
    lanes = block // TILE * 3 * HEAD + 128
    return pl.pallas_call(
        pack_kernel,
        in_specs=[VMEM, ANY, ANY, ANY],
        out_specs=VMEM,
        out_shape=jax.ShapeDtypeStruct((rows * kv_heads, TILE, lanes), BF16),
        scratch_shapes=[
            pltpu.VMEM(q.shape, BF16),
            pltpu.VMEM(k.shape, BF16),
            pltpu.VMEM(v.shape, BF16),
            pltpu.SemaphoreType.DMA((3,)),
        ],
        compiler_params=pltpu.CompilerParams(vmem_limit_bytes=WHOLE_VMEM),
        name="pack",
    )(seg, q, k, v)


def own_half_kernel(index_ref, x_ref, weight_ref, out_ref, turned_ref):
    rows, block, half = x_ref.shape
    x = x_ref[...].reshape(rows * block, half)
    own = pl.multiple_of(index_ref[0] * half, 128)
    other = pl.multiple_of((1 - index_ref[0]) * half, 128)
    for h in range(weight_ref.shape[0] // HEAD):
        at = slice(h * HEAD, (h + 1) * HEAD)
        out_ref[:, at] = dot(x, weight_ref[at, pl.ds(own, half)], 1, 1)
        turned_ref[:, at] = weight_ref[at, pl.ds(other, half)].T


def project_own(x, weight, index):
    rows, block, half = x.shape
    width = weight.shape[0]
    return pl.pallas_call(
        own_half_kernel,
        in_specs=[SMEM, VMEM, VMEM],
        out_specs=[VMEM, VMEM],
        out_shape=[
            jax.ShapeDtypeStruct((rows * block, width), F32),
            jax.ShapeDtypeStruct((half, width), BF16),
        ],
        compiler_params=pltpu.CompilerParams(vmem_limit_bytes=LARGE_VMEM),
        cost_estimate=pl.CostEstimate(
            flops=2 * rows * block * half * width,
            bytes_accessed=4 * half * width,
            transcendentals=0,
        ),
        name="project_own",
    )(index, x, weight)


def other_half_kernel(x_ref, turned_ref, part_ref, q_ref, out_ref):
    rows, block, half = x_ref.shape
    kv_heads = out_ref.shape[1]
    width = turned_ref.shape[1] // kv_heads
    x = x_ref[...].reshape(rows * block, half)
    for h in range(kv_heads):
        at = slice(h * width, (h + 1) * width)
        total = part_ref[:, at] + dot(x, turned_ref[:, at], 1, 0)
        out_ref[:, h, :, :width] = total.astype(BF16).reshape(rows, block, width)
        out_ref[:, h, :, width:] = q_ref[:, :, h * width + HEAD : (h + 1) * width]


def project_other(x, turned, part, q, kv_heads):
    rows, block, half = x.shape
    width = turned.shape[1]
    return pl.pallas_call(
        other_half_kernel,
        in_specs=[VMEM] * 4,
        out_specs=VMEM,
        out_shape=jax.ShapeDtypeStruct(
            (rows, kv_heads, block, 2 * width // kv_heads - HEAD), BF16
        ),
        compiler_params=pltpu.CompilerParams(vmem_limit_bytes=LARGE_VMEM),
        cost_estimate=pl.CostEstimate(
            flops=2 * 10**10, bytes_accessed=2 * half * width, transcendentals=0
        ),
        name="project_other",
    )(x, turned, part, q)


def attention_kernel(
    side_ref, own_ref, other_ref, do_ref, dq_ref, dkv_own, dkv_other, acc
):
    steps, block, width = dq_ref.shape
    per = 2
    lanes = per * block
    pieces = block // TILE
    side = side_ref[0]
    acc[...] = jnp.zeros_like(acc)

    def gathered(ref, low, high, start, stride, size):
        return jnp.concatenate(
            [
                ref[z, :, start + j * stride : start + j * stride + size]
                for z in range(low, high)
                for j in range(pieces)
            ],
            axis=0,
        )

    def ids(ref, low, high, start):
        return jnp.concatenate(
            [
                ref[z, :, start : start + 128].astype(F32)[:, j : j + 1]
                for z in range(low, high)
                for j in range(pieces)
            ],
            axis=0,
        )

    def positions(shape, axis, low, which):
        n = lax.broadcasted_iota(jnp.int32, shape, axis)
        return 2 * n - (n & (block - 1)) + (per * block * low + block * which)

    q_end = pieces * HEAD
    diagonal = lax.broadcasted_iota(
        jnp.int32, (lanes, lanes), 0
    ) == lax.broadcasted_iota(jnp.int32, (lanes, lanes), 1)

    for z in range(0, steps, per):
        low, high = max(0, z - 4), z + per
        keys = (high - low) * block
        do = do_ref[z:high].reshape(lanes, width + HEAD)
        q = jnp.concatenate(
            [gathered(own_ref, z, high, 0, HEAD, HEAD), do[:, width:]], axis=0
        )
        do = jnp.concatenate([do[:, :HEAD], do[:, HEAD:width]], axis=0)
        seg_q = ids(own_ref, z, high, q_end + pieces * 2 * HEAD)
        seg_q = jnp.sum(jnp.where(diagonal, seg_q, 0.0), axis=0, keepdims=True)
        pos_q = positions((1, lanes), 1, z, side)
        parts = []
        total = 0.0
        weighted = 0.0
        for which, ref, start in ((0, own_ref, q_end), (1, other_ref, 0)):
            k = gathered(ref, low, high, start, 2 * HEAD, HEAD)
            v = gathered(ref, low, high, start + HEAD, 2 * HEAD, HEAD)
            seg_k = ids(ref, low, high, start + pieces * 2 * HEAD)
            key_side = side if which == 0 else 1 - side
            pos_k = positions((keys, lanes), 0, low, key_side)
            allowed = (seg_k == seg_q) & (pos_k <= pos_q)
            allowed = jnp.concatenate([allowed, allowed], axis=1)
            t = jnp.tanh(dot(k, q, 1, 1) * (SCALE / CAP))
            e = jnp.where(allowed, jnp.exp2(t * (CAP * LOG2E)), 0.0)
            dp = dot(v, do, 1, 1)
            total += jnp.sum(e, axis=0, keepdims=True)
            weighted += jnp.sum(e.astype(BF16).astype(F32) * dp, axis=0, keepdims=True)
            parts.append((k, t, e, dp))
        inverse = 1.0 / total
        delta = weighted * inverse
        scaled = inverse * SCALE
        dq = 0.0
        for which, (k, t, e, dp) in enumerate(parts):
            prob = (e * inverse).astype(BF16)
            ds = ((e * scaled) * (dp - delta) * (1.0 - t * t)).astype(BF16)
            acc[which, low * block : high * block, :HEAD] += dot(ds, q, 1, 0)
            acc[which, low * block : high * block, HEAD:] += dot(prob, do, 1, 0)
            dq += dot(ds, k, 0, 0)
        dq = dq.astype(BF16)
        dq_ref[z:high, :, :HEAD] = dq[:lanes].reshape(per, block, HEAD)
        dq_ref[z:high, :, HEAD:] = dq[lanes:].reshape(per, block, HEAD)
    dkv_own[...] = acc[0].reshape(dkv_own.shape)
    dkv_other[...] = acc[1].astype(BF16).reshape(dkv_other.shape)


def attention(side, own, other, do):
    steps, block, width = do.shape
    width -= HEAD
    return pl.pallas_call(
        attention_kernel,
        in_specs=[SMEM, VMEM, VMEM, VMEM],
        out_specs=[VMEM] * 3,
        out_shape=[
            jax.ShapeDtypeStruct((steps, block, width), BF16),
            jax.ShapeDtypeStruct((steps, block, width), F32),
            jax.ShapeDtypeStruct((steps, block, width), BF16),
        ],
        scratch_shapes=[pltpu.VMEM((2, steps * block, width), F32)],
        compiler_params=pltpu.CompilerParams(vmem_limit_bytes=LARGE_VMEM),
        cost_estimate=pl.CostEstimate(
            flops=3 * 10**9, bytes_accessed=6 * 2**20, transcendentals=1200000
        ),
        name="attend",
    )(side, own, other, do)


def run_copies(copies):
    for copy in copies:
        copy.start()
    for copy in copies:
        copy.wait()


def pick_kernel(index_ref, in_ref, *outs):
    for i, out in enumerate(outs):
        out[...] = in_ref[index_ref[i]]


def pick_rows(index, source):
    count, rest = index.shape[0], source.shape[1:]
    return pl.pallas_call(
        pick_kernel,
        in_specs=[SMEM, VMEM],
        out_specs=[VMEM] * count,
        out_shape=[jax.ShapeDtypeStruct(rest, source.dtype)] * count,
        compiler_params=pltpu.CompilerParams(vmem_limit_bytes=SMALL_VMEM),
        name="pick",
    )(index, source)


def pick_stacked_kernel(index_ref, in_ref, out_ref, sems):
    run_copies(
        [
            pltpu.make_async_copy(in_ref.at[index_ref[i]], out_ref.at[i], sems.at[i])
            for i in range(out_ref.shape[0])
        ]
    )


def pick_stacked(index, source):
    count, rest = index.shape[0], source.shape[1:]
    return pl.pallas_call(
        pick_stacked_kernel,
        in_specs=[SMEM, VMEM],
        out_specs=ANY,
        out_shape=jax.ShapeDtypeStruct((count,) + rest, source.dtype),
        scratch_shapes=[pltpu.SemaphoreType.DMA((count,))],
        compiler_params=pltpu.CompilerParams(vmem_limit_bytes=SMALL_VMEM),
        name="pick_stacked",
    )(index, source)


def place_q_kernel(index_ref, *refs):
    ins, out_ref, sems = refs[:-2], refs[-2], refs[-1]
    kv_heads, _, width = ins[0].shape

    def copy(source, s, h):
        return pltpu.make_async_copy(
            source.at[h], out_ref.at[s, :, pl.ds(h * width, width)], sems.at[s, h]
        )

    for s in range(out_ref.shape[0]):
        for i, source in enumerate(ins):

            @pl.when(index_ref[s] == i)
            def _():
                for h in range(kv_heads):
                    copy(source, s, h).start()

    for s in range(out_ref.shape[0]):
        for h in range(kv_heads):
            copy(ins[0], s, h).wait()


def place_q(index, sources):
    count = index.shape[0]
    kv_heads, block, width = sources[0].shape
    return pl.pallas_call(
        place_q_kernel,
        in_specs=[SMEM] + [VMEM] * len(sources),
        out_specs=ANY,
        out_shape=jax.ShapeDtypeStruct((count, block, kv_heads * width), BF16),
        scratch_shapes=[pltpu.SemaphoreType.DMA((count, kv_heads))],
        compiler_params=pltpu.CompilerParams(vmem_limit_bytes=SMALL_VMEM),
        name="place_q",
    )(index, *sources)


def place_kv_kernel(index_ref, in_ref, key_ref, value_ref, sems):
    copies = []
    for s in range(key_ref.shape[0]):
        for h in range(in_ref.shape[1]):
            for w, out_ref in enumerate((key_ref, value_ref)):
                copies.append(
                    pltpu.make_async_copy(
                        in_ref.at[index_ref[s], h, :, pl.ds(w * HEAD, HEAD)],
                        out_ref.at[s, :, pl.ds(h * HEAD, HEAD)],
                        sems.at[s, h, w],
                    )
                )
    run_copies(copies)


def place_kv(index, source):
    count = index.shape[0]
    _, kv_heads, block, _ = source.shape
    return pl.pallas_call(
        place_kv_kernel,
        in_specs=[SMEM, VMEM],
        out_specs=[ANY] * 2,
        out_shape=[jax.ShapeDtypeStruct((count, block, kv_heads * HEAD), BF16)] * 2,
        scratch_shapes=[pltpu.SemaphoreType.DMA((count, kv_heads, 2))],
        compiler_params=pltpu.CompilerParams(vmem_limit_bytes=SMALL_VMEM),
        name="place_kv",
    )(index, source)


def exchange(x, axis, groups=None):
    return lax.all_to_all(
        x, axis, split_axis=0, concat_axis=0, tiled=True, axis_index_groups=groups
    )


def on_device(
    queries, key_states, value_state_rows, segment_ids, output_grad, out_weight, destination
):
    rows, block, q_width = queries.shape
    kv_heads = key_states.shape[2] // HEAD
    units = rows * kv_heads
    n_ctx = lax.axis_size("ctx")
    groups = lax.axis_size("dp")
    pair = n_ctx // units
    ctx = lax.axis_index("ctx")
    tp = lax.axis_index("tp")
    group = lax.axis_index("dp")
    side = ctx % pair
    columns = [[z * pair + h for z in range(units)] for h in range(pair)]
    swap = [(z * pair + h, z * pair + 1 - h) for z in range(units) for h in range(pair)]

    other_grad = lax.ppermute(output_grad, "tp", [(0, 1), (1, 0)])

    own = pack(segment_ids, queries, key_states, value_state_rows)
    own = exchange(own, "ctx", columns)
    other = lax.ppermute(own[:, :, block // TILE * HEAD :], "ctx", swap)

    def partner(g, i, sign):
        chips = groups // 2
        return (g // 2 + sign * (i // 2) + chips) % chips * 2 + (g % 2 + i) % 2

    steps = jnp.arange(groups, dtype=jnp.int32)
    dest = destination.reshape(groups, rows)
    own_targets = lax.dynamic_slice_in_dim(dest, group, 1, 0) // rows

    def row_for(targets):
        return jnp.sum(
            jnp.where(
                own_targets == targets[:, None],
                jnp.arange(rows, dtype=jnp.int32)[None, :],
                0,
            ),
            axis=1,
        )

    wanted = group * rows + jnp.arange(rows, dtype=jnp.int32)
    recv_index = jnp.sum(
        jnp.where(
            destination[None, :] == wanted[:, None],
            jnp.arange(groups * rows, dtype=jnp.int32)[None, :] // rows,
            0,
        ),
        axis=1,
    )
    recv_step = jnp.sum(
        jnp.where(recv_index[:, None] == partner(group, steps, -1)[None, :], steps, 0),
        axis=1,
    )
    send_index = row_for(steps)
    send_step = row_for(partner(group, steps, 1))

    index = tp[None].astype(jnp.int32)
    part, turned = project_own(output_grad, out_weight, index)
    do = project_other(other_grad, turned, part, queries, kv_heads)
    do = exchange(do.reshape(units, block, do.shape[3]), "ctx", columns)

    dq, dkv_mine, dkv_theirs = attention(
        side[None].astype(jnp.int32), own, other, do
    )

    dq = exchange(dq, "ctx", columns)
    dkv_back = lax.ppermute(dkv_theirs, "ctx", swap)
    dkv = (dkv_mine + dkv_back.astype(F32)).astype(BF16)
    dkv, dq = lax.optimization_barrier((dkv, dq))
    dkv = exchange(dkv, "ctx", columns)

    def by_row(x):
        return x.reshape(rows, kv_heads, block, x.shape[2])

    sent = pick_rows(send_step, by_row(dq))
    got = [sent[0]]
    for i in range(1, groups):
        route = [(g, partner(g, i, 1)) for g in range(groups)]
        got.append(lax.ppermute(sent[i], "dp", route))
    dkv, *got = lax.optimization_barrier((dkv, *got))
    query_out = place_q(recv_step, got)
    dkv = exchange(pick_stacked(send_index, by_row(dkv)), "dp")
    key_out, value_out = place_kv(recv_index, dkv)
    return query_out, key_out, value_out


def solution(mesh):
    in_specs = (
        P("dp", "ctx", "tp"),
        P("dp", "ctx", "tp"),
        P("dp", "ctx", "tp"),
        P("dp", "ctx"),
        P("dp", "ctx", "tp"),
        P("tp", None),
        P(),
    )
    out_specs = (P("dp", "ctx", "tp"), P("dp", "ctx", "tp"), P("dp", "ctx", "tp"))
    return jax.shard_map(
        on_device, mesh=mesh, in_specs=in_specs, out_specs=out_specs, check_vma=False
    )
```

time: 170 us -> 139 us (0.82)
  Pallas kernels: 28.8 us -> 15.4 us
  starting transfers between devices: 49.6 us -> 42.1 us
  local copies, waits for them, and re-layouts: 8.7 us -> 5.19 us
  waiting for transfers between devices: 76.6 us -> 73.3 us
  other arithmetic: 4.12 us -> 1.48 us
    all_to_all x8 -> x5, starting transfers between devices: 48.6 us -> 23.9 us  [exchange(): lax.all_to_all(x, axis, split_axis=0, concat_axis=0, tiled=True, axis_ind...]
    all_to_all x8 -> x5, waiting for transfers between devices: 56 us -> 37.8 us  [exchange(): lax.all_to_all(x, axis, split_axis=0, concat_axis=0, tiled=True, axis_ind...]
    pallas_call x6 -> x8, Pallas kernels: 28.8 us -> 15.4 us  [the longest x1 4.16 us: attention(): pl.pallas_call(attention_kernel, in_specs=[SMEM, VMEM, VMEM, VMEM], out_s...]
    ppermute x1 -> x8, starting transfers between devices: 0.37 us -> 13.6 us  [the longest x7 11 us: on_device(): got.append(lax.ppermute(sent[i], 'dp', route))]
    ppermute x1 -> x8, waiting for transfers between devices: 10.2 us -> 20.8 us  [the longest x1 12.8 us: on_device(): other = lax.ppermute(own[:, :, block // TILE * HEAD:], 'ctx', swap)]
    ppermute x1, waiting for transfers between devices: 9.46 us -> 12.3 us  [on_device(): dkv_back = lax.ppermute(dkv_theirs, 'ctx', swap)]
    another operation x7 -> x0, local copies, waits for them, and re-layouts: 2.5 us -> none
    ppermute x1, starting transfers between devices: 0.28 us -> 2.54 us  [on_device(): dkv_back = lax.ppermute(dkv_theirs, 'ctx', swap)]
  transfers between devices with their start and end apart: 11 -> 15, of which waited for: 11 -> 11; matrix products, arithmetic and copies ran while one was open for 5% -> 1% of each run, Pallas kernels for 12% -> 6%
where the time goes in v2:
time: 139 us; the launch traced here: 138 us
  waiting for transfers between devices  73.3 us (53%)
  starting transfers between devices  42.1 us (30%)
  Pallas kernels  15.4 us (11%)
  local copies, waits for them, and re-layouts  5.19 us (4%)
  other arithmetic  1.48 us (1%)
    all_to_all x5, waiting for transfers between devices, exchange(): lax.all_to_all(x, axis, split_axis=0, concat_axis=0, tiled=True, axis_ind...  37.8 us
    all_to_all x5, starting transfers between devices, exchange(): lax.all_to_all(x, axis, split_axis=0, concat_axis=0, tiled=True, axis_ind...  23.9 us
    ppermute x1, waiting for transfers between devices, on_device(): other = lax.ppermute(own[:, :, block // TILE * HEAD:], 'ctx', swap)  12.8 us
    ppermute x1, waiting for transfers between devices, on_device(): dkv_back = lax.ppermute(dkv_theirs, 'ctx', swap)  12.3 us
    ppermute x7, starting transfers between devices, on_device(): got.append(lax.ppermute(sent[i], 'dp', route))  11 us
    ppermute x7, waiting for transfers between devices, on_device(): got.append(lax.ppermute(sent[i], 'dp', route))  8.02 us
    unnamed x10, local copies, waits for them, and re-layouts  5.07 us
    pallas_call x1, Pallas kernels, attention(): pl.pallas_call(attention_kernel, in_specs=[SMEM, VMEM, VMEM, VMEM], out_s...  4.16 us
  transfers between devices with their start and end apart: 15, of which 11 were waited for; matrix products, arithmetic and copies ran while one was open for 1% of the time, Pallas kernels for 6%

profile of v2, /device:TPU:1, one launch (start us, length us, event | category | flops | bytes accessed | tf_op | source)
XLA Modules:
  0.0 138.2 jit_solution(16158440778281416359)
XLA Ops:
  0.6 0.0 copy-start.2
  0.6 2.1 %collective-permute-start.1 = (bf16[4,64,1792]{2,1,0:T(8,128)(2,1)}, bf16[4,64,1792]{2,1,0:T(8,128)(2,1)S(1)}, u32[]{:S(2)}, u32[]{:S(2)}) collective-permute-start(bf16[4,64,1792]{2,1,0:T(8,128)(2,1)} %x_ref.1), channel_id=1, source_target_pairs={{0,1},{1,0},{2,3},{3,2},{4,5},{5,4},{6,7},{7,6},{8,9},{9,8},{10,11... | collective-permute-start | bytes 2752520 | tf_op jit(solution)/shard_map/ppermute | solution.py:392
  2.8 2.8 %pack.1 = bf16[8,16,3200]{2,1,0:T(8,128)(2,1)} custom-call(s32[4,64]{1,0:T(4,128)} %seg_ref.1, bf16[4,64,1024]{2,1,0:T(8,128)(2,1)} %q_ref.1, bf16[4,64,512]{2,1,0:T(8,128)(2,1)} %k_hbm.1, bf16[4,64,512]{2,1,0:T(8,128)(2,1)} %v_hbm.1), custom_call_target="tpu_custom_call" | custom-call | tf_op jit(solution)/shard_map/pack/pallas_call | solution.py:76
  5.6 8.2 %all-to-all-start = ((bf16[8,16,3200]{2,1,0:T(8,128)(2,1)}), bf16[8,16,3200]{2,1,0:T(8,128)(2,1)S(1)}, u32[]{:S(2)}, u32[]{:S(2)}) async-start(bf16[8,16,3200]{2,1,0:T(8,128)(2,1)} %pack.1), calls=%async_computation | async-start | bytes 1638400 | tf_op jit(solution)/shard_map/all_to_all | solution.py:371
  13.8 0.0 copy-start
  13.8 3.1 %copy-done = bf16[1024,3584]{1,0:T(8,128)(2,1)S(1)} copy-done((bf16[1024,3584]{1,0:T(8,128)(2,1)S(1)}, bf16[1024,3584]{1,0:T(8,128)(2,1)}, u32[]{:S(2)}) %copy-start) | copy-done | bytes 7340056
  16.9 0.0 copy-start.1
  16.9 1.2 copy-done.1
  18.1 1.3 project_own.1
  19.4 2.4 %collective-permute-done.1.x_ref = bf16[4,64,1792]{2,1,0:T(8,128)(2,1)S(1)} collective-permute-done((bf16[4,64,1792]{2,1,0:T(8,128)(2,1)}, bf16[4,64,1792]{2,1,0:T(8,128)(2,1)S(1)}, u32[]{:S(2)}, u32[]{:S(2)}) %collective-permute-start.1) | collective-permute-done | bytes 917536 | tf_op jit(solution)/shard_map/ppermute | solution.py:392
  21.8 0.0 copy-done.2
  21.8 2.0 %project_other.1 = bf16[4,2,64,768]{3,2,1,0:T(8,128)(2,1)} custom-call(bf16[4,64,1792]{2,1,0:T(8,128)(2,1)S(1)} %collective-permute-done.1.x_ref, bf16[1792,1024]{1,0:T(8,128)(2,1)S(1)} %get-tuple-element.29.turned_ref, f32[256,1024]{1,0:T(8,128)S(1)} %get-tuple-element.30.part_ref, bf16[4,64,1024]{2,1,0:T(8,128)(2,1)S(1)} %copy-done.2), custom_call_target="tpu_custom_call" | custom-call | flops 20000000000 | bytes 3670016 | tf_op jit(solution)/shard_map/project_other/pallas_call | solution.py:139
  23.9 14.2 %all-to-all-done.own_ref = bf16[8,16,3200]{2,1,0:T(8,128)(2,1)S(1)} async-done(((bf16[8,16,3200]{2,1,0:T(8,128)(2,1)}), bf16[8,16,3200]{2,1,0:T(8,128)(2,1)S(1)}, u32[]{:S(2)}, u32[]{:S(2)}) %all-to-all-start) | async-done | bytes 819232 | tf_op jit(solution)/shard_map/all_to_all | solution.py:371
  38.1 3.5 %all-to-all-start.1 = ((bf16[8,64,768]{2,1,0:T(8,128)(2,1)}), bf16[8,64,768]{2,1,0:T(8,128)(2,1)S(1)}, u32[]{:S(2)}, u32[]{:S(2)}) async-start(bf16[8,64,768]{2,1,0:T(8,128)(2,1)} %bitcast.2), calls=%async_computation.1 | async-start | bytes 1572864 | tf_op jit(solution)/shard_map/all_to_all | solution.py:371
  41.7 2.5 %collective-permute-start = (bf16[8,16,2176]{2,1,0:T(8,128)(2,1)S(1)}, bf16[8,16,2176]{2,1,0:T(8,128)(2,1)S(1)}, u32[]{:S(2)}, u32[]{:S(2)}) collective-permute-start(bf16[8,16,2176]{2,1,0:T(8,128)(2,1)S(1)} %slice.4), channel_id=1, source_target_pairs={{0,2},{2,0},{4,6},{6,4},{8,10},{10,8},{12,14},{14,12},{16,18},{18,... | collective-permute-start | bytes 1671176 | tf_op jit(solution)/shard_map/ppermute | solution.py:396
  44.2 12.8 %collective-permute-done.other_ref = bf16[8,16,2176]{2,1,0:T(8,128)(2,1)S(1)} collective-permute-done((bf16[8,16,2176]{2,1,0:T(8,128)(2,1)S(1)}, bf16[8,16,2176]{2,1,0:T(8,128)(2,1)S(1)}, u32[]{:S(2)}, u32[]{:S(2)}) %collective-permute-start) | collective-permute-done | bytes 557088 | tf_op jit(solution)/shard_map/ppermute | solution.py:396
  57.0 8.2 %all-to-all-done.1.do_ref = bf16[8,64,768]{2,1,0:T(8,128)(2,1)S(1)} async-done(((bf16[8,64,768]{2,1,0:T(8,128)(2,1)}), bf16[8,64,768]{2,1,0:T(8,128)(2,1)S(1)}, u32[]{:S(2)}, u32[]{:S(2)}) %all-to-all-start.1) | async-done | bytes 786464 | tf_op jit(solution)/shard_map/all_to_all | solution.py:371
  65.2 0.0 copy-start.4
  65.2 4.2 %attend.1 = (bf16[8,64,512]{2,1,0:T(8,128)(2,1)}, f32[8,64,512]{2,1,0:T(8,128)S(1)}, bf16[8,64,512]{2,1,0:T(8,128)(2,1)S(1)}) custom-call(s32[1]{0:T(128)} %bitcast.side_ref, bf16[8,16,3200]{2,1,0:T(8,128)(2,1)S(1)} %all-to-all-done.own_ref, bf16[8,16,2176]{2,1,0:T(8,128)(2,1)S(1)} %collective-permute-done.other_ref, ...), custom_call_target="tpu_custom_call" | custom-call | flops 3000000000 | bytes 6291456 | tf_op jit(solution)/shard_map/attend/pallas_call | solution.py:241
  69.3 0.0 copy-start.3
  69.3 0.8 copy-done.3
  70.2 3.5 %all-to-all-start.2 = ((bf16[8,64,512]{2,1,0:T(8,128)(2,1)}), bf16[8,64,512]{2,1,0:T(8,128)(2,1)S(1)}, u32[]{:S(2)}, u32[]{:S(2)}) async-start(bf16[8,64,512]{2,1,0:T(8,128)(2,1)} %get-tuple-element.33), calls=%async_computation.2 | async-start | bytes 1048576 | tf_op jit(solution)/shard_map/all_to_all | solution.py:371
  73.7 2.5 %collective-permute-start.2 = (bf16[8,64,512]{2,1,0:T(8,128)(2,1)}, bf16[8,64,512]{2,1,0:T(8,128)(2,1)S(1)}, u32[]{:S(2)}, u32[]{:S(2)}) collective-permute-start(bf16[8,64,512]{2,1,0:T(8,128)(2,1)} %copy-done.3), channel_id=1, source_target_pairs={{0,2},{2,0},{4,6},{6,4},{8,10},{10,8},{12,14},{14,12},{16,18},{18,... | collective-permute-start | bytes 1572872 | tf_op jit(solution)/shard_map/ppermute | solution.py:442
  76.2 12.3 %collective-permute-done.2 = bf16[8,64,512]{2,1,0:T(8,128)(2,1)S(1)} collective-permute-done((bf16[8,64,512]{2,1,0:T(8,128)(2,1)}, bf16[8,64,512]{2,1,0:T(8,128)(2,1)S(1)}, u32[]{:S(2)}, u32[]{:S(2)}) %collective-permute-start.2) | collective-permute-done | bytes 524320 | tf_op jit(solution)/shard_map/ppermute | solution.py:442
  88.5 1.0 add_convert_fusion
  89.4 2.1 %all-to-all-done.2 = bf16[8,64,512]{2,1,0:T(8,128)(2,1)S(1)} async-done(((bf16[8,64,512]{2,1,0:T(8,128)(2,1)}), bf16[8,64,512]{2,1,0:T(8,128)(2,1)S(1)}, u32[]{:S(2)}, u32[]{:S(2)}) %all-to-all-start.2) | async-done | bytes 524320 | tf_op jit(solution)/shard_map/all_to_all | solution.py:371
  91.5 4.1 %all-to-all-start.3 = ((bf16[8,64,512]{2,1,0:T(8,128)(2,1)}), bf16[8,64,512]{2,1,0:T(8,128)(2,1)S(1)}, u32[]{:S(2)}, u32[]{:S(2)}) async-start(bf16[8,64,512]{2,1,0:T(8,128)(2,1)} %add_convert_fusion), calls=%async_computation.3 | async-start | bytes 1048576 | tf_op jit(solution)/shard_map/all_to_all | solution.py:371
  95.6 0.0 copy-done.4
  95.6 0.1 reshape.145
  95.7 0.1 select_reduce_fusion
  95.8 0.6 pick.1
  96.4 2.0 %collective-permute-start.3 = (bf16[2,64,512]{2,1,0:T(8,128)(2,1)S(1)}, bf16[2,64,512]{2,1,0:T(8,128)(2,1)S(1)}, u32[]{:S(2)}, u32[]{:S(2)}) collective-permute-start(bf16[2,64,512]{2,1,0:T(8,128)(2,1)S(1)} %get-tuple-element.37), channel_id=1, source_target_pairs={{0,32},{32,0},{64,96},{96,64},{128,160},{160,128},{192,224},{224,1... | collective-permute-start | bytes 393224 | tf_op jit(solution)/shard_map/ppermute | solution.py:454
  98.4 1.3 collective-permute-start.4
  99.8 1.5 %collective-permute-start.5 = (bf16[2,64,512]{2,1,0:T(8,128)(2,1)S(1)}, bf16[2,64,512]{2,1,0:T(8,128)(2,1)S(1)}, u32[]{:S(2)}, u32[]{:S(2)}) collective-permute-start(bf16[2,64,512]{2,1,0:T(8,128)(2,1)S(1)} %get-tuple-element.39), channel_id=1, source_target_pairs={{0,96},{32,64},{64,160},{96,128},{128,224},{160,192},{192,32},{224... | collective-permute-start | bytes 393224 | tf_op jit(solution)/shard_map/ppermute | solution.py:454
  101.3 1.3 collective-permute-start.6
  102.6 2.0 %collective-permute-start.7 = (bf16[2,64,512]{2,1,0:T(8,128)(2,1)S(1)}, bf16[2,64,512]{2,1,0:T(8,128)(2,1)S(1)}, u32[]{:S(2)}, u32[]{:S(2)}) collective-permute-start(bf16[2,64,512]{2,1,0:T(8,128)(2,1)S(1)} %get-tuple-element.41), channel_id=1, source_target_pairs={{0,160},{32,128},{64,224},{96,192},{128,32},{160,0},{192,96},{224,... | collective-permute-start | bytes 393224 | tf_op jit(solution)/shard_map/ppermute | solution.py:454
  104.6 0.0 collective-permute-done.3.refs_1_
  104.6 1.4 collective-permute-start.8
  106.0 0.0 collective-permute-done.4.refs_2_
  106.0 1.5 %collective-permute-start.9 = (bf16[2,64,512]{2,1,0:T(8,128)(2,1)S(1)}, bf16[2,64,512]{2,1,0:T(8,128)(2,1)S(1)}, u32[]{:S(2)}, u32[]{:S(2)}) collective-permute-start(bf16[2,64,512]{2,1,0:T(8,128)(2,1)S(1)} %get-tuple-element.43), channel_id=1, source_target_pairs={{0,224},{32,192},{64,32},{96,0},{128,96},{160,64},{192,160},{224,1... | collective-permute-start | bytes 393224 | tf_op jit(solution)/shard_map/ppermute | solution.py:454
  107.5 0.6 collective-permute-done.5.refs_3_
  108.0 3.5 %collective-permute-done.6.refs_4_ = bf16[2,64,512]{2,1,0:T(8,128)(2,1)S(1)} collective-permute-done((bf16[2,64,512]{2,1,0:T(8,128)(2,1)S(1)}, bf16[2,64,512]{2,1,0:T(8,128)(2,1)S(1)}, u32[]{:S(2)}, u32[]{:S(2)}) %collective-permute-start.6) | collective-permute-done | bytes 131104 | tf_op jit(solution)/shard_map/ppermute | solution.py:454
  111.6 3.0 %collective-permute-done.7.refs_5_ = bf16[2,64,512]{2,1,0:T(8,128)(2,1)S(1)} collective-permute-done((bf16[2,64,512]{2,1,0:T(8,128)(2,1)S(1)}, bf16[2,64,512]{2,1,0:T(8,128)(2,1)S(1)}, u32[]{:S(2)}, u32[]{:S(2)}) %collective-permute-start.7) | collective-permute-done | bytes 131104 | tf_op jit(solution)/shard_map/ppermute | solution.py:454
  114.6 0.0 collective-permute-done.8.refs_6_
  114.6 0.9 collective-permute-done.9.refs_7_
  115.5 0.0 all-to-all-done.3
  115.5 1.6 %pick_stacked.1 = bf16[8,2,64,512]{3,2,1,0:T(8,128)(2,1)} custom-call(s32[8]{0:T(128)S(1)} %get-tuple-element.55.index_ref, bf16[4,2,64,512]{3,2,1,0:T(8,128)(2,1)S(1)} %bitcast.7), custom_call_target="tpu_custom_call" | custom-call | tf_op jit(solution)/shard_map/pick_stacked/pallas_call | solution.py:294
  117.1 4.6 %all-to-all-start.4 = ((bf16[8,2,64,512]{3,2,1,0:T(8,128)(2,1)}), bf16[8,2,64,512]{3,2,1,0:T(8,128)(2,1)S(1)}, u32[]{:S(2)}, u32[]{:S(2)}) async-start(bf16[8,2,64,512]{3,2,1,0:T(8,128)(2,1)} %pick_stacked.1), calls=%async_computation.4 | async-start | bytes 2097152 | tf_op jit(solution)/shard_map/all_to_all | solution.py:371
  121.7 0.2 select_reduce_fusion.3.index_ref
  121.9 0.2 select_reduce_fusion.2.index_ref
  122.0 1.4 %place_q.1 = bf16[4,64,1024]{2,1,0:T(8,128)(2,1)} custom-call(s32[4]{0:T(128)S(1)} %select_reduce_fusion.2.index_ref, bf16[2,64,512]{2,1,0:T(8,128)(2,1)S(1)} %get-tuple-element.44.refs_0_, bf16[2,64,512]{2,1,0:T(8,128)(2,1)S(1)} %collective-permute-done.3.refs_1_, bf16[2,64,512]{2,1,0:T(8,128)(2,1)S(1)} %collective-permute-done.4.refs_2_, ...), custom_call_target="tpu_custom_call" | custom-call | tf_op jit(solution)/shard_map/place_q/pallas_call | solution.py:330
  123.4 13.3 %all-to-all-done.4.in_ref = bf16[8,2,64,512]{3,2,1,0:T(8,128)(2,1)S(1)} async-done(((bf16[8,2,64,512]{3,2,1,0:T(8,128)(2,1)}), bf16[8,2,64,512]{3,2,1,0:T(8,128)(2,1)S(1)}, u32[]{:S(2)}, u32[]{:S(2)}) %all-to-all-start.4) | async-done | bytes 1048608 | tf_op jit(solution)/shard_map/all_to_all | solution.py:371
  136.7 1.5 %place_kv.1 = (bf16[4,64,512]{2,1,0:T(8,128)(2,1)}, bf16[4,64,512]{2,1,0:T(8,128)(2,1)}) custom-call(s32[4]{0:T(128)S(1)} %select_reduce_fusion.3.index_ref, bf16[8,2,64,512]{3,2,1,0:T(8,128)(2,1)S(1)} %all-to-all-done.4.in_ref), custom_call_target="tpu_custom_call" | custom-call | tf_op jit(solution)/shard_map/place_kv/pallas_call | solution.py:359
  (6 shorter events, 0.1 us)
Async XLA Ops:
  0.6 21.2 %copy-start.2 = (bf16[4,64,1024]{2,1,0:T(8,128)(2,1)S(1)}, bf16[4,64,1024]{2,1,0:T(8,128)(2,1)}, u32[]{:S(2)}) copy-start(bf16[4,64,1024]{2,1,0:T(8,128)(2,1)} %q_ref.1) | copy-start | bytes 1572868
  0.6 21.2 %collective-permute-start.1 = (bf16[4,64,1792]{2,1,0:T(8,128)(2,1)}, bf16[4,64,1792]{2,1,0:T(8,128)(2,1)S(1)}, u32[]{:S(2)}, u32[]{:S(2)}) collective-permute-start(bf16[4,64,1792]{2,1,0:T(8,128)(2,1)} %x_ref.1), channel_id=1, source_target_pairs={{0,1},{1,0},{2,3},{3,2},{4,5},{5,4},{6,7},{7,6},{8,9},{9,8},{10,11... | collective-permute-start | bytes 2752520 | tf_op jit(solution)/shard_map/ppermute | solution.py:392
  5.6 32.5 %all-to-all-start = ((bf16[8,16,3200]{2,1,0:T(8,128)(2,1)}), bf16[8,16,3200]{2,1,0:T(8,128)(2,1)S(1)}, u32[]{:S(2)}, u32[]{:S(2)}) async-start(bf16[8,16,3200]{2,1,0:T(8,128)(2,1)} %pack.1), calls=%async_computation | async-start | bytes 1638400 | tf_op jit(solution)/shard_map/all_to_all | solution.py:371
  13.8 3.1 %copy-start = (bf16[1024,3584]{1,0:T(8,128)(2,1)S(1)}, bf16[1024,3584]{1,0:T(8,128)(2,1)}, u32[]{:S(2)}) copy-start(bf16[1024,3584]{1,0:T(8,128)(2,1)} %weight_ref.1) | copy-start | bytes 22020100
  16.9 1.2 copy-start.1
  38.1 27.1 %all-to-all-start.1 = ((bf16[8,64,768]{2,1,0:T(8,128)(2,1)}), bf16[8,64,768]{2,1,0:T(8,128)(2,1)S(1)}, u32[]{:S(2)}, u32[]{:S(2)}) async-start(bf16[8,64,768]{2,1,0:T(8,128)(2,1)} %bitcast.2), calls=%async_computation.1 | async-start | bytes 1572864 | tf_op jit(solution)/shard_map/all_to_all | solution.py:371
  41.7 15.3 %collective-permute-start = (bf16[8,16,2176]{2,1,0:T(8,128)(2,1)S(1)}, bf16[8,16,2176]{2,1,0:T(8,128)(2,1)S(1)}, u32[]{:S(2)}, u32[]{:S(2)}) collective-permute-start(bf16[8,16,2176]{2,1,0:T(8,128)(2,1)S(1)} %slice.4), channel_id=1, source_target_pairs={{0,2},{2,0},{4,6},{6,4},{8,10},{10,8},{12,14},{14,12},{16,18},{18,... | collective-permute-start | bytes 1671176 | tf_op jit(solution)/shard_map/ppermute | solution.py:396
  65.2 30.4 %copy-start.4 = (s32[32]{0:T(128)S(1)}, s32[32]{0:T(128)}, u32[]{:S(2)}) copy-start(s32[32]{0:T(128)} %param.13) | copy-start | bytes 388
  69.3 0.8 copy-start.3
  70.2 21.4 %all-to-all-start.2 = ((bf16[8,64,512]{2,1,0:T(8,128)(2,1)}), bf16[8,64,512]{2,1,0:T(8,128)(2,1)S(1)}, u32[]{:S(2)}, u32[]{:S(2)}) async-start(bf16[8,64,512]{2,1,0:T(8,128)(2,1)} %get-tuple-element.33), calls=%async_computation.2 | async-start | bytes 1048576 | tf_op jit(solution)/shard_map/all_to_all | solution.py:371
  73.7 14.8 %collective-permute-start.2 = (bf16[8,64,512]{2,1,0:T(8,128)(2,1)}, bf16[8,64,512]{2,1,0:T(8,128)(2,1)S(1)}, u32[]{:S(2)}, u32[]{:S(2)}) collective-permute-start(bf16[8,64,512]{2,1,0:T(8,128)(2,1)} %copy-done.3), channel_id=1, source_target_pairs={{0,2},{2,0},{4,6},{6,4},{8,10},{10,8},{12,14},{14,12},{16,18},{18,... | collective-permute-start | bytes 1572872 | tf_op jit(solution)/shard_map/ppermute | solution.py:442
  91.5 24.0 %all-to-all-start.3 = ((bf16[8,64,512]{2,1,0:T(8,128)(2,1)}), bf16[8,64,512]{2,1,0:T(8,128)(2,1)S(1)}, u32[]{:S(2)}, u32[]{:S(2)}) async-start(bf16[8,64,512]{2,1,0:T(8,128)(2,1)} %add_convert_fusion), calls=%async_computation.3 | async-start | bytes 1048576 | tf_op jit(solution)/shard_map/all_to_all | solution.py:371
  96.4 8.2 %collective-permute-start.3 = (bf16[2,64,512]{2,1,0:T(8,128)(2,1)S(1)}, bf16[2,64,512]{2,1,0:T(8,128)(2,1)S(1)}, u32[]{:S(2)}, u32[]{:S(2)}) collective-permute-start(bf16[2,64,512]{2,1,0:T(8,128)(2,1)S(1)} %get-tuple-element.37), channel_id=1, source_target_pairs={{0,32},{32,0},{64,96},{96,64},{128,160},{160,128},{192,224},{224,1... | collective-permute-start | bytes 393224 | tf_op jit(solution)/shard_map/ppermute | solution.py:454
  98.4 7.5 %collective-permute-start.4 = (bf16[2,64,512]{2,1,0:T(8,128)(2,1)S(1)}, bf16[2,64,512]{2,1,0:T(8,128)(2,1)S(1)}, u32[]{:S(2)}, u32[]{:S(2)}) collective-permute-start(bf16[2,64,512]{2,1,0:T(8,128)(2,1)S(1)} %get-tuple-element.38), channel_id=1, source_target_pairs={{0,64},{32,96},{64,128},{96,160},{128,192},{160,224},{192,0},{224,... | collective-permute-start | bytes 393224 | tf_op jit(solution)/shard_map/ppermute | solution.py:454
  99.8 8.3 %collective-permute-start.5 = (bf16[2,64,512]{2,1,0:T(8,128)(2,1)S(1)}, bf16[2,64,512]{2,1,0:T(8,128)(2,1)S(1)}, u32[]{:S(2)}, u32[]{:S(2)}) collective-permute-start(bf16[2,64,512]{2,1,0:T(8,128)(2,1)S(1)} %get-tuple-element.39), channel_id=1, source_target_pairs={{0,96},{32,64},{64,160},{96,128},{128,224},{160,192},{192,32},{224... | collective-permute-start | bytes 393224 | tf_op jit(solution)/shard_map/ppermute | solution.py:454
  101.3 10.3 %collective-permute-start.6 = (bf16[2,64,512]{2,1,0:T(8,128)(2,1)S(1)}, bf16[2,64,512]{2,1,0:T(8,128)(2,1)S(1)}, u32[]{:S(2)}, u32[]{:S(2)}) collective-permute-start(bf16[2,64,512]{2,1,0:T(8,128)(2,1)S(1)} %get-tuple-element.40), channel_id=1, source_target_pairs={{0,128},{32,160},{64,192},{96,224},{128,0},{160,32},{192,64},{224,... | collective-permute-start | bytes 393224 | tf_op jit(solution)/shard_map/ppermute | solution.py:454
  102.6 12.0 %collective-permute-start.7 = (bf16[2,64,512]{2,1,0:T(8,128)(2,1)S(1)}, bf16[2,64,512]{2,1,0:T(8,128)(2,1)S(1)}, u32[]{:S(2)}, u32[]{:S(2)}) collective-permute-start(bf16[2,64,512]{2,1,0:T(8,128)(2,1)S(1)} %get-tuple-element.41), channel_id=1, source_target_pairs={{0,160},{32,128},{64,224},{96,192},{128,32},{160,0},{192,96},{224,... | collective-permute-start | bytes 393224 | tf_op jit(solution)/shard_map/ppermute | solution.py:454
  104.6 10.0 %collective-permute-start.8 = (bf16[2,64,512]{2,1,0:T(8,128)(2,1)S(1)}, bf16[2,64,512]{2,1,0:T(8,128)(2,1)S(1)}, u32[]{:S(2)}, u32[]{:S(2)}) collective-permute-start(bf16[2,64,512]{2,1,0:T(8,128)(2,1)S(1)} %get-tuple-element.42), channel_id=1, source_target_pairs={{0,192},{32,224},{64,0},{96,32},{128,64},{160,96},{192,128},{224,1... | collective-permute-start | bytes 393224 | tf_op jit(solution)/shard_map/ppermute | solution.py:454
  106.0 9.5 %collective-permute-start.9 = (bf16[2,64,512]{2,1,0:T(8,128)(2,1)S(1)}, bf16[2,64,512]{2,1,0:T(8,128)(2,1)S(1)}, u32[]{:S(2)}, u32[]{:S(2)}) collective-permute-start(bf16[2,64,512]{2,1,0:T(8,128)(2,1)S(1)} %get-tuple-element.43), channel_id=1, source_target_pairs={{0,224},{32,192},{64,32},{96,0},{128,96},{160,64},{192,160},{224,1... | collective-permute-start | bytes 393224 | tf_op jit(solution)/shard_map/ppermute | solution.py:454
  117.1 19.7 %all-to-all-start.4 = ((bf16[8,2,64,512]{3,2,1,0:T(8,128)(2,1)}), bf16[8,2,64,512]{3,2,1,0:T(8,128)(2,1)S(1)}, u32[]{:S(2)}, u32[]{:S(2)}) async-start(bf16[8,2,64,512]{3,2,1,0:T(8,128)(2,1)} %pick_stacked.1), calls=%async_computation.4 | async-start | bytes 2097152 | tf_op jit(solution)/shard_map/all_to_all | solution.py:371

commit v3 on v2

--- a/solution.py
+++ b/solution.py
@@ -12,8 +12,9 @@
 F32 = jnp.float32
 BF16 = jnp.bfloat16
 TILE = 16
+ORDER = (0, 2, 4, 6, 1, 3, 5, 7)
+SLOT = tuple(ORDER.index(z) for z in range(len(ORDER)))
 SMALL_VMEM = 8 * 1024 * 1024
-WHOLE_VMEM = 60 * 1024 * 1024
 LARGE_VMEM = 28 * 1024 * 1024
 
 
@@ -26,23 +27,22 @@
 ANY = pl.BlockSpec(memory_space=pl.ANY)
 
 
-def pack_kernel(seg_ref, q_hbm, k_hbm, v_hbm, out_ref, q_ref, k_ref, v_ref, sems):
-    rows, block, q_width = q_ref.shape
-    kv_heads = k_ref.shape[2] // HEAD
-    width = q_width // kv_heads
+def pack_kernel(seg_hbm, k_hbm, v_hbm, out_ref, seg_ref, k_ref, v_ref, sems):
+    rows, block, kv_width = k_ref.shape
+    kv_heads = kv_width // HEAD
     pieces = block // TILE
     copies = [
         pltpu.make_async_copy(source, target, sems.at[i])
         for i, (source, target) in enumerate(
-            ((q_hbm, q_ref), (k_hbm, k_ref), (v_hbm, v_ref))
+            ((seg_hbm, seg_ref), (k_hbm, k_ref), (v_hbm, v_ref))
         )
     ]
     for copy in copies:
         copy.start()
+    copies[0].wait()
     place = lax.broadcasted_iota(jnp.int32, (TILE, block), 1)
     row = lax.broadcasted_iota(jnp.int32, (TILE, block), 0)
     lane = lax.broadcasted_iota(jnp.int32, (TILE, 128), 1)
-    ids = []
     for r in range(rows):
         spread = jnp.broadcast_to(seg_ref[r : r + 1], (TILE, block)).astype(F32)
         columns = jnp.zeros((TILE, 128), F32)
@@ -51,42 +51,39 @@
                 jnp.where(place == row + j * TILE, spread, 0.0), axis=1, keepdims=True
             )
             columns = jnp.where(lane == j, column, columns)
-        ids.append(columns.astype(BF16))
-    for copy in copies:
-        copy.wait()
+        for h in range(kv_heads):
+            out_ref[r * kv_heads + h, :, pieces * 2 * HEAD :] = columns.astype(BF16)
+    copies[1].wait()
+    copies[2].wait()
     for r in range(rows):
         for h in range(kv_heads):
             u = r * kv_heads + h
             heads = slice(h * HEAD, (h + 1) * HEAD)
             for j in range(pieces):
                 at = slice(j * TILE, (j + 1) * TILE)
-                k_at = pieces * HEAD + j * 2 * HEAD
-                out_ref[u, :, j * HEAD : (j + 1) * HEAD] = q_ref[
-                    r, at, h * width : h * width + HEAD
-                ]
+                k_at = j * 2 * HEAD
                 out_ref[u, :, k_at : k_at + HEAD] = k_ref[r, at, heads]
                 out_ref[u, :, k_at + HEAD : k_at + 2 * HEAD] = v_ref[r, at, heads]
-            out_ref[u, :, pieces * 3 * HEAD :] = ids[r]
-
-
-def pack(seg, q, k, v):
-    rows, block, _ = q.shape
-    kv_heads = k.shape[2] // HEAD
-    lanes = block // TILE * 3 * HEAD + 128
+
+
+def pack(seg, k, v):
+    rows, block, kv_width = k.shape
+    kv_heads = kv_width // HEAD
+    lanes = block // TILE * 2 * HEAD + 128
     return pl.pallas_call(
         pack_kernel,
-        in_specs=[VMEM, ANY, ANY, ANY],
+        in_specs=[ANY] * 3,
         out_specs=VMEM,
         out_shape=jax.ShapeDtypeStruct((rows * kv_heads, TILE, lanes), BF16),
         scratch_shapes=[
-            pltpu.VMEM(q.shape, BF16),
+            pltpu.VMEM(seg.shape, jnp.int32),
             pltpu.VMEM(k.shape, BF16),
             pltpu.VMEM(v.shape, BF16),
             pltpu.SemaphoreType.DMA((3,)),
         ],
-        compiler_params=pltpu.CompilerParams(vmem_limit_bytes=WHOLE_VMEM),
+        compiler_params=pltpu.CompilerParams(vmem_limit_bytes=SMALL_VMEM),
         name="pack",
-    )(seg, q, k, v)
+    )(*(pltpu.with_memory_space_constraint(x, pltpu.HBM) for x in (seg, k, v)))
 
 
 def own_half_kernel(index_ref, x_ref, weight_ref, out_ref, turned_ref):
@@ -128,53 +125,54 @@
     x = x_ref[...].reshape(rows * block, half)
     for h in range(kv_heads):
         at = slice(h * width, (h + 1) * width)
+        out_ref[:, h, :, :width] = q_ref[:, :, at]
         total = part_ref[:, at] + dot(x, turned_ref[:, at], 1, 0)
-        out_ref[:, h, :, :width] = total.astype(BF16).reshape(rows, block, width)
-        out_ref[:, h, :, width:] = q_ref[:, :, h * width + HEAD : (h + 1) * width]
+        out_ref[:, h, :, width:] = total.astype(BF16).reshape(rows, block, width)
 
 
 def project_other(x, turned, part, q, kv_heads):
     rows, block, half = x.shape
-    width = turned.shape[1]
+    total = turned.shape[1]
     return pl.pallas_call(
         other_half_kernel,
         in_specs=[VMEM] * 4,
         out_specs=VMEM,
         out_shape=jax.ShapeDtypeStruct(
-            (rows, kv_heads, block, 2 * width // kv_heads - HEAD), BF16
+            (rows, kv_heads, block, 2 * total // kv_heads), BF16
         ),
         compiler_params=pltpu.CompilerParams(vmem_limit_bytes=LARGE_VMEM),
         cost_estimate=pl.CostEstimate(
-            flops=2 * 10**10, bytes_accessed=2 * half * width, transcendentals=0
+            flops=2 * rows * block * half * total,
+            bytes_accessed=2 * half * total,
+            transcendentals=0,
         ),
         name="project_other",
     )(x, turned, part, q)
 
 
 def attention_kernel(
-    side_ref, own_ref, other_ref, do_ref, dq_ref, dkv_own, dkv_other, acc
+    side_ref, own_ref, other_ref, qd_ref, dq_ref, dkv_own, dkv_other, acc
 ):
     steps, block, width = dq_ref.shape
     per = 2
     lanes = per * block
     pieces = block // TILE
     side = side_ref[0]
-    acc[...] = jnp.zeros_like(acc)
-
-    def gathered(ref, low, high, start, stride, size):
+
+    def gathered(ref, low, high, start):
         return jnp.concatenate(
             [
-                ref[z, :, start + j * stride : start + j * stride + size]
+                ref[SLOT[z], :, start + j * 2 * HEAD : start + j * 2 * HEAD + HEAD]
                 for z in range(low, high)
                 for j in range(pieces)
             ],
             axis=0,
         )
 
-    def ids(ref, low, high, start):
+    def ids(ref, low, high):
         return jnp.concatenate(
             [
-                ref[z, :, start : start + 128].astype(F32)[:, j : j + 1]
+                ref[SLOT[z], :, pieces * 2 * HEAD :].astype(F32)[:, j : j + 1]
                 for z in range(low, high)
                 for j in range(pieces)
             ],
@@ -185,67 +183,80 @@
         n = lax.broadcasted_iota(jnp.int32, shape, axis)
         return 2 * n - (n & (block - 1)) + (per * block * low + block * which)
 
-    q_end = pieces * HEAD
     diagonal = lax.broadcasted_iota(
         jnp.int32, (lanes, lanes), 0
     ) == lax.broadcasted_iota(jnp.int32, (lanes, lanes), 1)
 
     for z in range(0, steps, per):
         low, high = max(0, z - 4), z + per
-        keys = (high - low) * block
-        do = do_ref[z:high].reshape(lanes, width + HEAD)
-        q = jnp.concatenate(
-            [gathered(own_ref, z, high, 0, HEAD, HEAD), do[:, width:]], axis=0
-        )
-        do = jnp.concatenate([do[:, :HEAD], do[:, HEAD:width]], axis=0)
-        seg_q = ids(own_ref, z, high, q_end + pieces * 2 * HEAD)
+        qd = jnp.concatenate([qd_ref[SLOT[i]] for i in range(z, high)], axis=0)
+        q = jnp.concatenate([qd[:, :HEAD], qd[:, HEAD:width]], axis=0)
+        do = jnp.concatenate(
+            [qd[:, width : width + HEAD], qd[:, width + HEAD :]], axis=0
+        )
+        seg_q = ids(own_ref, z, high)
         seg_q = jnp.sum(jnp.where(diagonal, seg_q, 0.0), axis=0, keepdims=True)
         pos_q = positions((1, lanes), 1, z, side)
         parts = []
         total = 0.0
         weighted = 0.0
-        for which, ref, start in ((0, own_ref, q_end), (1, other_ref, 0)):
-            k = gathered(ref, low, high, start, 2 * HEAD, HEAD)
-            v = gathered(ref, low, high, start + HEAD, 2 * HEAD, HEAD)
-            seg_k = ids(ref, low, high, start + pieces * 2 * HEAD)
-            key_side = side if which == 0 else 1 - side
-            pos_k = positions((keys, lanes), 0, low, key_side)
-            allowed = (seg_k == seg_q) & (pos_k <= pos_q)
-            allowed = jnp.concatenate([allowed, allowed], axis=1)
-            t = jnp.tanh(dot(k, q, 1, 1) * (SCALE / CAP))
-            e = jnp.where(allowed, jnp.exp2(t * (CAP * LOG2E)), 0.0)
-            dp = dot(v, do, 1, 1)
-            total += jnp.sum(e, axis=0, keepdims=True)
-            weighted += jnp.sum(e.astype(BF16).astype(F32) * dp, axis=0, keepdims=True)
-            parts.append((k, t, e, dp))
+        for which, ref in enumerate((own_ref, other_ref)):
+            for start, stop in ((low, z), (z, high)):
+                if start == stop:
+                    continue
+                k = gathered(ref, start, stop, 0)
+                v = gathered(ref, start, stop, HEAD)
+                allowed = ids(ref, start, stop) == seg_q
+                if start == z:
+                    key_side = side if which == 0 else 1 - side
+                    pos_k = positions((lanes, lanes), 0, z, key_side)
+                    allowed &= pos_k <= pos_q
+                allowed = jnp.concatenate([allowed, allowed], axis=1)
+                t = jnp.tanh(dot(k, q, 1, 1) * (SCALE / CAP))
+                e = jnp.where(allowed, jnp.exp2(t * (CAP * LOG2E)), 0.0)
+                dp = dot(v, do, 1, 1)
+                total += jnp.sum(e, axis=0, keepdims=True)
+                weighted += jnp.sum(e * dp, axis=0, keepdims=True)
+                parts.append((which, start, stop, k, t, e, dp))
         inverse = 1.0 / total
         delta = weighted * inverse
-        scaled = inverse * SCALE
         dq = 0.0
-        for which, (k, t, e, dp) in enumerate(parts):
-            prob = (e * inverse).astype(BF16)
-            ds = ((e * scaled) * (dp - delta) * (1.0 - t * t)).astype(BF16)
-            acc[which, low * block : high * block, :HEAD] += dot(ds, q, 1, 0)
-            acc[which, low * block : high * block, HEAD:] += dot(prob, do, 1, 0)
+        for which, start, stop, k, t, e, dp in parts:
+            prob = e * inverse
+            ds = (prob * (dp - delta) * (1.0 - t * t)).astype(BF16)
+            at = slice(start * block, stop * block)
+            dk, dv = dot(ds, q, 1, 0), dot(prob.astype(BF16), do, 1, 0)
+            if z == start:
+                acc[which, at, :HEAD] = dk
+                acc[which, at, HEAD:] = dv
+            else:
+                acc[which, at, :HEAD] += dk
+                acc[which, at, HEAD:] += dv
             dq += dot(ds, k, 0, 0)
+        dq *= SCALE
         dq = dq.astype(BF16)
-        dq_ref[z:high, :, :HEAD] = dq[:lanes].reshape(per, block, HEAD)
-        dq_ref[z:high, :, HEAD:] = dq[lanes:].reshape(per, block, HEAD)
-    dkv_own[...] = acc[0].reshape(dkv_own.shape)
-    dkv_other[...] = acc[1].astype(BF16).reshape(dkv_other.shape)
-
-
-def attention(side, own, other, do):
-    steps, block, width = do.shape
-    width -= HEAD
+        for i in range(per):
+            at = slice(i * block, (i + 1) * block)
+            dq_ref[SLOT[z + i], :, :HEAD] = dq[:lanes][at]
+            dq_ref[SLOT[z + i], :, HEAD:] = dq[lanes:][at]
+    for z in range(steps):
+        at = slice(z * block, (z + 1) * block)
+        for which, out_ref in enumerate((dkv_own, dkv_other)):
+            out_ref[SLOT[z], :, :HEAD] = (acc[which, at, :HEAD] * SCALE).astype(BF16)
+            out_ref[SLOT[z], :, HEAD:] = acc[which, at, HEAD:].astype(BF16)
+
+
+def attention(side, own, other, q_and_grad):
+    steps, block, width = q_and_grad.shape
+    width //= 2
     return pl.pallas_call(
         attention_kernel,
-        in_specs=[SMEM, VMEM, VMEM, VMEM],
+        in_specs=[SMEM] + [VMEM] * 3,
         out_specs=[VMEM] * 3,
         out_shape=[
-            jax.ShapeDtypeStruct((steps, block, width), BF16),
-            jax.ShapeDtypeStruct((steps, block, width), F32),
-            jax.ShapeDtypeStruct((steps, block, width), BF16),
+            pltpu.HBM((steps, block, width), BF16),
+            pltpu.VMEM((steps, block, width), BF16),
+            pltpu.VMEM((steps, block, width), BF16),
         ],
         scratch_shapes=[pltpu.VMEM((2, steps * block, width), F32)],
         compiler_params=pltpu.CompilerParams(vmem_limit_bytes=LARGE_VMEM),
@@ -253,7 +264,7 @@
             flops=3 * 10**9, bytes_accessed=6 * 2**20, transcendentals=1200000
         ),
         name="attend",
-    )(side, own, other, do)
+    )(side, own, other, q_and_grad)
 
 
 def run_copies(copies):
@@ -386,14 +397,14 @@
     tp = lax.axis_index("tp")
     group = lax.axis_index("dp")
     side = ctx % pair
-    columns = [[z * pair + h for z in range(units)] for h in range(pair)]
+    columns = [[z * pair + h for z in ORDER] for h in range(pair)]
     swap = [(z * pair + h, z * pair + 1 - h) for z in range(units) for h in range(pair)]
 
     other_grad = lax.ppermute(output_grad, "tp", [(0, 1), (1, 0)])
 
-    own = pack(segment_ids, queries, key_states, value_state_rows)
+    own = pack(segment_ids, key_states, value_state_rows)
     own = exchange(own, "ctx", columns)
-    other = lax.ppermute(own[:, :, block // TILE * HEAD :], "ctx", swap)
+    other = lax.ppermute(own, "ctx", swap)
 
     def partner(g, i, sign):
         chips = groups // 2
@@ -431,16 +442,17 @@
 
     index = tp[None].astype(jnp.int32)
     part, turned = project_own(output_grad, out_weight, index)
-    do = project_other(other_grad, turned, part, queries, kv_heads)
-    do = exchange(do.reshape(units, block, do.shape[3]), "ctx", columns)
+    q_and_grad = project_other(other_grad, turned, part, queries, kv_heads)
+    q_and_grad = q_and_grad.reshape(units, block, q_and_grad.shape[3])
+    q_and_grad = exchange(q_and_grad, "ctx", columns)
 
     dq, dkv_mine, dkv_theirs = attention(
-        side[None].astype(jnp.int32), own, other, do
-    )
-
+        side[None].astype(jnp.int32), own, other, q_and_grad
+    )
+
+    dkv_back = lax.ppermute(dkv_theirs, "ctx", swap)
     dq = exchange(dq, "ctx", columns)
-    dkv_back = lax.ppermute(dkv_theirs, "ctx", swap)
-    dkv = (dkv_mine + dkv_back.astype(F32)).astype(BF16)
+    dkv = (dkv_mine.astype(F32) + dkv_back.astype(F32)).astype(BF16)
     dkv, dq = lax.optimization_barrier((dkv, dq))
     dkv = exchange(dkv, "ctx", columns)
 

time: 139 us -> 132 us (0.950)
  waiting for transfers between devices: 73.3 us -> 61.4 us
  starting transfers between devices: 42.1 us -> 49 us
    all_to_all x5, waiting for transfers between devices: 37.8 us -> 28.7 us  [exchange(): lax.all_to_all(x, axis, split_axis=0, concat_axis=0, tiled=True, axis_ind...]
    all_to_all x5, starting transfers between devices: 23.9 us -> 29 us  [exchange(): lax.all_to_all(x, axis, split_axis=0, concat_axis=0, tiled=True, axis_ind...]
    ppermute x1, waiting for transfers between devices: 12.3 us -> 10.4 us  [on_device(): dkv_back = lax.ppermute(dkv_theirs, 'ctx', swap)]
    ppermute x1, waiting for transfers between devices: 12.8 us -> 11.1 us  [on_device(): other = lax.ppermute(own, 'ctx', swap)]
    unnamed x10 -> x8, local copies, waits for them, and re-layouts: 5.07 us -> 4.27 us
  transfers between devices with their start and end apart: 15 -> 15, of which waited for: 11 -> 10; matrix products, arithmetic and copies ran while one was open for 1% -> 1% of each run, Pallas kernels for 6% -> 6%
where the time goes in v3:
time: 132 us
  waiting for transfers between devices  61.4 us (47%)
  starting transfers between devices  49 us (37%)
  Pallas kernels  14.7 us (11%)
  local copies, waits for them, and re-layouts  4.34 us (3%)
  other arithmetic  1.44 us (1%)
    all_to_all x5, starting transfers between devices, exchange(): lax.all_to_all(x, axis, split_axis=0, concat_axis=0, tiled=True, axis_ind...  29 us
    all_to_all x5, waiting for transfers between devices, exchange(): lax.all_to_all(x, axis, split_axis=0, concat_axis=0, tiled=True, axis_ind...  28.7 us
    ppermute x7, starting transfers between devices, on_device(): got.append(lax.ppermute(sent[i], 'dp', route))  12.4 us
    ppermute x1, waiting for transfers between devices, on_device(): other = lax.ppermute(own, 'ctx', swap)  11.1 us
    ppermute x1, waiting for transfers between devices, on_device(): dkv_back = lax.ppermute(dkv_theirs, 'ctx', swap)  10.4 us
    ppermute x7, waiting for transfers between devices, on_device(): got.append(lax.ppermute(sent[i], 'dp', route))  8.04 us
    unnamed x8, local copies, waits for them, and re-layouts  4.27 us
    pallas_call x1, Pallas kernels, attention(): pl.pallas_call(attention_kernel, in_specs=[SMEM] + [VMEM] * 3, out_specs=...  4.24 us
  transfers between devices with their start and end apart: 15, of which 10 were waited for; matrix products, arithmetic and copies ran while one was open for 1% of the time, Pallas kernels for 6%

profile of v3, /device:TPU:1, one launch (start us, length us, event | category | flops | bytes accessed | tf_op | source)
XLA Modules:
  0.0 131.6 jit_solution(13756822011281666905)
XLA Ops:
  0.6 0.0 copy-start.2
  0.6 2.1 %collective-permute-start.1 = (bf16[4,64,1792]{2,1,0:T(8,128)(2,1)}, bf16[4,64,1792]{2,1,0:T(8,128)(2,1)S(1)}, u32[]{:S(2)}, u32[]{:S(2)}) collective-permute-start(bf16[4,64,1792]{2,1,0:T(8,128)(2,1)} %x_ref.1), channel_id=1, source_target_pairs={{0,1},{1,0},{2,3},{3,2},{4,5},{5,4},{6,7},{7,6},{8,9},{9,8},{10,11... | collective-permute-start | bytes 2752520 | tf_op jit(solution)/shard_map/ppermute | solution.py:403
  2.8 1.9 %pack.1 = bf16[8,16,2176]{2,1,0:T(8,128)(2,1)} custom-call(s32[4,64]{1,0:T(4,128)} %seg_hbm.1, bf16[4,64,512]{2,1,0:T(8,128)(2,1)} %k_hbm.1, bf16[4,64,512]{2,1,0:T(8,128)(2,1)} %v_hbm.1), custom_call_target="tpu_custom_call" | custom-call | tf_op jit(solution)/shard_map/pack/pallas_call | solution.py:73
  4.7 8.2 %all-to-all-start = ((bf16[8,16,2176]{2,1,0:T(8,128)(2,1)}), bf16[8,16,2176]{2,1,0:T(8,128)(2,1)S(1)}, u32[]{:S(2)}, u32[]{:S(2)}) async-start(bf16[8,16,2176]{2,1,0:T(8,128)(2,1)} %pack.1), calls=%async_computation | async-start | bytes 1114112 | tf_op jit(solution)/shard_map/all_to_all | solution.py:382
  12.9 0.0 copy-start
  12.9 3.1 %copy-done = bf16[1024,3584]{1,0:T(8,128)(2,1)S(1)} copy-done((bf16[1024,3584]{1,0:T(8,128)(2,1)S(1)}, bf16[1024,3584]{1,0:T(8,128)(2,1)}, u32[]{:S(2)}) %copy-start) | copy-done | bytes 7340056
  16.0 0.0 copy-start.1
  16.0 1.2 copy-done.1
  17.2 1.3 %project_own.1 = (f32[256,1024]{1,0:T(8,128)S(1)}, bf16[1792,1024]{1,0:T(8,128)(2,1)S(1)}) custom-call(s32[1]{0:T(128)} %bitcast.1.index_ref, bf16[4,64,1792]{2,1,0:T(8,128)(2,1)S(1)} %copy-done.1, bf16[1024,3584]{1,0:T(8,128)(2,1)S(1)} %copy-done), custom_call_target="tpu_custom_call" | custom-call | flops 939524096 | bytes 7340032 | tf_op jit(solution)/shard_map/project_own/pallas_call | solution.py:103
  18.5 3.3 %collective-permute-done.1.x_ref = bf16[4,64,1792]{2,1,0:T(8,128)(2,1)S(1)} collective-permute-done((bf16[4,64,1792]{2,1,0:T(8,128)(2,1)}, bf16[4,64,1792]{2,1,0:T(8,128)(2,1)S(1)}, u32[]{:S(2)}, u32[]{:S(2)}) %collective-permute-start.1) | collective-permute-done | bytes 917536 | tf_op jit(solution)/shard_map/ppermute | solution.py:403
  21.8 0.0 copy-done.2
  21.8 2.1 %project_other.1 = bf16[4,2,64,1024]{3,2,1,0:T(8,128)(2,1)} custom-call(bf16[4,64,1792]{2,1,0:T(8,128)(2,1)S(1)} %collective-permute-done.1.x_ref, bf16[1792,1024]{1,0:T(8,128)(2,1)S(1)} %get-tuple-element.29.turned_ref, f32[256,1024]{1,0:T(8,128)S(1)} %get-tuple-element.30.part_ref, bf16[4,64,1024]{2,1,0:T(8,128)(2,1)S(1)} %copy-done.2), custom_call_target="tpu_custom_call" | custom-call | flops 939524096 | bytes 3670016 | tf_op jit(solution)/shard_map/project_other/pallas_call | solution.py:136
  23.9 3.6 %all-to-all-done.own_ref = bf16[8,16,2176]{2,1,0:T(8,128)(2,1)S(1)} async-done(((bf16[8,16,2176]{2,1,0:T(8,128)(2,1)}), bf16[8,16,2176]{2,1,0:T(8,128)(2,1)S(1)}, u32[]{:S(2)}, u32[]{:S(2)}) %all-to-all-start) | async-done | bytes 557088 | tf_op jit(solution)/shard_map/all_to_all | solution.py:382
  27.6 5.7 %all-to-all-start.1 = ((bf16[8,64,1024]{2,1,0:T(8,128)(2,1)}), bf16[8,64,1024]{2,1,0:T(8,128)(2,1)S(1)}, u32[]{:S(2)}, u32[]{:S(2)}) async-start(bf16[8,64,1024]{2,1,0:T(8,128)(2,1)} %bitcast.2), calls=%async_computation.1 | async-start | bytes 2097152 | tf_op jit(solution)/shard_map/all_to_all | solution.py:382
  33.3 2.7 %collective-permute-start = (bf16[8,16,2176]{2,1,0:T(8,128)(2,1)S(1)}, bf16[8,16,2176]{2,1,0:T(8,128)(2,1)S(1)}, u32[]{:S(2)}, u32[]{:S(2)}) collective-permute-start(bf16[8,16,2176]{2,1,0:T(8,128)(2,1)S(1)} %all-to-all-done.own_ref), channel_id=1, source_target_pairs={{0,2},{2,0},{4,6},{6,4},{8,10},{10,8},{12,14},{14,12},{16,18},{18,... | collective-permute-start | bytes 1671176 | tf_op jit(solution)/shard_map/ppermute | solution.py:407
  36.0 11.1 %collective-permute-done.other_ref = bf16[8,16,2176]{2,1,0:T(8,128)(2,1)S(1)} collective-permute-done((bf16[8,16,2176]{2,1,0:T(8,128)(2,1)S(1)}, bf16[8,16,2176]{2,1,0:T(8,128)(2,1)S(1)}, u32[]{:S(2)}, u32[]{:S(2)}) %collective-permute-start) | collective-permute-done | bytes 557088 | tf_op jit(solution)/shard_map/ppermute | solution.py:407
  47.1 11.7 %all-to-all-done.1.qd_ref = bf16[8,64,1024]{2,1,0:T(8,128)(2,1)S(1)} async-done(((bf16[8,64,1024]{2,1,0:T(8,128)(2,1)}), bf16[8,64,1024]{2,1,0:T(8,128)(2,1)S(1)}, u32[]{:S(2)}, u32[]{:S(2)}) %all-to-all-start.1) | async-done | bytes 1048608 | tf_op jit(solution)/shard_map/all_to_all | solution.py:382
  58.8 0.0 copy-start.3
  58.8 4.2 %attend.1 = (bf16[8,64,512]{2,1,0:T(8,128)(2,1)}, bf16[8,64,512]{2,1,0:T(8,128)(2,1)S(1)}, bf16[8,64,512]{2,1,0:T(8,128)(2,1)S(1)}) custom-call(s32[1]{0:T(128)} %bitcast.side_ref, bf16[8,16,2176]{2,1,0:T(8,128)(2,1)S(1)} %all-to-all-done.own_ref, bf16[8,16,2176]{2,1,0:T(8,128)(2,1)S(1)} %collective-permute-done.other_ref, ...), custom_call_target="tpu_custom_call" | custom-call | flops 3000000000 | bytes 6291456 | tf_op jit(solution)/shard_map/attend/pallas_call | solution.py:252
  63.1 4.2 %all-to-all-start.2 = ((bf16[8,64,512]{2,1,0:T(8,128)(2,1)}), bf16[8,64,512]{2,1,0:T(8,128)(2,1)S(1)}, u32[]{:S(2)}, u32[]{:S(2)}) async-start(bf16[8,64,512]{2,1,0:T(8,128)(2,1)} %get-tuple-element.33), calls=%async_computation.2 | async-start | bytes 1048576 | tf_op jit(solution)/shard_map/all_to_all | solution.py:382
  67.2 2.7 %collective-permute-start.2 = (bf16[8,64,512]{2,1,0:T(8,128)(2,1)S(1)}, bf16[8,64,512]{2,1,0:T(8,128)(2,1)S(1)}, u32[]{:S(2)}, u32[]{:S(2)}) collective-permute-start(bf16[8,64,512]{2,1,0:T(8,128)(2,1)S(1)} %get-tuple-element.32), channel_id=1, source_target_pairs={{0,2},{2,0},{4,6},{6,4},{8,10},{10,8},{12,14},{14,12},{16,18},{18,... | collective-permute-start | bytes 1572872 | tf_op jit(solution)/shard_map/ppermute | solution.py:453
  70.0 10.4 %collective-permute-done.2 = bf16[8,64,512]{2,1,0:T(8,128)(2,1)S(1)} collective-permute-done((bf16[8,64,512]{2,1,0:T(8,128)(2,1)S(1)}, bf16[8,64,512]{2,1,0:T(8,128)(2,1)S(1)}, u32[]{:S(2)}, u32[]{:S(2)}) %collective-permute-start.2) | collective-permute-done | bytes 524320 | tf_op jit(solution)/shard_map/ppermute | solution.py:453
  80.3 0.9 add_convert_fusion
  81.3 0.0 all-to-all-done.2
  81.3 6.4 %all-to-all-start.3 = ((bf16[8,64,512]{2,1,0:T(8,128)(2,1)}), bf16[8,64,512]{2,1,0:T(8,128)(2,1)S(1)}, u32[]{:S(2)}, u32[]{:S(2)}) async-start(bf16[8,64,512]{2,1,0:T(8,128)(2,1)} %add_convert_fusion), calls=%async_computation.3 | async-start | bytes 1048576 | tf_op jit(solution)/shard_map/all_to_all | solution.py:382
  87.6 0.0 copy-done.3
  87.6 0.1 reshape.145
  87.8 0.1 select_reduce_fusion
  87.8 0.6 pick.1
  88.5 3.4 %collective-permute-start.3 = (bf16[2,64,512]{2,1,0:T(8,128)(2,1)S(1)}, bf16[2,64,512]{2,1,0:T(8,128)(2,1)S(1)}, u32[]{:S(2)}, u32[]{:S(2)}) collective-permute-start(bf16[2,64,512]{2,1,0:T(8,128)(2,1)S(1)} %get-tuple-element.37), channel_id=1, source_target_pairs={{0,32},{32,0},{64,96},{96,64},{128,160},{160,128},{192,224},{224,1... | collective-permute-start | bytes 393224 | tf_op jit(solution)/shard_map/ppermute | solution.py:466
  91.9 1.3 %collective-permute-start.4 = (bf16[2,64,512]{2,1,0:T(8,128)(2,1)S(1)}, bf16[2,64,512]{2,1,0:T(8,128)(2,1)S(1)}, u32[]{:S(2)}, u32[]{:S(2)}) collective-permute-start(bf16[2,64,512]{2,1,0:T(8,128)(2,1)S(1)} %get-tuple-element.38), channel_id=1, source_target_pairs={{0,64},{32,96},{64,128},{96,160},{128,192},{160,224},{192,0},{224,... | collective-permute-start | bytes 393224 | tf_op jit(solution)/shard_map/ppermute | solution.py:466
  93.2 1.5 %collective-permute-start.5 = (bf16[2,64,512]{2,1,0:T(8,128)(2,1)S(1)}, bf16[2,64,512]{2,1,0:T(8,128)(2,1)S(1)}, u32[]{:S(2)}, u32[]{:S(2)}) collective-permute-start(bf16[2,64,512]{2,1,0:T(8,128)(2,1)S(1)} %get-tuple-element.39), channel_id=1, source_target_pairs={{0,96},{32,64},{64,160},{96,128},{128,224},{160,192},{192,32},{224... | collective-permute-start | bytes 393224 | tf_op jit(solution)/shard_map/ppermute | solution.py:466
  94.7 1.3 collective-permute-start.6
  96.0 2.0 %collective-permute-start.7 = (bf16[2,64,512]{2,1,0:T(8,128)(2,1)S(1)}, bf16[2,64,512]{2,1,0:T(8,128)(2,1)S(1)}, u32[]{:S(2)}, u32[]{:S(2)}) collective-permute-start(bf16[2,64,512]{2,1,0:T(8,128)(2,1)S(1)} %get-tuple-element.41), channel_id=1, source_target_pairs={{0,160},{32,128},{64,224},{96,192},{128,32},{160,0},{192,96},{224,... | collective-permute-start | bytes 393224 | tf_op jit(solution)/shard_map/ppermute | solution.py:466
  98.0 0.0 collective-permute-done.3.refs_1_
  98.0 1.4 %collective-permute-start.8 = (bf16[2,64,512]{2,1,0:T(8,128)(2,1)S(1)}, bf16[2,64,512]{2,1,0:T(8,128)(2,1)S(1)}, u32[]{:S(2)}, u32[]{:S(2)}) collective-permute-start(bf16[2,64,512]{2,1,0:T(8,128)(2,1)S(1)} %get-tuple-element.42), channel_id=1, source_target_pairs={{0,192},{32,224},{64,0},{96,32},{128,64},{160,96},{192,128},{224,1... | collective-permute-start | bytes 393224 | tf_op jit(solution)/shard_map/ppermute | solution.py:466
  99.4 0.0 collective-permute-done.4.refs_2_
  99.4 1.5 %collective-permute-start.9 = (bf16[2,64,512]{2,1,0:T(8,128)(2,1)S(1)}, bf16[2,64,512]{2,1,0:T(8,128)(2,1)S(1)}, u32[]{:S(2)}, u32[]{:S(2)}) collective-permute-start(bf16[2,64,512]{2,1,0:T(8,128)(2,1)S(1)} %get-tuple-element.43), channel_id=1, source_target_pairs={{0,224},{32,192},{64,32},{96,0},{128,96},{160,64},{192,160},{224,1... | collective-permute-start | bytes 393224 | tf_op jit(solution)/shard_map/ppermute | solution.py:466
  100.9 0.6 collective-permute-done.5.refs_3_
  101.5 3.5 %collective-permute-done.6.refs_4_ = bf16[2,64,512]{2,1,0:T(8,128)(2,1)S(1)} collective-permute-done((bf16[2,64,512]{2,1,0:T(8,128)(2,1)S(1)}, bf16[2,64,512]{2,1,0:T(8,128)(2,1)S(1)}, u32[]{:S(2)}, u32[]{:S(2)}) %collective-permute-start.6) | collective-permute-done | bytes 131104 | tf_op jit(solution)/shard_map/ppermute | solution.py:466
  105.0 3.0 %collective-permute-done.7.refs_5_ = bf16[2,64,512]{2,1,0:T(8,128)(2,1)S(1)} collective-permute-done((bf16[2,64,512]{2,1,0:T(8,128)(2,1)S(1)}, bf16[2,64,512]{2,1,0:T(8,128)(2,1)S(1)}, u32[]{:S(2)}, u32[]{:S(2)}) %collective-permute-start.7) | collective-permute-done | bytes 131104 | tf_op jit(solution)/shard_map/ppermute | solution.py:466
  108.0 0.0 collective-permute-done.8.refs_6_
  108.0 0.9 collective-permute-done.9.refs_7_
  108.9 0.0 all-to-all-done.3
  108.9 1.6 %pick_stacked.1 = bf16[8,2,64,512]{3,2,1,0:T(8,128)(2,1)} custom-call(s32[8]{0:T(128)S(1)} %get-tuple-element.55.index_ref, bf16[4,2,64,512]{3,2,1,0:T(8,128)(2,1)S(1)} %bitcast.7), custom_call_target="tpu_custom_call" | custom-call | tf_op jit(solution)/shard_map/pick_stacked/pallas_call | solution.py:305
  110.5 4.6 %all-to-all-start.4 = ((bf16[8,2,64,512]{3,2,1,0:T(8,128)(2,1)}), bf16[8,2,64,512]{3,2,1,0:T(8,128)(2,1)S(1)}, u32[]{:S(2)}, u32[]{:S(2)}) async-start(bf16[8,2,64,512]{3,2,1,0:T(8,128)(2,1)} %pick_stacked.1), calls=%async_computation.4 | async-start | bytes 2097152 | tf_op jit(solution)/shard_map/all_to_all | solution.py:382
  115.1 0.2 select_reduce_fusion.3.index_ref
  115.3 0.2 select_reduce_fusion.2.index_ref
  115.5 1.4 %place_q.1 = bf16[4,64,1024]{2,1,0:T(8,128)(2,1)} custom-call(s32[4]{0:T(128)S(1)} %select_reduce_fusion.2.index_ref, bf16[2,64,512]{2,1,0:T(8,128)(2,1)S(1)} %get-tuple-element.44.refs_0_, bf16[2,64,512]{2,1,0:T(8,128)(2,1)S(1)} %collective-permute-done.3.refs_1_, bf16[2,64,512]{2,1,0:T(8,128)(2,1)S(1)} %collective-permute-done.4.refs_2_, ...), custom_call_target="tpu_custom_call" | custom-call | tf_op jit(solution)/shard_map/place_q/pallas_call | solution.py:341
  116.9 13.3 %all-to-all-done.4.in_ref = bf16[8,2,64,512]{3,2,1,0:T(8,128)(2,1)S(1)} async-done(((bf16[8,2,64,512]{3,2,1,0:T(8,128)(2,1)}), bf16[8,2,64,512]{3,2,1,0:T(8,128)(2,1)S(1)}, u32[]{:S(2)}, u32[]{:S(2)}) %all-to-all-start.4) | async-done | bytes 1048608 | tf_op jit(solution)/shard_map/all_to_all | solution.py:382
  130.2 1.5 %place_kv.1 = (bf16[4,64,512]{2,1,0:T(8,128)(2,1)}, bf16[4,64,512]{2,1,0:T(8,128)(2,1)}) custom-call(s32[4]{0:T(128)S(1)} %select_reduce_fusion.3.index_ref, bf16[8,2,64,512]{3,2,1,0:T(8,128)(2,1)S(1)} %all-to-all-done.4.in_ref), custom_call_target="tpu_custom_call" | custom-call | tf_op jit(solution)/shard_map/place_kv/pallas_call | solution.py:370
  (5 shorter events, 0.1 us)
Async XLA Ops:
  0.6 21.2 %copy-start.2 = (bf16[4,64,1024]{2,1,0:T(8,128)(2,1)S(1)}, bf16[4,64,1024]{2,1,0:T(8,128)(2,1)}, u32[]{:S(2)}) copy-start(bf16[4,64,1024]{2,1,0:T(8,128)(2,1)} %q_ref.1) | copy-start | bytes 1572868
  0.6 21.2 %collective-permute-start.1 = (bf16[4,64,1792]{2,1,0:T(8,128)(2,1)}, bf16[4,64,1792]{2,1,0:T(8,128)(2,1)S(1)}, u32[]{:S(2)}, u32[]{:S(2)}) collective-permute-start(bf16[4,64,1792]{2,1,0:T(8,128)(2,1)} %x_ref.1), channel_id=1, source_target_pairs={{0,1},{1,0},{2,3},{3,2},{4,5},{5,4},{6,7},{7,6},{8,9},{9,8},{10,11... | collective-permute-start | bytes 2752520 | tf_op jit(solution)/shard_map/ppermute | solution.py:403
  4.7 22.8 %all-to-all-start = ((bf16[8,16,2176]{2,1,0:T(8,128)(2,1)}), bf16[8,16,2176]{2,1,0:T(8,128)(2,1)S(1)}, u32[]{:S(2)}, u32[]{:S(2)}) async-start(bf16[8,16,2176]{2,1,0:T(8,128)(2,1)} %pack.1), calls=%async_computation | async-start | bytes 1114112 | tf_op jit(solution)/shard_map/all_to_all | solution.py:382
  12.9 3.1 %copy-start = (bf16[1024,3584]{1,0:T(8,128)(2,1)S(1)}, bf16[1024,3584]{1,0:T(8,128)(2,1)}, u32[]{:S(2)}) copy-start(bf16[1024,3584]{1,0:T(8,128)(2,1)} %weight_ref.1) | copy-start | bytes 22020100
  16.0 1.2 copy-start.1
  27.6 31.3 %all-to-all-start.1 = ((bf16[8,64,1024]{2,1,0:T(8,128)(2,1)}), bf16[8,64,1024]{2,1,0:T(8,128)(2,1)S(1)}, u32[]{:S(2)}, u32[]{:S(2)}) async-start(bf16[8,64,1024]{2,1,0:T(8,128)(2,1)} %bitcast.2), calls=%async_computation.1 | async-start | bytes 2097152 | tf_op jit(solution)/shard_map/all_to_all | solution.py:382
  33.3 13.8 %collective-permute-start = (bf16[8,16,2176]{2,1,0:T(8,128)(2,1)S(1)}, bf16[8,16,2176]{2,1,0:T(8,128)(2,1)S(1)}, u32[]{:S(2)}, u32[]{:S(2)}) collective-permute-start(bf16[8,16,2176]{2,1,0:T(8,128)(2,1)S(1)} %all-to-all-done.own_ref), channel_id=1, source_target_pairs={{0,2},{2,0},{4,6},{6,4},{8,10},{10,8},{12,14},{14,12},{16,18},{18,... | collective-permute-start | bytes 1671176 | tf_op jit(solution)/shard_map/ppermute | solution.py:407
  58.8 28.8 %copy-start.3 = (s32[32]{0:T(128)S(1)}, s32[32]{0:T(128)}, u32[]{:S(2)}) copy-start(s32[32]{0:T(128)} %param.13) | copy-start | bytes 388
  63.1 18.2 %all-to-all-start.2 = ((bf16[8,64,512]{2,1,0:T(8,128)(2,1)}), bf16[8,64,512]{2,1,0:T(8,128)(2,1)S(1)}, u32[]{:S(2)}, u32[]{:S(2)}) async-start(bf16[8,64,512]{2,1,0:T(8,128)(2,1)} %get-tuple-element.33), calls=%async_computation.2 | async-start | bytes 1048576 | tf_op jit(solution)/shard_map/all_to_all | solution.py:382
  67.2 13.1 %collective-permute-start.2 = (bf16[8,64,512]{2,1,0:T(8,128)(2,1)S(1)}, bf16[8,64,512]{2,1,0:T(8,128)(2,1)S(1)}, u32[]{:S(2)}, u32[]{:S(2)}) collective-permute-start(bf16[8,64,512]{2,1,0:T(8,128)(2,1)S(1)} %get-tuple-element.32), channel_id=1, source_target_pairs={{0,2},{2,0},{4,6},{6,4},{8,10},{10,8},{12,14},{14,12},{16,18},{18,... | collective-permute-start | bytes 1572872 | tf_op jit(solution)/shard_map/ppermute | solution.py:453
  81.3 27.6 %all-to-all-start.3 = ((bf16[8,64,512]{2,1,0:T(8,128)(2,1)}), bf16[8,64,512]{2,1,0:T(8,128)(2,1)S(1)}, u32[]{:S(2)}, u32[]{:S(2)}) async-start(bf16[8,64,512]{2,1,0:T(8,128)(2,1)} %add_convert_fusion), calls=%async_computation.3 | async-start | bytes 1048576 | tf_op jit(solution)/shard_map/all_to_all | solution.py:382
  88.5 9.5 %collective-permute-start.3 = (bf16[2,64,512]{2,1,0:T(8,128)(2,1)S(1)}, bf16[2,64,512]{2,1,0:T(8,128)(2,1)S(1)}, u32[]{:S(2)}, u32[]{:S(2)}) collective-permute-start(bf16[2,64,512]{2,1,0:T(8,128)(2,1)S(1)} %get-tuple-element.37), channel_id=1, source_target_pairs={{0,32},{32,0},{64,96},{96,64},{128,160},{160,128},{192,224},{224,1... | collective-permute-start | bytes 393224 | tf_op jit(solution)/shard_map/ppermute | solution.py:466
  91.9 7.6 %collective-permute-start.4 = (bf16[2,64,512]{2,1,0:T(8,128)(2,1)S(1)}, bf16[2,64,512]{2,1,0:T(8,128)(2,1)S(1)}, u32[]{:S(2)}, u32[]{:S(2)}) collective-permute-start(bf16[2,64,512]{2,1,0:T(8,128)(2,1)S(1)} %get-tuple-element.38), channel_id=1, source_target_pairs={{0,64},{32,96},{64,128},{96,160},{128,192},{160,224},{192,0},{224,... | collective-permute-start | bytes 393224 | tf_op jit(solution)/shard_map/ppermute | solution.py:466
  93.2 8.3 %collective-permute-start.5 = (bf16[2,64,512]{2,1,0:T(8,128)(2,1)S(1)}, bf16[2,64,512]{2,1,0:T(8,128)(2,1)S(1)}, u32[]{:S(2)}, u32[]{:S(2)}) collective-permute-start(bf16[2,64,512]{2,1,0:T(8,128)(2,1)S(1)} %get-tuple-element.39), channel_id=1, source_target_pairs={{0,96},{32,64},{64,160},{96,128},{128,224},{160,192},{192,32},{224... | collective-permute-start | bytes 393224 | tf_op jit(solution)/shard_map/ppermute | solution.py:466
  94.7 10.3 %collective-permute-start.6 = (bf16[2,64,512]{2,1,0:T(8,128)(2,1)S(1)}, bf16[2,64,512]{2,1,0:T(8,128)(2,1)S(1)}, u32[]{:S(2)}, u32[]{:S(2)}) collective-permute-start(bf16[2,64,512]{2,1,0:T(8,128)(2,1)S(1)} %get-tuple-element.40), channel_id=1, source_target_pairs={{0,128},{32,160},{64,192},{96,224},{128,0},{160,32},{192,64},{224,... | collective-permute-start | bytes 393224 | tf_op jit(solution)/shard_map/ppermute | solution.py:466
  96.0 12.0 %collective-permute-start.7 = (bf16[2,64,512]{2,1,0:T(8,128)(2,1)S(1)}, bf16[2,64,512]{2,1,0:T(8,128)(2,1)S(1)}, u32[]{:S(2)}, u32[]{:S(2)}) collective-permute-start(bf16[2,64,512]{2,1,0:T(8,128)(2,1)S(1)} %get-tuple-element.41), channel_id=1, source_target_pairs={{0,160},{32,128},{64,224},{96,192},{128,32},{160,0},{192,96},{224,... | collective-permute-start | bytes 393224 | tf_op jit(solution)/shard_map/ppermute | solution.py:466
  98.0 10.0 %collective-permute-start.8 = (bf16[2,64,512]{2,1,0:T(8,128)(2,1)S(1)}, bf16[2,64,512]{2,1,0:T(8,128)(2,1)S(1)}, u32[]{:S(2)}, u32[]{:S(2)}) collective-permute-start(bf16[2,64,512]{2,1,0:T(8,128)(2,1)S(1)} %get-tuple-element.42), channel_id=1, source_target_pairs={{0,192},{32,224},{64,0},{96,32},{128,64},{160,96},{192,128},{224,1... | collective-permute-start | bytes 393224 | tf_op jit(solution)/shard_map/ppermute | solution.py:466
  99.4 9.5 %collective-permute-start.9 = (bf16[2,64,512]{2,1,0:T(8,128)(2,1)S(1)}, bf16[2,64,512]{2,1,0:T(8,128)(2,1)S(1)}, u32[]{:S(2)}, u32[]{:S(2)}) collective-permute-start(bf16[2,64,512]{2,1,0:T(8,128)(2,1)S(1)} %get-tuple-element.43), channel_id=1, source_target_pairs={{0,224},{32,192},{64,32},{96,0},{128,96},{160,64},{192,160},{224,1... | collective-permute-start | bytes 393224 | tf_op jit(solution)/shard_map/ppermute | solution.py:466
  110.5 19.7 %all-to-all-start.4 = ((bf16[8,2,64,512]{3,2,1,0:T(8,128)(2,1)}), bf16[8,2,64,512]{3,2,1,0:T(8,128)(2,1)S(1)}, u32[]{:S(2)}, u32[]{:S(2)}) async-start(bf16[8,2,64,512]{3,2,1,0:T(8,128)(2,1)} %pick_stacked.1), calls=%async_computation.4 | async-start | bytes 2097152 | tf_op jit(solution)/shard_map/all_to_all | solution.py:382

commit v4 on v3

--- a/solution.py
+++ b/solution.py
@@ -15,6 +15,7 @@
 ORDER = (0, 2, 4, 6, 1, 3, 5, 7)
 SLOT = tuple(ORDER.index(z) for z in range(len(ORDER)))
 SMALL_VMEM = 8 * 1024 * 1024
+MEDIUM_VMEM = 14 * 1024 * 1024
 LARGE_VMEM = 28 * 1024 * 1024
 
 
@@ -27,18 +28,62 @@
 ANY = pl.BlockSpec(memory_space=pl.ANY)
 
 
-def pack_kernel(seg_hbm, k_hbm, v_hbm, out_ref, seg_ref, k_ref, v_ref, sems):
+def load_half(index, weight_hbm, weight_ref, sems):
+    half = weight_ref.shape[1]
+    columns = pl.ds(pl.multiple_of(index * half, 128), half)
+    parts = [slice(h, h + HEAD) for h in range(0, weight_ref.shape[0], HEAD)]
+    copies = [
+        pltpu.make_async_copy(weight_hbm.at[at, columns], weight_ref.at[at], sems.at[i])
+        for i, at in enumerate(parts)
+    ]
+    for copy in copies:
+        copy.start()
+    for at, copy in zip(parts, copies):
+        copy.wait()
+        yield at
+
+
+def own_half(tp, x_ref, weight_hbm, part_ref, weight_ref, sems):
+    rows, block, half = x_ref.shape
+    for at in load_half(tp, weight_hbm, weight_ref, sems):
+        x = x_ref[...].reshape(rows * block, half)
+        part_ref[:, at] = dot(x, weight_ref[at], 1, 1)
+
+
+def begin_kernel(
+    place_ref,
+    seg_hbm,
+    k_hbm,
+    v_hbm,
+    x_hbm,
+    weight_hbm,
+    out_ref,
+    x_ref,
+    part_ref,
+    seg_ref,
+    k_ref,
+    v_ref,
+    weight_ref,
+    sems,
+    weight_sems,
+):
     rows, block, kv_width = k_ref.shape
     kv_heads = kv_width // HEAD
     pieces = block // TILE
     copies = [
         pltpu.make_async_copy(source, target, sems.at[i])
         for i, (source, target) in enumerate(
-            ((seg_hbm, seg_ref), (k_hbm, k_ref), (v_hbm, v_ref))
+            ((seg_hbm, seg_ref), (k_hbm, k_ref), (v_hbm, v_ref), (x_hbm, x_ref))
         )
     ]
     for copy in copies:
         copy.start()
+    copies[3].wait()
+
+    @pl.when(place_ref[1] == 0)
+    def _():
+        own_half(place_ref[0], x_ref, weight_hbm, part_ref, weight_ref, weight_sems)
+
     copies[0].wait()
     place = lax.broadcasted_iota(jnp.int32, (TILE, block), 1)
     row = lax.broadcasted_iota(jnp.int32, (TILE, block), 0)
@@ -66,59 +111,74 @@
                 out_ref[u, :, k_at + HEAD : k_at + 2 * HEAD] = v_ref[r, at, heads]
 
 
-def pack(seg, k, v):
+def in_hbm(*arrays):
+    return [pltpu.with_memory_space_constraint(x, pltpu.HBM) for x in arrays]
+
+
+def begin(place, seg, k, v, x, weight):
     rows, block, kv_width = k.shape
     kv_heads = kv_width // HEAD
     lanes = block // TILE * 2 * HEAD + 128
-    return pl.pallas_call(
-        pack_kernel,
-        in_specs=[ANY] * 3,
-        out_specs=VMEM,
-        out_shape=jax.ShapeDtypeStruct((rows * kv_heads, TILE, lanes), BF16),
+    width, half = weight.shape[0], x.shape[2]
+    return pl.pallas_call(
+        begin_kernel,
+        in_specs=[SMEM] + [ANY] * 5,
+        out_specs=[VMEM] * 3,
+        out_shape=[
+            pltpu.HBM((rows * kv_heads, TILE, lanes), BF16),
+            jax.ShapeDtypeStruct(x.shape, BF16),
+            jax.ShapeDtypeStruct((rows * block, width), F32),
+        ],
         scratch_shapes=[
             pltpu.VMEM(seg.shape, jnp.int32),
             pltpu.VMEM(k.shape, BF16),
             pltpu.VMEM(v.shape, BF16),
-            pltpu.SemaphoreType.DMA((3,)),
+            pltpu.VMEM((width, half), BF16),
+            pltpu.SemaphoreType.DMA((4,)),
+            pltpu.SemaphoreType.DMA((width // HEAD,)),
         ],
-        compiler_params=pltpu.CompilerParams(vmem_limit_bytes=SMALL_VMEM),
-        name="pack",
-    )(*(pltpu.with_memory_space_constraint(x, pltpu.HBM) for x in (seg, k, v)))
-
-
-def own_half_kernel(index_ref, x_ref, weight_ref, out_ref, turned_ref):
-    rows, block, half = x_ref.shape
-    x = x_ref[...].reshape(rows * block, half)
-    own = pl.multiple_of(index_ref[0] * half, 128)
-    other = pl.multiple_of((1 - index_ref[0]) * half, 128)
-    for h in range(weight_ref.shape[0] // HEAD):
-        at = slice(h * HEAD, (h + 1) * HEAD)
-        out_ref[:, at] = dot(x, weight_ref[at, pl.ds(own, half)], 1, 1)
-        turned_ref[:, at] = weight_ref[at, pl.ds(other, half)].T
-
-
-def project_own(x, weight, index):
+        compiler_params=pltpu.CompilerParams(vmem_limit_bytes=MEDIUM_VMEM),
+        name="begin",
+    )(place, *in_hbm(seg, k, v, x, weight))
+
+
+def project_own_kernel(
+    place_ref, x_ref, weight_hbm, part_ref, turned_ref, weight_ref, sems
+):
+    for at in load_half(1 - place_ref[0], weight_hbm, weight_ref, sems):
+        turned_ref[:, at] = weight_ref[at].T
+
+    @pl.when(place_ref[1] != 0)
+    def _():
+        own_half(place_ref[0], x_ref, weight_hbm, part_ref, weight_ref, sems)
+
+
+def project_own(place, x, weight):
     rows, block, half = x.shape
     width = weight.shape[0]
     return pl.pallas_call(
-        own_half_kernel,
-        in_specs=[SMEM, VMEM, VMEM],
+        project_own_kernel,
+        in_specs=[SMEM, VMEM, ANY],
         out_specs=[VMEM, VMEM],
         out_shape=[
             jax.ShapeDtypeStruct((rows * block, width), F32),
             jax.ShapeDtypeStruct((half, width), BF16),
         ],
-        compiler_params=pltpu.CompilerParams(vmem_limit_bytes=LARGE_VMEM),
+        scratch_shapes=[
+            pltpu.VMEM((width, half), BF16),
+            pltpu.SemaphoreType.DMA((width // HEAD,)),
+        ],
+        compiler_params=pltpu.CompilerParams(vmem_limit_bytes=MEDIUM_VMEM),
         cost_estimate=pl.CostEstimate(
             flops=2 * rows * block * half * width,
             bytes_accessed=4 * half * width,
             transcendentals=0,
         ),
         name="project_own",
-    )(index, x, weight)
-
-
-def other_half_kernel(x_ref, turned_ref, part_ref, q_ref, out_ref):
+    )(place, x, *in_hbm(weight))
+
+
+def other_half_kernel(place_ref, x_ref, q_ref, part_0, part_1, turned_ref, out_ref):
     rows, block, half = x_ref.shape
     kv_heads = out_ref.shape[1]
     width = turned_ref.shape[1] // kv_heads
@@ -126,28 +186,27 @@
     for h in range(kv_heads):
         at = slice(h * width, (h + 1) * width)
         out_ref[:, h, :, :width] = q_ref[:, :, at]
-        total = part_ref[:, at] + dot(x, turned_ref[:, at], 1, 0)
+        part = jnp.where(place_ref[1] == 0, part_0[:, at], part_1[:, at])
+        total = part + dot(x, turned_ref[:, at], 1, 0)
         out_ref[:, h, :, width:] = total.astype(BF16).reshape(rows, block, width)
 
 
-def project_other(x, turned, part, q, kv_heads):
+def project_other(place, x, q, part_0, part_1, turned, kv_heads):
     rows, block, half = x.shape
     total = turned.shape[1]
     return pl.pallas_call(
         other_half_kernel,
-        in_specs=[VMEM] * 4,
+        in_specs=[SMEM] + [VMEM] * 5,
         out_specs=VMEM,
-        out_shape=jax.ShapeDtypeStruct(
-            (rows, kv_heads, block, 2 * total // kv_heads), BF16
-        ),
-        compiler_params=pltpu.CompilerParams(vmem_limit_bytes=LARGE_VMEM),
+        out_shape=pltpu.HBM((rows, kv_heads, block, 2 * total // kv_heads), BF16),
+        compiler_params=pltpu.CompilerParams(vmem_limit_bytes=MEDIUM_VMEM),
         cost_estimate=pl.CostEstimate(
             flops=2 * rows * block * half * total,
             bytes_accessed=2 * half * total,
             transcendentals=0,
         ),
         name="project_other",
-    )(x, turned, part, q)
+    )(place, x, q, part_0, part_1, turned)
 
 
 def attention_kernel(
@@ -187,7 +246,7 @@
         jnp.int32, (lanes, lanes), 0
     ) == lax.broadcasted_iota(jnp.int32, (lanes, lanes), 1)
 
-    for z in range(0, steps, per):
+    def scores(z):
         low, high = max(0, z - 4), z + per
         qd = jnp.concatenate([qd_ref[SLOT[i]] for i in range(z, high)], axis=0)
         q = jnp.concatenate([qd[:, :HEAD], qd[:, HEAD:width]], axis=0)
@@ -218,6 +277,9 @@
                 total += jnp.sum(e, axis=0, keepdims=True)
                 weighted += jnp.sum(e * dp, axis=0, keepdims=True)
                 parts.append((which, start, stop, k, t, e, dp))
+        return z, q, do, parts, total, weighted
+
+    def gradients(z, q, do, parts, total, weighted):
         inverse = 1.0 / total
         delta = weighted * inverse
         dq = 0.0
@@ -233,12 +295,19 @@
                 acc[which, at, :HEAD] += dk
                 acc[which, at, HEAD:] += dv
             dq += dot(ds, k, 0, 0)
-        dq *= SCALE
-        dq = dq.astype(BF16)
+        dq = (dq * SCALE).astype(BF16)
         for i in range(per):
             at = slice(i * block, (i + 1) * block)
             dq_ref[SLOT[z + i], :, :HEAD] = dq[:lanes][at]
             dq_ref[SLOT[z + i], :, HEAD:] = dq[lanes:][at]
+
+    held = None
+    for z in range(0, steps, per):
+        ready = scores(z)
+        if held is not None:
+            gradients(*held)
+        held = ready
+    gradients(*held)
     for z in range(steps):
         at = slice(z * block, (z + 1) * block)
         for which, out_ref in enumerate((dkv_own, dkv_other)):
@@ -400,9 +469,11 @@
     columns = [[z * pair + h for z in ORDER] for h in range(pair)]
     swap = [(z * pair + h, z * pair + 1 - h) for z in range(units) for h in range(pair)]
 
-    other_grad = lax.ppermute(output_grad, "tp", [(0, 1), (1, 0)])
-
-    own = pack(segment_ids, key_states, value_state_rows)
+    place = jnp.stack([tp, group % 2]).astype(jnp.int32)
+    own, grad, part_0 = begin(
+        place, segment_ids, key_states, value_state_rows, output_grad, out_weight
+    )
+    other_grad = lax.ppermute(grad, "tp", [(0, 1), (1, 0)])
     own = exchange(own, "ctx", columns)
     other = lax.ppermute(own, "ctx", swap)
 
@@ -440,9 +511,10 @@
     send_index = row_for(steps)
     send_step = row_for(partner(group, steps, 1))
 
-    index = tp[None].astype(jnp.int32)
-    part, turned = project_own(output_grad, out_weight, index)
-    q_and_grad = project_other(other_grad, turned, part, queries, kv_heads)
+    part_1, turned = project_own(place, grad, out_weight)
+    q_and_grad = project_other(
+        place, other_grad, queries, part_0, part_1, turned, kv_heads
+    )
     q_and_grad = q_and_grad.reshape(units, block, q_and_grad.shape[3])
     q_and_grad = exchange(q_and_grad, "ctx", columns)
 

time: 132 us -> 131 us (level)
  Pallas kernels: 14.7 us -> 21.2 us
  waiting for transfers between devices: 61.4 us -> 55.2 us
  local copies, waits for them, and re-layouts: 4.34 us -> 0.08 us
  starting transfers between devices: 49 us -> 51.3 us
    pallas_call x3, Pallas kernels: 5.37 us -> 12.4 us  [the longest x1 6.73 us: project_own(): pl.pallas_call(project_own_kernel, in_specs=[SMEM, VMEM, ANY], out_specs=...]
    unnamed x8 -> x4, local copies, waits for them, and re-layouts: 4.27 us -> 0.01 us
    ppermute x1, waiting for transfers between devices: 11.1 us -> 7.14 us  [on_device(): other = lax.ppermute(own, 'ctx', swap)]
    ppermute x1, waiting for transfers between devices: 3.31 us -> 0.01 us  [on_device(): other_grad = lax.ppermute(grad, 'tp', [(0, 1), (1, 0)])]
    all_to_all x5, waiting for transfers between devices: 28.7 us -> 30.3 us  [exchange(): lax.all_to_all(x, axis, split_axis=0, concat_axis=0, tiled=True, axis_ind...]
    all_to_all x5, starting transfers between devices: 29 us -> 30.5 us  [exchange(): lax.all_to_all(x, axis, split_axis=0, concat_axis=0, tiled=True, axis_ind...]
  transfers between devices with their start and end apart: 15 -> 15, of which waited for: 10 -> 10; matrix products, arithmetic and copies ran while one was open for 1% -> 1% of each run, Pallas kernels for 6% -> 9%
where the time goes in v4:
time: 131 us; the launch traced here: 130 us
  waiting for transfers between devices  55.2 us (42%)
  starting transfers between devices  51.3 us (39%)
  Pallas kernels  21.2 us (16%)
  other arithmetic  1.52 us (1%)
    all_to_all x5, starting transfers between devices, exchange(): lax.all_to_all(x, axis, split_axis=0, concat_axis=0, tiled=True, axis_ind...  30.5 us
    all_to_all x5, waiting for transfers between devices, exchange(): lax.all_to_all(x, axis, split_axis=0, concat_axis=0, tiled=True, axis_ind...  30.3 us
    ppermute x7, starting transfers between devices, on_device(): got.append(lax.ppermute(sent[i], 'dp', route))  13.1 us
    ppermute x1, waiting for transfers between devices, on_device(): dkv_back = lax.ppermute(dkv_theirs, 'ctx', swap)  9.74 us
    ppermute x7, waiting for transfers between devices, on_device(): got.append(lax.ppermute(sent[i], 'dp', route))  8.03 us
    ppermute x1, waiting for transfers between devices, on_device(): other = lax.ppermute(own, 'ctx', swap)  7.14 us
    pallas_call x1, Pallas kernels, project_own(): pl.pallas_call(project_own_kernel, in_specs=[SMEM, VMEM, ANY], out_specs=...  6.73 us
    pallas_call x1, Pallas kernels, attention(): pl.pallas_call(attention_kernel, in_specs=[SMEM] + [VMEM] * 3, out_specs=...  3.78 us
  transfers between devices with their start and end apart: 15, of which 10 were waited for; matrix products, arithmetic and copies ran while one was open for 1% of the time, Pallas kernels for 9%

profile of v4, /device:TPU:1, one launch (start us, length us, event | category | flops | bytes accessed | tf_op | source)
XLA Modules:
  0.0 130.2 jit_solution(13482346787611263239)
XLA Ops:
  0.6 0.1 pad_add_fusion.place_ref
  0.7 3.0 %begin.1 = (bf16[8,16,2176]{2,1,0:T(8,128)(2,1)}, bf16[4,64,1792]{2,1,0:T(8,128)(2,1)S(1)}, f32[256,1024]{1,0:T(8,128)S(1)}) custom-call(s32[2]{0:T(128)S(1)} %pad_add_fusion.place_ref, s32[4,64]{1,0:T(4,128)} %seg_hbm.1, bf16[4,64,512]{2,1,0:T(8,128)(2,1)} %k_hbm.1, bf16[4,64,512]{2,1,0:T(8,128)(2,1)} %v_hbm.1, bf16[4,64,1792]{2,1,0:T(8,128)(2,1)} %x_hbm.1, ...), custom_call_target="tpu_custom_call" | custom-call | tf_op jit(solution)/shard_map/begin/pallas_call | solution.py:123
  3.7 2.1 %collective-permute-start.1 = (bf16[4,64,1792]{2,1,0:T(8,128)(2,1)S(1)}, bf16[4,64,1792]{2,1,0:T(8,128)(2,1)S(1)}, u32[]{:S(2)}, u32[]{:S(2)}) collective-permute-start(bf16[4,64,1792]{2,1,0:T(8,128)(2,1)S(1)} %get-tuple-element.33.x_ref), channel_id=1, source_target_pairs={{0,1},{1,0},{2,3},{3,2},{4,5},{5,4},{6,7},{7,6},{8,9},{9,8},{10,11... | collective-permute-start | bytes 2752520 | tf_op jit(solution)/shard_map/ppermute | solution.py:476
  5.8 8.2 %all-to-all-start = ((bf16[8,16,2176]{2,1,0:T(8,128)(2,1)}), bf16[8,16,2176]{2,1,0:T(8,128)(2,1)S(1)}, u32[]{:S(2)}, u32[]{:S(2)}) async-start(bf16[8,16,2176]{2,1,0:T(8,128)(2,1)} %get-tuple-element.32), calls=%async_computation | async-start | bytes 1114112 | tf_op jit(solution)/shard_map/all_to_all | solution.py:451
  14.0 0.0 copy-start
  14.0 6.7 %project_own.1 = (f32[256,1024]{1,0:T(8,128)S(1)}, bf16[1792,1024]{1,0:T(8,128)(2,1)S(1)}) custom-call(s32[2]{0:T(128)S(1)} %pad_add_fusion.place_ref, bf16[4,64,1792]{2,1,0:T(8,128)(2,1)S(1)} %get-tuple-element.33.x_ref, bf16[1024,3584]{1,0:T(8,128)(2,1)} %weight_hbm.3), custom_call_target="tpu_custom_call" | custom-call | flops 939524096 | bytes 7340032 | tf_op jit(solution)/shard_map/project_own/pallas_call | solution.py:159
  20.7 0.0 collective-permute-done.1.x_ref
  20.8 0.0 copy-done
  20.8 2.7 %project_other.1 = bf16[4,2,64,1024]{3,2,1,0:T(8,128)(2,1)} custom-call(s32[2]{0:T(128)S(1)} %pad_add_fusion.place_ref, bf16[4,64,1792]{2,1,0:T(8,128)(2,1)S(1)} %collective-permute-done.1.x_ref, bf16[4,64,1024]{2,1,0:T(8,128)(2,1)S(1)} %copy-done, f32[256,1024]{1,0:T(8,128)S(1)} %get-tuple-element.34.part_0, f32[256,1024]{1,0:T(8,128)S(1)} %get-tuple-element.35.part_1, ...), custom_call_target="tpu_custom_call" | custom-call | flops 939524096 | bytes 3670016 | tf_op jit(solution)/shard_map/project_other/pallas_call | solution.py:197
  23.5 0.9 all-to-all-done.own_ref
  24.3 8.5 %all-to-all-start.1 = ((bf16[8,64,1024]{2,1,0:T(8,128)(2,1)}), bf16[8,64,1024]{2,1,0:T(8,128)(2,1)S(1)}, u32[]{:S(2)}, u32[]{:S(2)}) async-start(bf16[8,64,1024]{2,1,0:T(8,128)(2,1)} %bitcast.10), calls=%async_computation.1 | async-start | bytes 2097152 | tf_op jit(solution)/shard_map/all_to_all | solution.py:451
  32.9 2.7 %collective-permute-start = (bf16[8,16,2176]{2,1,0:T(8,128)(2,1)S(1)}, bf16[8,16,2176]{2,1,0:T(8,128)(2,1)S(1)}, u32[]{:S(2)}, u32[]{:S(2)}) collective-permute-start(bf16[8,16,2176]{2,1,0:T(8,128)(2,1)S(1)} %all-to-all-done.own_ref), channel_id=1, source_target_pairs={{0,2},{2,0},{4,6},{6,4},{8,10},{10,8},{12,14},{14,12},{16,18},{18,... | collective-permute-start | bytes 1671176 | tf_op jit(solution)/shard_map/ppermute | solution.py:478
  35.6 7.1 %collective-permute-done.other_ref = bf16[8,16,2176]{2,1,0:T(8,128)(2,1)S(1)} collective-permute-done((bf16[8,16,2176]{2,1,0:T(8,128)(2,1)S(1)}, bf16[8,16,2176]{2,1,0:T(8,128)(2,1)S(1)}, u32[]{:S(2)}, u32[]{:S(2)}) %collective-permute-start) | collective-permute-done | bytes 557088 | tf_op jit(solution)/shard_map/ppermute | solution.py:478
  42.7 15.6 %all-to-all-done.1.qd_ref = bf16[8,64,1024]{2,1,0:T(8,128)(2,1)S(1)} async-done(((bf16[8,64,1024]{2,1,0:T(8,128)(2,1)}), bf16[8,64,1024]{2,1,0:T(8,128)(2,1)S(1)}, u32[]{:S(2)}, u32[]{:S(2)}) %all-to-all-start.1) | async-done | bytes 1048608 | tf_op jit(solution)/shard_map/all_to_all | solution.py:451
  58.4 0.0 copy-start.1
  58.4 3.8 %attend.1 = (bf16[8,64,512]{2,1,0:T(8,128)(2,1)}, bf16[8,64,512]{2,1,0:T(8,128)(2,1)S(1)}, bf16[8,64,512]{2,1,0:T(8,128)(2,1)S(1)}) custom-call(s32[1]{0:T(128)} %bitcast.side_ref, bf16[8,16,2176]{2,1,0:T(8,128)(2,1)S(1)} %all-to-all-done.own_ref, bf16[8,16,2176]{2,1,0:T(8,128)(2,1)S(1)} %collective-permute-done.other_ref, ...), custom_call_target="tpu_custom_call" | custom-call | flops 3000000000 | bytes 6291456 | tf_op jit(solution)/shard_map/attend/pallas_call | solution.py:321
  62.2 3.5 %all-to-all-start.2 = ((bf16[8,64,512]{2,1,0:T(8,128)(2,1)}), bf16[8,64,512]{2,1,0:T(8,128)(2,1)S(1)}, u32[]{:S(2)}, u32[]{:S(2)}) async-start(bf16[8,64,512]{2,1,0:T(8,128)(2,1)} %get-tuple-element.39), calls=%async_computation.2 | async-start | bytes 1048576 | tf_op jit(solution)/shard_map/all_to_all | solution.py:451
  65.7 2.8 %collective-permute-start.2 = (bf16[8,64,512]{2,1,0:T(8,128)(2,1)S(1)}, bf16[8,64,512]{2,1,0:T(8,128)(2,1)S(1)}, u32[]{:S(2)}, u32[]{:S(2)}) collective-permute-start(bf16[8,64,512]{2,1,0:T(8,128)(2,1)S(1)} %get-tuple-element.38), channel_id=1, source_target_pairs={{0,2},{2,0},{4,6},{6,4},{8,10},{10,8},{12,14},{14,12},{16,18},{18,... | collective-permute-start | bytes 1572872 | tf_op jit(solution)/shard_map/ppermute | solution.py:525
  68.5 9.7 %collective-permute-done.2 = bf16[8,64,512]{2,1,0:T(8,128)(2,1)S(1)} collective-permute-done((bf16[8,64,512]{2,1,0:T(8,128)(2,1)S(1)}, bf16[8,64,512]{2,1,0:T(8,128)(2,1)S(1)}, u32[]{:S(2)}, u32[]{:S(2)}) %collective-permute-start.2) | collective-permute-done | bytes 524320 | tf_op jit(solution)/shard_map/ppermute | solution.py:525
  78.2 0.9 add_convert_fusion
  79.2 0.5 all-to-all-done.2
  79.6 5.8 %all-to-all-start.3 = ((bf16[8,64,512]{2,1,0:T(8,128)(2,1)}), bf16[8,64,512]{2,1,0:T(8,128)(2,1)S(1)}, u32[]{:S(2)}, u32[]{:S(2)}) async-start(bf16[8,64,512]{2,1,0:T(8,128)(2,1)} %add_convert_fusion), calls=%async_computation.3 | async-start | bytes 1048576 | tf_op jit(solution)/shard_map/all_to_all | solution.py:451
  85.4 0.0 copy-done.1
  85.4 0.1 reshape.145
  85.5 0.1 select_reduce_fusion
  85.6 0.6 pick.1
  86.2 4.1 %collective-permute-start.3 = (bf16[2,64,512]{2,1,0:T(8,128)(2,1)S(1)}, bf16[2,64,512]{2,1,0:T(8,128)(2,1)S(1)}, u32[]{:S(2)}, u32[]{:S(2)}) collective-permute-start(bf16[2,64,512]{2,1,0:T(8,128)(2,1)S(1)} %get-tuple-element.43), channel_id=1, source_target_pairs={{0,32},{32,0},{64,96},{96,64},{128,160},{160,128},{192,224},{224,1... | collective-permute-start | bytes 393224 | tf_op jit(solution)/shard_map/ppermute | solution.py:538
  90.3 1.3 %collective-permute-start.4 = (bf16[2,64,512]{2,1,0:T(8,128)(2,1)S(1)}, bf16[2,64,512]{2,1,0:T(8,128)(2,1)S(1)}, u32[]{:S(2)}, u32[]{:S(2)}) collective-permute-start(bf16[2,64,512]{2,1,0:T(8,128)(2,1)S(1)} %get-tuple-element.44), channel_id=1, source_target_pairs={{0,64},{32,96},{64,128},{96,160},{128,192},{160,224},{192,0},{224,... | collective-permute-start | bytes 393224 | tf_op jit(solution)/shard_map/ppermute | solution.py:538
  91.6 1.5 %collective-permute-start.5 = (bf16[2,64,512]{2,1,0:T(8,128)(2,1)S(1)}, bf16[2,64,512]{2,1,0:T(8,128)(2,1)S(1)}, u32[]{:S(2)}, u32[]{:S(2)}) collective-permute-start(bf16[2,64,512]{2,1,0:T(8,128)(2,1)S(1)} %get-tuple-element.45), channel_id=1, source_target_pairs={{0,96},{32,64},{64,160},{96,128},{128,224},{160,192},{192,32},{224... | collective-permute-start | bytes 393224 | tf_op jit(solution)/shard_map/ppermute | solution.py:538
  93.2 1.3 collective-permute-start.6
  94.4 2.0 %collective-permute-start.7 = (bf16[2,64,512]{2,1,0:T(8,128)(2,1)S(1)}, bf16[2,64,512]{2,1,0:T(8,128)(2,1)S(1)}, u32[]{:S(2)}, u32[]{:S(2)}) collective-permute-start(bf16[2,64,512]{2,1,0:T(8,128)(2,1)S(1)} %get-tuple-element.47), channel_id=1, source_target_pairs={{0,160},{32,128},{64,224},{96,192},{128,32},{160,0},{192,96},{224,... | collective-permute-start | bytes 393224 | tf_op jit(solution)/shard_map/ppermute | solution.py:538
  96.5 0.0 collective-permute-done.3.refs_1_
  96.5 1.4 %collective-permute-start.8 = (bf16[2,64,512]{2,1,0:T(8,128)(2,1)S(1)}, bf16[2,64,512]{2,1,0:T(8,128)(2,1)S(1)}, u32[]{:S(2)}, u32[]{:S(2)}) collective-permute-start(bf16[2,64,512]{2,1,0:T(8,128)(2,1)S(1)} %get-tuple-element.48), channel_id=1, source_target_pairs={{0,192},{32,224},{64,0},{96,32},{128,64},{160,96},{192,128},{224,1... | collective-permute-start | bytes 393224 | tf_op jit(solution)/shard_map/ppermute | solution.py:538
  97.8 0.0 collective-permute-done.4.refs_2_
  97.9 1.5 %collective-permute-start.9 = (bf16[2,64,512]{2,1,0:T(8,128)(2,1)S(1)}, bf16[2,64,512]{2,1,0:T(8,128)(2,1)S(1)}, u32[]{:S(2)}, u32[]{:S(2)}) collective-permute-start(bf16[2,64,512]{2,1,0:T(8,128)(2,1)S(1)} %get-tuple-element.49), channel_id=1, source_target_pairs={{0,224},{32,192},{64,32},{96,0},{128,96},{160,64},{192,160},{224,1... | collective-permute-start | bytes 393224 | tf_op jit(solution)/shard_map/ppermute | solution.py:538
  99.3 0.6 collective-permute-done.5.refs_3_
  99.9 3.5 %collective-permute-done.6.refs_4_ = bf16[2,64,512]{2,1,0:T(8,128)(2,1)S(1)} collective-permute-done((bf16[2,64,512]{2,1,0:T(8,128)(2,1)S(1)}, bf16[2,64,512]{2,1,0:T(8,128)(2,1)S(1)}, u32[]{:S(2)}, u32[]{:S(2)}) %collective-permute-start.6) | collective-permute-done | bytes 131104 | tf_op jit(solution)/shard_map/ppermute | solution.py:538
  103.4 3.0 %collective-permute-done.7.refs_5_ = bf16[2,64,512]{2,1,0:T(8,128)(2,1)S(1)} collective-permute-done((bf16[2,64,512]{2,1,0:T(8,128)(2,1)S(1)}, bf16[2,64,512]{2,1,0:T(8,128)(2,1)S(1)}, u32[]{:S(2)}, u32[]{:S(2)}) %collective-permute-start.7) | collective-permute-done | bytes 131104 | tf_op jit(solution)/shard_map/ppermute | solution.py:538
  106.4 0.0 collective-permute-done.8.refs_6_
  106.4 0.9 collective-permute-done.9.refs_7_
  107.3 0.0 all-to-all-done.3
  107.3 1.6 %pick_stacked.1 = bf16[8,2,64,512]{3,2,1,0:T(8,128)(2,1)} custom-call(s32[8]{0:T(128)S(1)} %get-tuple-element.61.index_ref, bf16[4,2,64,512]{3,2,1,0:T(8,128)(2,1)S(1)} %bitcast.8), custom_call_target="tpu_custom_call" | custom-call | tf_op jit(solution)/shard_map/pick_stacked/pallas_call | solution.py:374
  108.9 4.6 %all-to-all-start.4 = ((bf16[8,2,64,512]{3,2,1,0:T(8,128)(2,1)}), bf16[8,2,64,512]{3,2,1,0:T(8,128)(2,1)S(1)}, u32[]{:S(2)}, u32[]{:S(2)}) async-start(bf16[8,2,64,512]{3,2,1,0:T(8,128)(2,1)} %pick_stacked.1), calls=%async_computation.4 | async-start | bytes 2097152 | tf_op jit(solution)/shard_map/all_to_all | solution.py:451
  113.5 0.2 select_reduce_fusion.3.index_ref
  113.7 0.2 select_reduce_fusion.2.index_ref
  113.9 1.4 %place_q.1 = bf16[4,64,1024]{2,1,0:T(8,128)(2,1)} custom-call(s32[4]{0:T(128)S(1)} %select_reduce_fusion.2.index_ref, bf16[2,64,512]{2,1,0:T(8,128)(2,1)S(1)} %get-tuple-element.50.refs_0_, bf16[2,64,512]{2,1,0:T(8,128)(2,1)S(1)} %collective-permute-done.3.refs_1_, bf16[2,64,512]{2,1,0:T(8,128)(2,1)S(1)} %collective-permute-done.4.refs_2_, ...), custom_call_target="tpu_custom_call" | custom-call | tf_op jit(solution)/shard_map/place_q/pallas_call | solution.py:410
  115.3 13.3 %all-to-all-done.4.in_ref = bf16[8,2,64,512]{3,2,1,0:T(8,128)(2,1)S(1)} async-done(((bf16[8,2,64,512]{3,2,1,0:T(8,128)(2,1)}), bf16[8,2,64,512]{3,2,1,0:T(8,128)(2,1)S(1)}, u32[]{:S(2)}, u32[]{:S(2)}) %all-to-all-start.4) | async-done | bytes 1048608 | tf_op jit(solution)/shard_map/all_to_all | solution.py:451
  128.6 1.5 %place_kv.1 = (bf16[4,64,512]{2,1,0:T(8,128)(2,1)}, bf16[4,64,512]{2,1,0:T(8,128)(2,1)}) custom-call(s32[4]{0:T(128)S(1)} %select_reduce_fusion.3.index_ref, bf16[8,2,64,512]{3,2,1,0:T(8,128)(2,1)S(1)} %all-to-all-done.4.in_ref), custom_call_target="tpu_custom_call" | custom-call | tf_op jit(solution)/shard_map/place_kv/pallas_call | solution.py:439
  (5 shorter events, 0.1 us)
Async XLA Ops:
  3.7 17.1 %collective-permute-start.1 = (bf16[4,64,1792]{2,1,0:T(8,128)(2,1)S(1)}, bf16[4,64,1792]{2,1,0:T(8,128)(2,1)S(1)}, u32[]{:S(2)}, u32[]{:S(2)}) collective-permute-start(bf16[4,64,1792]{2,1,0:T(8,128)(2,1)S(1)} %get-tuple-element.33.x_ref), channel_id=1, source_target_pairs={{0,1},{1,0},{2,3},{3,2},{4,5},{5,4},{6,7},{7,6},{8,9},{9,8},{10,11... | collective-permute-start | bytes 2752520 | tf_op jit(solution)/shard_map/ppermute | solution.py:476
  5.8 18.5 %all-to-all-start = ((bf16[8,16,2176]{2,1,0:T(8,128)(2,1)}), bf16[8,16,2176]{2,1,0:T(8,128)(2,1)S(1)}, u32[]{:S(2)}, u32[]{:S(2)}) async-start(bf16[8,16,2176]{2,1,0:T(8,128)(2,1)} %get-tuple-element.32), calls=%async_computation | async-start | bytes 1114112 | tf_op jit(solution)/shard_map/all_to_all | solution.py:451
  14.0 6.8 %copy-start = (bf16[4,64,1024]{2,1,0:T(8,128)(2,1)S(1)}, bf16[4,64,1024]{2,1,0:T(8,128)(2,1)}, u32[]{:S(2)}) copy-start(bf16[4,64,1024]{2,1,0:T(8,128)(2,1)} %q_ref.1) | copy-start | bytes 1572868
  24.3 34.0 %all-to-all-start.1 = ((bf16[8,64,1024]{2,1,0:T(8,128)(2,1)}), bf16[8,64,1024]{2,1,0:T(8,128)(2,1)S(1)}, u32[]{:S(2)}, u32[]{:S(2)}) async-start(bf16[8,64,1024]{2,1,0:T(8,128)(2,1)} %bitcast.10), calls=%async_computation.1 | async-start | bytes 2097152 | tf_op jit(solution)/shard_map/all_to_all | solution.py:451
  32.9 9.9 %collective-permute-start = (bf16[8,16,2176]{2,1,0:T(8,128)(2,1)S(1)}, bf16[8,16,2176]{2,1,0:T(8,128)(2,1)S(1)}, u32[]{:S(2)}, u32[]{:S(2)}) collective-permute-start(bf16[8,16,2176]{2,1,0:T(8,128)(2,1)S(1)} %all-to-all-done.own_ref), channel_id=1, source_target_pairs={{0,2},{2,0},{4,6},{6,4},{8,10},{10,8},{12,14},{14,12},{16,18},{18,... | collective-permute-start | bytes 1671176 | tf_op jit(solution)/shard_map/ppermute | solution.py:478
  58.4 27.0 %copy-start.1 = (s32[32]{0:T(128)S(1)}, s32[32]{0:T(128)}, u32[]{:S(2)}) copy-start(s32[32]{0:T(128)} %param.13) | copy-start | bytes 388
  62.2 17.5 %all-to-all-start.2 = ((bf16[8,64,512]{2,1,0:T(8,128)(2,1)}), bf16[8,64,512]{2,1,0:T(8,128)(2,1)S(1)}, u32[]{:S(2)}, u32[]{:S(2)}) async-start(bf16[8,64,512]{2,1,0:T(8,128)(2,1)} %get-tuple-element.39), calls=%async_computation.2 | async-start | bytes 1048576 | tf_op jit(solution)/shard_map/all_to_all | solution.py:451
  65.7 12.6 %collective-permute-start.2 = (bf16[8,64,512]{2,1,0:T(8,128)(2,1)S(1)}, bf16[8,64,512]{2,1,0:T(8,128)(2,1)S(1)}, u32[]{:S(2)}, u32[]{:S(2)}) collective-permute-start(bf16[8,64,512]{2,1,0:T(8,128)(2,1)S(1)} %get-tuple-element.38), channel_id=1, source_target_pairs={{0,2},{2,0},{4,6},{6,4},{8,10},{10,8},{12,14},{14,12},{16,18},{18,... | collective-permute-start | bytes 1572872 | tf_op jit(solution)/shard_map/ppermute | solution.py:525
  79.6 27.7 %all-to-all-start.3 = ((bf16[8,64,512]{2,1,0:T(8,128)(2,1)}), bf16[8,64,512]{2,1,0:T(8,128)(2,1)S(1)}, u32[]{:S(2)}, u32[]{:S(2)}) async-start(bf16[8,64,512]{2,1,0:T(8,128)(2,1)} %add_convert_fusion), calls=%async_computation.3 | async-start | bytes 1048576 | tf_op jit(solution)/shard_map/all_to_all | solution.py:451
  86.2 10.2 %collective-permute-start.3 = (bf16[2,64,512]{2,1,0:T(8,128)(2,1)S(1)}, bf16[2,64,512]{2,1,0:T(8,128)(2,1)S(1)}, u32[]{:S(2)}, u32[]{:S(2)}) collective-permute-start(bf16[2,64,512]{2,1,0:T(8,128)(2,1)S(1)} %get-tuple-element.43), channel_id=1, source_target_pairs={{0,32},{32,0},{64,96},{96,64},{128,160},{160,128},{192,224},{224,1... | collective-permute-start | bytes 393224 | tf_op jit(solution)/shard_map/ppermute | solution.py:538
  90.3 7.5 %collective-permute-start.4 = (bf16[2,64,512]{2,1,0:T(8,128)(2,1)S(1)}, bf16[2,64,512]{2,1,0:T(8,128)(2,1)S(1)}, u32[]{:S(2)}, u32[]{:S(2)}) collective-permute-start(bf16[2,64,512]{2,1,0:T(8,128)(2,1)S(1)} %get-tuple-element.44), channel_id=1, source_target_pairs={{0,64},{32,96},{64,128},{96,160},{128,192},{160,224},{192,0},{224,... | collective-permute-start | bytes 393224 | tf_op jit(solution)/shard_map/ppermute | solution.py:538
  91.6 8.3 %collective-permute-start.5 = (bf16[2,64,512]{2,1,0:T(8,128)(2,1)S(1)}, bf16[2,64,512]{2,1,0:T(8,128)(2,1)S(1)}, u32[]{:S(2)}, u32[]{:S(2)}) collective-permute-start(bf16[2,64,512]{2,1,0:T(8,128)(2,1)S(1)} %get-tuple-element.45), channel_id=1, source_target_pairs={{0,96},{32,64},{64,160},{96,128},{128,224},{160,192},{192,32},{224... | collective-permute-start | bytes 393224 | tf_op jit(solution)/shard_map/ppermute | solution.py:538
  93.2 10.3 %collective-permute-start.6 = (bf16[2,64,512]{2,1,0:T(8,128)(2,1)S(1)}, bf16[2,64,512]{2,1,0:T(8,128)(2,1)S(1)}, u32[]{:S(2)}, u32[]{:S(2)}) collective-permute-start(bf16[2,64,512]{2,1,0:T(8,128)(2,1)S(1)} %get-tuple-element.46), channel_id=1, source_target_pairs={{0,128},{32,160},{64,192},{96,224},{128,0},{160,32},{192,64},{224,... | collective-permute-start | bytes 393224 | tf_op jit(solution)/shard_map/ppermute | solution.py:538
  94.4 12.0 %collective-permute-start.7 = (bf16[2,64,512]{2,1,0:T(8,128)(2,1)S(1)}, bf16[2,64,512]{2,1,0:T(8,128)(2,1)S(1)}, u32[]{:S(2)}, u32[]{:S(2)}) collective-permute-start(bf16[2,64,512]{2,1,0:T(8,128)(2,1)S(1)} %get-tuple-element.47), channel_id=1, source_target_pairs={{0,160},{32,128},{64,224},{96,192},{128,32},{160,0},{192,96},{224,... | collective-permute-start | bytes 393224 | tf_op jit(solution)/shard_map/ppermute | solution.py:538
  96.5 10.0 %collective-permute-start.8 = (bf16[2,64,512]{2,1,0:T(8,128)(2,1)S(1)}, bf16[2,64,512]{2,1,0:T(8,128)(2,1)S(1)}, u32[]{:S(2)}, u32[]{:S(2)}) collective-permute-start(bf16[2,64,512]{2,1,0:T(8,128)(2,1)S(1)} %get-tuple-element.48), channel_id=1, source_target_pairs={{0,192},{32,224},{64,0},{96,32},{128,64},{160,96},{192,128},{224,1... | collective-permute-start | bytes 393224 | tf_op jit(solution)/shard_map/ppermute | solution.py:538
  97.9 9.5 %collective-permute-start.9 = (bf16[2,64,512]{2,1,0:T(8,128)(2,1)S(1)}, bf16[2,64,512]{2,1,0:T(8,128)(2,1)S(1)}, u32[]{:S(2)}, u32[]{:S(2)}) collective-permute-start(bf16[2,64,512]{2,1,0:T(8,128)(2,1)S(1)} %get-tuple-element.49), channel_id=1, source_target_pairs={{0,224},{32,192},{64,32},{96,0},{128,96},{160,64},{192,160},{224,1... | collective-permute-start | bytes 393224 | tf_op jit(solution)/shard_map/ppermute | solution.py:538
  108.9 19.7 %all-to-all-start.4 = ((bf16[8,2,64,512]{3,2,1,0:T(8,128)(2,1)}), bf16[8,2,64,512]{3,2,1,0:T(8,128)(2,1)S(1)}, u32[]{:S(2)}, u32[]{:S(2)}) async-start(bf16[8,2,64,512]{3,2,1,0:T(8,128)(2,1)} %pick_stacked.1), calls=%async_computation.4 | async-start | bytes 2097152 | tf_op jit(solution)/shard_map/all_to_all | solution.py:451

commit v5 on v4

--- a/solution.py
+++ b/solution.py
@@ -50,8 +50,11 @@
         part_ref[:, at] = dot(x, weight_ref[at], 1, 1)
 
 
+def on_core():
+    return lax.rem(lax.axis_index("dp"), 2)
+
+
 def begin_kernel(
-    place_ref,
     seg_hbm,
     k_hbm,
     v_hbm,
@@ -80,9 +83,9 @@
         copy.start()
     copies[3].wait()
 
-    @pl.when(place_ref[1] == 0)
+    @pl.when(on_core() == 0)
     def _():
-        own_half(place_ref[0], x_ref, weight_hbm, part_ref, weight_ref, weight_sems)
+        own_half(lax.axis_index("tp"), x_ref, weight_hbm, part_ref, weight_ref, weight_sems)
 
     copies[0].wait()
     place = lax.broadcasted_iota(jnp.int32, (TILE, block), 1)
@@ -115,14 +118,14 @@
     return [pltpu.with_memory_space_constraint(x, pltpu.HBM) for x in arrays]
 
 
-def begin(place, seg, k, v, x, weight):
+def begin(seg, k, v, x, weight):
     rows, block, kv_width = k.shape
     kv_heads = kv_width // HEAD
     lanes = block // TILE * 2 * HEAD + 128
     width, half = weight.shape[0], x.shape[2]
     return pl.pallas_call(
         begin_kernel,
-        in_specs=[SMEM] + [ANY] * 5,
+        in_specs=[ANY] * 5,
         out_specs=[VMEM] * 3,
         out_shape=[
             pltpu.HBM((rows * kv_heads, TILE, lanes), BF16),
@@ -139,26 +142,26 @@
         ],
         compiler_params=pltpu.CompilerParams(vmem_limit_bytes=MEDIUM_VMEM),
         name="begin",
-    )(place, *in_hbm(seg, k, v, x, weight))
+    )(*in_hbm(seg, k, v, x, weight))
 
 
 def project_own_kernel(
-    place_ref, x_ref, weight_hbm, part_ref, turned_ref, weight_ref, sems
+    x_ref, weight_hbm, part_ref, turned_ref, weight_ref, sems
 ):
-    for at in load_half(1 - place_ref[0], weight_hbm, weight_ref, sems):
+    for at in load_half(1 - lax.axis_index("tp"), weight_hbm, weight_ref, sems):
         turned_ref[:, at] = weight_ref[at].T
 
-    @pl.when(place_ref[1] != 0)
+    @pl.when(on_core() != 0)
     def _():
-        own_half(place_ref[0], x_ref, weight_hbm, part_ref, weight_ref, sems)
-
-
-def project_own(place, x, weight):
+        own_half(lax.axis_index("tp"), x_ref, weight_hbm, part_ref, weight_ref, sems)
+
+
+def project_own(x, weight):
     rows, block, half = x.shape
     width = weight.shape[0]
     return pl.pallas_call(
         project_own_kernel,
-        in_specs=[SMEM, VMEM, ANY],
+        in_specs=[VMEM, ANY],
         out_specs=[VMEM, VMEM],
         out_shape=[
             jax.ShapeDtypeStruct((rows * block, width), F32),
@@ -175,10 +178,10 @@
             transcendentals=0,
         ),
         name="project_own",
-    )(place, x, *in_hbm(weight))
-
-
-def other_half_kernel(place_ref, x_ref, q_ref, part_0, part_1, turned_ref, out_ref):
+    )(x, *in_hbm(weight))
+
+
+def other_half_kernel(x_ref, q_ref, part_0, part_1, turned_ref, out_ref):
     rows, block, half = x_ref.shape
     kv_heads = out_ref.shape[1]
     width = turned_ref.shape[1] // kv_heads
@@ -186,17 +189,17 @@
     for h in range(kv_heads):
         at = slice(h * width, (h + 1) * width)
         out_ref[:, h, :, :width] = q_ref[:, :, at]
-        part = jnp.where(place_ref[1] == 0, part_0[:, at], part_1[:, at])
+        part = jnp.where(on_core() == 0, part_0[:, at], part_1[:, at])
         total = part + dot(x, turned_ref[:, at], 1, 0)
         out_ref[:, h, :, width:] = total.astype(BF16).reshape(rows, block, width)
 
 
-def project_other(place, x, q, part_0, part_1, turned, kv_heads):
+def project_other(x, q, part_0, part_1, turned, kv_heads):
     rows, block, half = x.shape
     total = turned.shape[1]
     return pl.pallas_call(
         other_half_kernel,
-        in_specs=[SMEM] + [VMEM] * 5,
+        in_specs=[VMEM] * 5,
         out_specs=VMEM,
         out_shape=pltpu.HBM((rows, kv_heads, block, 2 * total // kv_heads), BF16),
         compiler_params=pltpu.CompilerParams(vmem_limit_bytes=MEDIUM_VMEM),
@@ -206,17 +209,25 @@
             transcendentals=0,
         ),
         name="project_other",
-    )(place, x, q, part_0, part_1, turned)
+    )(x, q, part_0, part_1, turned)
 
 
 def attention_kernel(
-    side_ref, own_ref, other_ref, qd_ref, dq_ref, dkv_own, dkv_other, acc
+    own_ref,
+    other_ref,
+    qd_ref,
+    dq_hbm,
+    dkv_own,
+    dkv_other,
+    acc,
+    dq_ref,
+    sems,
 ):
     steps, block, width = dq_ref.shape
     per = 2
     lanes = per * block
     pieces = block // TILE
-    side = side_ref[0]
+    side = lax.rem(lax.axis_index("ctx"), 2)
 
     def gathered(ref, low, high, start):
         return jnp.concatenate(
@@ -298,10 +309,16 @@
         dq = (dq * SCALE).astype(BF16)
         for i in range(per):
             at = slice(i * block, (i + 1) * block)
-            dq_ref[SLOT[z + i], :, :HEAD] = dq[:lanes][at]
-            dq_ref[SLOT[z + i], :, HEAD:] = dq[lanes:][at]
+            slot = SLOT[z + i]
+            dq_ref[slot, :, :HEAD] = dq[:lanes][at]
+            dq_ref[slot, :, HEAD:] = dq[lanes:][at]
+            copies.append(
+                pltpu.make_async_copy(dq_ref.at[slot], dq_hbm.at[slot], sems.at[slot])
+            )
+            copies[-1].start()
 
     held = None
+    copies = []
     for z in range(0, steps, per):
         ready = scores(z)
         if held is not None:
@@ -313,27 +330,33 @@
         for which, out_ref in enumerate((dkv_own, dkv_other)):
             out_ref[SLOT[z], :, :HEAD] = (acc[which, at, :HEAD] * SCALE).astype(BF16)
             out_ref[SLOT[z], :, HEAD:] = acc[which, at, HEAD:].astype(BF16)
-
-
-def attention(side, own, other, q_and_grad):
+    for copy in copies:
+        copy.wait()
+
+
+def attention(own, other, q_and_grad):
     steps, block, width = q_and_grad.shape
     width //= 2
     return pl.pallas_call(
         attention_kernel,
-        in_specs=[SMEM] + [VMEM] * 3,
-        out_specs=[VMEM] * 3,
+        in_specs=[VMEM] * 3,
+        out_specs=[ANY, VMEM, VMEM],
         out_shape=[
             pltpu.HBM((steps, block, width), BF16),
             pltpu.VMEM((steps, block, width), BF16),
             pltpu.VMEM((steps, block, width), BF16),
         ],
-        scratch_shapes=[pltpu.VMEM((2, steps * block, width), F32)],
+        scratch_shapes=[
+            pltpu.VMEM((2, steps * block, width), F32),
+            pltpu.VMEM((steps, block, width), BF16),
+            pltpu.SemaphoreType.DMA((steps,)),
+        ],
         compiler_params=pltpu.CompilerParams(vmem_limit_bytes=LARGE_VMEM),
         cost_estimate=pl.CostEstimate(
             flops=3 * 10**9, bytes_accessed=6 * 2**20, transcendentals=1200000
         ),
         name="attend",
-    )(side, own, other, q_and_grad)
+    )(own, other, q_and_grad)
 
 
 def run_copies(copies):
@@ -345,7 +368,10 @@
 
 def pick_kernel(index_ref, in_ref, *outs):
     for i, out in enumerate(outs):
-        out[...] = in_ref[index_ref[i]]
+
+        @pl.when(index_ref[i] >= 0)
+        def _():
+            out[...] = in_ref[index_ref[i]]
 
 
 def pick_rows(index, source):
@@ -361,12 +387,19 @@
 
 
 def pick_stacked_kernel(index_ref, in_ref, out_ref, sems):
-    run_copies(
-        [
-            pltpu.make_async_copy(in_ref.at[index_ref[i]], out_ref.at[i], sems.at[i])
-            for i in range(out_ref.shape[0])
-        ]
-    )
+    def each(act):
+        for i in range(out_ref.shape[0]):
+
+            @pl.when(index_ref[i] >= 0)
+            def _():
+                act(
+                    pltpu.make_async_copy(
+                        in_ref.at[index_ref[i]], out_ref.at[i], sems.at[i]
+                    )
+                )
+
+    each(lambda copy: copy.start())
+    each(lambda copy: copy.wait())
 
 
 def pick_stacked(index, source):
@@ -463,15 +496,13 @@
     groups = lax.axis_size("dp")
     pair = n_ctx // units
     ctx = lax.axis_index("ctx")
-    tp = lax.axis_index("tp")
     group = lax.axis_index("dp")
     side = ctx % pair
     columns = [[z * pair + h for z in ORDER] for h in range(pair)]
     swap = [(z * pair + h, z * pair + 1 - h) for z in range(units) for h in range(pair)]
 
-    place = jnp.stack([tp, group % 2]).astype(jnp.int32)
     own, grad, part_0 = begin(
-        place, segment_ids, key_states, value_state_rows, output_grad, out_weight
+        segment_ids, key_states, value_state_rows, output_grad, out_weight
     )
     other_grad = lax.ppermute(grad, "tp", [(0, 1), (1, 0)])
     own = exchange(own, "ctx", columns)
@@ -486,13 +517,16 @@
     own_targets = lax.dynamic_slice_in_dim(dest, group, 1, 0) // rows
 
     def row_for(targets):
-        return jnp.sum(
-            jnp.where(
-                own_targets == targets[:, None],
-                jnp.arange(rows, dtype=jnp.int32)[None, :],
-                0,
-            ),
-            axis=1,
+        return (
+            jnp.sum(
+                jnp.where(
+                    own_targets == targets[:, None],
+                    jnp.arange(1, rows + 1, dtype=jnp.int32)[None, :],
+                    0,
+                ),
+                axis=1,
+            )
+            - 1
         )
 
     wanted = group * rows + jnp.arange(rows, dtype=jnp.int32)
@@ -511,16 +545,14 @@
     send_index = row_for(steps)
     send_step = row_for(partner(group, steps, 1))
 
-    part_1, turned = project_own(place, grad, out_weight)
+    part_1, turned = project_own(grad, out_weight)
     q_and_grad = project_other(
-        place, other_grad, queries, part_0, part_1, turned, kv_heads
+        other_grad, queries, part_0, part_1, turned, kv_heads
     )
     q_and_grad = q_and_grad.reshape(units, block, q_and_grad.shape[3])
     q_and_grad = exchange(q_and_grad, "ctx", columns)
 
-    dq, dkv_mine, dkv_theirs = attention(
-        side[None].astype(jnp.int32), own, other, q_and_grad
-    )
+    dq, dkv_mine, dkv_theirs = attention(own, other, q_and_grad)
 
     dkv_back = lax.ppermute(dkv_theirs, "ctx", swap)
     dq = exchange(dq, "ctx", columns)

time: 131 us -> 129 us (0.985)
  Pallas kernels: 21.2 us -> 19.4 us
    pallas_call x4, Pallas kernels: 16.2 us -> 14.4 us  [the longest x1 6.24 us: project_own(): pl.pallas_call(project_own_kernel, in_specs=[VMEM, ANY], out_specs=[VMEM,...]
  transfers between devices with their start and end apart: 15 -> 15, of which waited for: 10 -> 11; matrix products, arithmetic and copies ran while one was open for 1% -> 1% of each run, Pallas kernels for 9% -> 8%
where the time goes in v5:
time: 129 us
  waiting for transfers between devices  56.2 us (44%)
  starting transfers between devices  50.8 us (39%)
  Pallas kernels  19.4 us (15%)
  other arithmetic  1.45 us (1%)
    all_to_all x5, waiting for transfers between devices, exchange(): lax.all_to_all(x, axis, split_axis=0, concat_axis=0, tiled=True, axis_ind...  30.9 us
    all_to_all x5, starting transfers between devices, exchange(): lax.all_to_all(x, axis, split_axis=0, concat_axis=0, tiled=True, axis_ind...  30.1 us
    ppermute x7, starting transfers between devices, on_device(): got.append(lax.ppermute(sent[i], 'dp', route))  13.1 us
    ppermute x1, waiting for transfers between devices, on_device(): dkv_back = lax.ppermute(dkv_theirs, 'ctx', swap)  9.65 us
    ppermute x7, waiting for transfers between devices, on_device(): got.append(lax.ppermute(sent[i], 'dp', route))  8.02 us
    ppermute x1, waiting for transfers between devices, on_device(): other = lax.ppermute(own, 'ctx', swap)  7.14 us
    pallas_call x1, Pallas kernels, project_own(): pl.pallas_call(project_own_kernel, in_specs=[VMEM, ANY], out_specs=[VMEM,...  6.24 us
    pallas_call x1, Pallas kernels, attention(): pl.pallas_call(attention_kernel, in_specs=[VMEM] * 3, out_specs=[ANY, VME...  3.67 us
  transfers between devices with their start and end apart: 15, of which 11 were waited for; matrix products, arithmetic and copies ran while one was open for 1% of the time, Pallas kernels for 8%

profile of v5, /device:TPU:1, one launch (start us, length us, event | category | flops | bytes accessed | tf_op | source)
XLA Modules:
  0.0 128.8 jit_solution(3598005172914538101)
XLA Ops:
  0.6 2.4 %begin.1 = (bf16[8,16,2176]{2,1,0:T(8,128)(2,1)}, bf16[4,64,1792]{2,1,0:T(8,128)(2,1)S(1)}, f32[256,1024]{1,0:T(8,128)S(1)}) custom-call(s32[4,64]{1,0:T(4,128)} %seg_hbm.1, bf16[4,64,512]{2,1,0:T(8,128)(2,1)} %k_hbm.1, bf16[4,64,512]{2,1,0:T(8,128)(2,1)} %v_hbm.1, bf16[4,64,1792]{2,1,0:T(8,128)(2,1)} %x_hbm.1, bf16[1024,3584]{1,0:T(8,128)(2,1)} %weight_hbm.3), custom_call_target="tpu_custom_call" | custom-call | tf_op jit(solution)/shard_map/begin/pallas_call | solution.py:126
  3.0 2.1 %collective-permute-start.1 = (bf16[4,64,1792]{2,1,0:T(8,128)(2,1)S(1)}, bf16[4,64,1792]{2,1,0:T(8,128)(2,1)S(1)}, u32[]{:S(2)}, u32[]{:S(2)}) collective-permute-start(bf16[4,64,1792]{2,1,0:T(8,128)(2,1)S(1)} %get-tuple-element.33.x_ref), channel_id=1, source_target_pairs={{0,1},{1,0},{2,3},{3,2},{4,5},{5,4},{6,7},{7,6},{8,9},{9,8},{10,11... | collective-permute-start | bytes 2752520 | tf_op jit(solution)/shard_map/ppermute | solution.py:507
  5.2 8.2 %all-to-all-start = ((bf16[8,16,2176]{2,1,0:T(8,128)(2,1)}), bf16[8,16,2176]{2,1,0:T(8,128)(2,1)S(1)}, u32[]{:S(2)}, u32[]{:S(2)}) async-start(bf16[8,16,2176]{2,1,0:T(8,128)(2,1)} %get-tuple-element.32), calls=%async_computation | async-start | bytes 1114112 | tf_op jit(solution)/shard_map/all_to_all | solution.py:484
  13.4 0.0 copy-start
  13.4 6.2 %project_own.1 = (f32[256,1024]{1,0:T(8,128)S(1)}, bf16[1792,1024]{1,0:T(8,128)(2,1)S(1)}) custom-call(bf16[4,64,1792]{2,1,0:T(8,128)(2,1)S(1)} %get-tuple-element.33.x_ref, bf16[1024,3584]{1,0:T(8,128)(2,1)} %weight_hbm.3), custom_call_target="tpu_custom_call" | custom-call | flops 939524096 | bytes 7340032 | tf_op jit(solution)/shard_map/project_own/pallas_call | solution.py:162
  19.6 0.5 collective-permute-done.1.x_ref
  20.1 0.0 copy-done
  20.1 2.1 %project_other.1 = bf16[4,2,64,1024]{3,2,1,0:T(8,128)(2,1)} custom-call(bf16[4,64,1792]{2,1,0:T(8,128)(2,1)S(1)} %collective-permute-done.1.x_ref, bf16[4,64,1024]{2,1,0:T(8,128)(2,1)S(1)} %copy-done, f32[256,1024]{1,0:T(8,128)S(1)} %get-tuple-element.34.part_0, f32[256,1024]{1,0:T(8,128)S(1)} %get-tuple-element.35.part_1, ...), custom_call_target="tpu_custom_call" | custom-call | flops 939524096 | bytes 3670016 | tf_op jit(solution)/shard_map/project_other/pallas_call | solution.py:200
  22.2 0.0 copy-start.1
  22.2 1.5 %all-to-all-done.own_ref = bf16[8,16,2176]{2,1,0:T(8,128)(2,1)S(1)} async-done(((bf16[8,16,2176]{2,1,0:T(8,128)(2,1)}), bf16[8,16,2176]{2,1,0:T(8,128)(2,1)S(1)}, u32[]{:S(2)}, u32[]{:S(2)}) %all-to-all-start) | async-done | bytes 557088 | tf_op jit(solution)/shard_map/all_to_all | solution.py:484
  23.7 8.1 %all-to-all-start.1 = ((bf16[8,64,1024]{2,1,0:T(8,128)(2,1)}), bf16[8,64,1024]{2,1,0:T(8,128)(2,1)S(1)}, u32[]{:S(2)}, u32[]{:S(2)}) async-start(bf16[8,64,1024]{2,1,0:T(8,128)(2,1)} %bitcast.7), calls=%async_computation.1 | async-start | bytes 2097152 | tf_op jit(solution)/shard_map/all_to_all | solution.py:484
  31.8 2.7 %collective-permute-start = (bf16[8,16,2176]{2,1,0:T(8,128)(2,1)S(1)}, bf16[8,16,2176]{2,1,0:T(8,128)(2,1)S(1)}, u32[]{:S(2)}, u32[]{:S(2)}) collective-permute-start(bf16[8,16,2176]{2,1,0:T(8,128)(2,1)S(1)} %all-to-all-done.own_ref), channel_id=1, source_target_pairs={{0,2},{2,0},{4,6},{6,4},{8,10},{10,8},{12,14},{14,12},{16,18},{18,... | collective-permute-start | bytes 1671176 | tf_op jit(solution)/shard_map/ppermute | solution.py:509
  34.5 7.1 %collective-permute-done.other_ref = bf16[8,16,2176]{2,1,0:T(8,128)(2,1)S(1)} collective-permute-done((bf16[8,16,2176]{2,1,0:T(8,128)(2,1)S(1)}, bf16[8,16,2176]{2,1,0:T(8,128)(2,1)S(1)}, u32[]{:S(2)}, u32[]{:S(2)}) %collective-permute-start) | collective-permute-done | bytes 557088 | tf_op jit(solution)/shard_map/ppermute | solution.py:509
  41.7 15.6 %all-to-all-done.1.qd_ref = bf16[8,64,1024]{2,1,0:T(8,128)(2,1)S(1)} async-done(((bf16[8,64,1024]{2,1,0:T(8,128)(2,1)}), bf16[8,64,1024]{2,1,0:T(8,128)(2,1)S(1)}, u32[]{:S(2)}, u32[]{:S(2)}) %all-to-all-start.1) | async-done | bytes 1048608 | tf_op jit(solution)/shard_map/all_to_all | solution.py:484
  57.3 3.7 %attend.1 = (bf16[8,64,512]{2,1,0:T(8,128)(2,1)}, bf16[8,64,512]{2,1,0:T(8,128)(2,1)S(1)}, bf16[8,64,512]{2,1,0:T(8,128)(2,1)S(1)}) custom-call(bf16[8,16,2176]{2,1,0:T(8,128)(2,1)S(1)} %all-to-all-done.own_ref, bf16[8,16,2176]{2,1,0:T(8,128)(2,1)S(1)} %collective-permute-done.other_ref, bf16[8,64,1024]{2,1,0:T(8,128)(2,1)S(1)} %all-to-all-done.1.qd_ref), custom_call_target="tpu_custom_call" | custom-call | flops 3000000000 | bytes 6291456 | tf_op jit(solution)/shard_map/attend/pallas_call | solution.py:340
  61.0 3.5 %all-to-all-start.2 = ((bf16[8,64,512]{2,1,0:T(8,128)(2,1)}), bf16[8,64,512]{2,1,0:T(8,128)(2,1)S(1)}, u32[]{:S(2)}, u32[]{:S(2)}) async-start(bf16[8,64,512]{2,1,0:T(8,128)(2,1)} %get-tuple-element.39), calls=%async_computation.2 | async-start | bytes 1048576 | tf_op jit(solution)/shard_map/all_to_all | solution.py:484
  64.5 2.8 %collective-permute-start.2 = (bf16[8,64,512]{2,1,0:T(8,128)(2,1)S(1)}, bf16[8,64,512]{2,1,0:T(8,128)(2,1)S(1)}, u32[]{:S(2)}, u32[]{:S(2)}) collective-permute-start(bf16[8,64,512]{2,1,0:T(8,128)(2,1)S(1)} %get-tuple-element.38), channel_id=1, source_target_pairs={{0,2},{2,0},{4,6},{6,4},{8,10},{10,8},{12,14},{14,12},{16,18},{18,... | collective-permute-start | bytes 1572872 | tf_op jit(solution)/shard_map/ppermute | solution.py:557
  67.3 0.0 copy-done.1
  67.3 0.1 reshape.149
  67.4 9.6 %collective-permute-done.2 = bf16[8,64,512]{2,1,0:T(8,128)(2,1)S(1)} collective-permute-done((bf16[8,64,512]{2,1,0:T(8,128)(2,1)S(1)}, bf16[8,64,512]{2,1,0:T(8,128)(2,1)S(1)}, u32[]{:S(2)}, u32[]{:S(2)}) %collective-permute-start.2) | collective-permute-done | bytes 524320 | tf_op jit(solution)/shard_map/ppermute | solution.py:557
  77.1 0.9 add_convert_fusion
  78.0 0.5 all-to-all-done.2
  78.5 5.8 %all-to-all-start.3 = ((bf16[8,64,512]{2,1,0:T(8,128)(2,1)}), bf16[8,64,512]{2,1,0:T(8,128)(2,1)S(1)}, u32[]{:S(2)}, u32[]{:S(2)}) async-start(bf16[8,64,512]{2,1,0:T(8,128)(2,1)} %add_convert_fusion), calls=%async_computation.3 | async-start | bytes 1048576 | tf_op jit(solution)/shard_map/all_to_all | solution.py:484
  84.3 0.1 select_reduce_fusion
  84.4 0.6 pick.1
  85.0 4.1 %collective-permute-start.3 = (bf16[2,64,512]{2,1,0:T(8,128)(2,1)S(1)}, bf16[2,64,512]{2,1,0:T(8,128)(2,1)S(1)}, u32[]{:S(2)}, u32[]{:S(2)}) collective-permute-start(bf16[2,64,512]{2,1,0:T(8,128)(2,1)S(1)} %get-tuple-element.43), channel_id=1, source_target_pairs={{0,32},{32,0},{64,96},{96,64},{128,160},{160,128},{192,224},{224,1... | collective-permute-start | bytes 393224 | tf_op jit(solution)/shard_map/ppermute | solution.py:570
  89.1 1.3 %collective-permute-start.4 = (bf16[2,64,512]{2,1,0:T(8,128)(2,1)S(1)}, bf16[2,64,512]{2,1,0:T(8,128)(2,1)S(1)}, u32[]{:S(2)}, u32[]{:S(2)}) collective-permute-start(bf16[2,64,512]{2,1,0:T(8,128)(2,1)S(1)} %get-tuple-element.44), channel_id=1, source_target_pairs={{0,64},{32,96},{64,128},{96,160},{128,192},{160,224},{192,0},{224,... | collective-permute-start | bytes 393224 | tf_op jit(solution)/shard_map/ppermute | solution.py:570
  90.4 1.5 %collective-permute-start.5 = (bf16[2,64,512]{2,1,0:T(8,128)(2,1)S(1)}, bf16[2,64,512]{2,1,0:T(8,128)(2,1)S(1)}, u32[]{:S(2)}, u32[]{:S(2)}) collective-permute-start(bf16[2,64,512]{2,1,0:T(8,128)(2,1)S(1)} %get-tuple-element.45), channel_id=1, source_target_pairs={{0,96},{32,64},{64,160},{96,128},{128,224},{160,192},{192,32},{224... | collective-permute-start | bytes 393224 | tf_op jit(solution)/shard_map/ppermute | solution.py:570
  91.9 1.3 collective-permute-start.6
  93.2 2.0 %collective-permute-start.7 = (bf16[2,64,512]{2,1,0:T(8,128)(2,1)S(1)}, bf16[2,64,512]{2,1,0:T(8,128)(2,1)S(1)}, u32[]{:S(2)}, u32[]{:S(2)}) collective-permute-start(bf16[2,64,512]{2,1,0:T(8,128)(2,1)S(1)} %get-tuple-element.47), channel_id=1, source_target_pairs={{0,160},{32,128},{64,224},{96,192},{128,32},{160,0},{192,96},{224,... | collective-permute-start | bytes 393224 | tf_op jit(solution)/shard_map/ppermute | solution.py:570
  95.3 0.0 collective-permute-done.3.refs_1_
  95.3 1.4 %collective-permute-start.8 = (bf16[2,64,512]{2,1,0:T(8,128)(2,1)S(1)}, bf16[2,64,512]{2,1,0:T(8,128)(2,1)S(1)}, u32[]{:S(2)}, u32[]{:S(2)}) collective-permute-start(bf16[2,64,512]{2,1,0:T(8,128)(2,1)S(1)} %get-tuple-element.48), channel_id=1, source_target_pairs={{0,192},{32,224},{64,0},{96,32},{128,64},{160,96},{192,128},{224,1... | collective-permute-start | bytes 393224 | tf_op jit(solution)/shard_map/ppermute | solution.py:570
  96.6 0.0 collective-permute-done.4.refs_2_
  96.6 1.5 %collective-permute-start.9 = (bf16[2,64,512]{2,1,0:T(8,128)(2,1)S(1)}, bf16[2,64,512]{2,1,0:T(8,128)(2,1)S(1)}, u32[]{:S(2)}, u32[]{:S(2)}) collective-permute-start(bf16[2,64,512]{2,1,0:T(8,128)(2,1)S(1)} %get-tuple-element.49), channel_id=1, source_target_pairs={{0,224},{32,192},{64,32},{96,0},{128,96},{160,64},{192,160},{224,1... | collective-permute-start | bytes 393224 | tf_op jit(solution)/shard_map/ppermute | solution.py:570
  98.1 0.6 collective-permute-done.5.refs_3_
  98.7 3.5 %collective-permute-done.6.refs_4_ = bf16[2,64,512]{2,1,0:T(8,128)(2,1)S(1)} collective-permute-done((bf16[2,64,512]{2,1,0:T(8,128)(2,1)S(1)}, bf16[2,64,512]{2,1,0:T(8,128)(2,1)S(1)}, u32[]{:S(2)}, u32[]{:S(2)}) %collective-permute-start.6) | collective-permute-done | bytes 131104 | tf_op jit(solution)/shard_map/ppermute | solution.py:570
  102.2 3.0 %collective-permute-done.7.refs_5_ = bf16[2,64,512]{2,1,0:T(8,128)(2,1)S(1)} collective-permute-done((bf16[2,64,512]{2,1,0:T(8,128)(2,1)S(1)}, bf16[2,64,512]{2,1,0:T(8,128)(2,1)S(1)}, u32[]{:S(2)}, u32[]{:S(2)}) %collective-permute-start.7) | collective-permute-done | bytes 131104 | tf_op jit(solution)/shard_map/ppermute | solution.py:570
  105.2 0.0 collective-permute-done.8.refs_6_
  105.2 0.9 collective-permute-done.9.refs_7_
  106.1 0.0 all-to-all-done.3
  106.1 1.4 %pick_stacked.1 = bf16[8,2,64,512]{3,2,1,0:T(8,128)(2,1)} custom-call(s32[8]{0:T(128)S(1)} %get-tuple-element.63.index_ref, bf16[4,2,64,512]{3,2,1,0:T(8,128)(2,1)S(1)} %bitcast.6), custom_call_target="tpu_custom_call" | custom-call | tf_op jit(solution)/shard_map/pick_stacked/pallas_call | solution.py:407
  107.6 4.5 %all-to-all-start.4 = ((bf16[8,2,64,512]{3,2,1,0:T(8,128)(2,1)}), bf16[8,2,64,512]{3,2,1,0:T(8,128)(2,1)S(1)}, u32[]{:S(2)}, u32[]{:S(2)}) async-start(bf16[8,2,64,512]{3,2,1,0:T(8,128)(2,1)} %pick_stacked.1), calls=%async_computation.4 | async-start | bytes 2097152 | tf_op jit(solution)/shard_map/all_to_all | solution.py:484
  112.1 0.2 select_reduce_fusion.3.index_ref
  112.3 0.2 select_reduce_fusion.2.index_ref
  112.5 1.4 %place_q.1 = bf16[4,64,1024]{2,1,0:T(8,128)(2,1)} custom-call(s32[4]{0:T(128)S(1)} %select_reduce_fusion.2.index_ref, bf16[2,64,512]{2,1,0:T(8,128)(2,1)S(1)} %get-tuple-element.50.refs_0_, bf16[2,64,512]{2,1,0:T(8,128)(2,1)S(1)} %collective-permute-done.3.refs_1_, bf16[2,64,512]{2,1,0:T(8,128)(2,1)S(1)} %collective-permute-done.4.refs_2_, ...), custom_call_target="tpu_custom_call" | custom-call | tf_op jit(solution)/shard_map/place_q/pallas_call | solution.py:443
  113.9 13.3 %all-to-all-done.4.in_ref = bf16[8,2,64,512]{3,2,1,0:T(8,128)(2,1)S(1)} async-done(((bf16[8,2,64,512]{3,2,1,0:T(8,128)(2,1)}), bf16[8,2,64,512]{3,2,1,0:T(8,128)(2,1)S(1)}, u32[]{:S(2)}, u32[]{:S(2)}) %all-to-all-start.4) | async-done | bytes 1048608 | tf_op jit(solution)/shard_map/all_to_all | solution.py:484
  127.2 1.5 %place_kv.1 = (bf16[4,64,512]{2,1,0:T(8,128)(2,1)}, bf16[4,64,512]{2,1,0:T(8,128)(2,1)}) custom-call(s32[4]{0:T(128)S(1)} %select_reduce_fusion.3.index_ref, bf16[8,2,64,512]{3,2,1,0:T(8,128)(2,1)S(1)} %all-to-all-done.4.in_ref), custom_call_target="tpu_custom_call" | custom-call | tf_op jit(solution)/shard_map/place_kv/pallas_call | solution.py:472
  (7 shorter events, 0.1 us)
Async XLA Ops:
  3.0 17.1 %collective-permute-start.1 = (bf16[4,64,1792]{2,1,0:T(8,128)(2,1)S(1)}, bf16[4,64,1792]{2,1,0:T(8,128)(2,1)S(1)}, u32[]{:S(2)}, u32[]{:S(2)}) collective-permute-start(bf16[4,64,1792]{2,1,0:T(8,128)(2,1)S(1)} %get-tuple-element.33.x_ref), channel_id=1, source_target_pairs={{0,1},{1,0},{2,3},{3,2},{4,5},{5,4},{6,7},{7,6},{8,9},{9,8},{10,11... | collective-permute-start | bytes 2752520 | tf_op jit(solution)/shard_map/ppermute | solution.py:507
  5.2 18.5 %all-to-all-start = ((bf16[8,16,2176]{2,1,0:T(8,128)(2,1)}), bf16[8,16,2176]{2,1,0:T(8,128)(2,1)S(1)}, u32[]{:S(2)}, u32[]{:S(2)}) async-start(bf16[8,16,2176]{2,1,0:T(8,128)(2,1)} %get-tuple-element.32), calls=%async_computation | async-start | bytes 1114112 | tf_op jit(solution)/shard_map/all_to_all | solution.py:484
  13.4 6.7 %copy-start = (bf16[4,64,1024]{2,1,0:T(8,128)(2,1)S(1)}, bf16[4,64,1024]{2,1,0:T(8,128)(2,1)}, u32[]{:S(2)}) copy-start(bf16[4,64,1024]{2,1,0:T(8,128)(2,1)} %q_ref.1) | copy-start | bytes 1572868
  22.2 45.1 %copy-start.1 = (s32[32]{0:T(128)S(1)}, s32[32]{0:T(128)}, u32[]{:S(2)}) copy-start(s32[32]{0:T(128)} %param.13) | copy-start | bytes 388
  23.7 33.6 %all-to-all-start.1 = ((bf16[8,64,1024]{2,1,0:T(8,128)(2,1)}), bf16[8,64,1024]{2,1,0:T(8,128)(2,1)S(1)}, u32[]{:S(2)}, u32[]{:S(2)}) async-start(bf16[8,64,1024]{2,1,0:T(8,128)(2,1)} %bitcast.7), calls=%async_computation.1 | async-start | bytes 2097152 | tf_op jit(solution)/shard_map/all_to_all | solution.py:484
  31.8 9.9 %collective-permute-start = (bf16[8,16,2176]{2,1,0:T(8,128)(2,1)S(1)}, bf16[8,16,2176]{2,1,0:T(8,128)(2,1)S(1)}, u32[]{:S(2)}, u32[]{:S(2)}) collective-permute-start(bf16[8,16,2176]{2,1,0:T(8,128)(2,1)S(1)} %all-to-all-done.own_ref), channel_id=1, source_target_pairs={{0,2},{2,0},{4,6},{6,4},{8,10},{10,8},{12,14},{14,12},{16,18},{18,... | collective-permute-start | bytes 1671176 | tf_op jit(solution)/shard_map/ppermute | solution.py:509
  61.0 17.5 %all-to-all-start.2 = ((bf16[8,64,512]{2,1,0:T(8,128)(2,1)}), bf16[8,64,512]{2,1,0:T(8,128)(2,1)S(1)}, u32[]{:S(2)}, u32[]{:S(2)}) async-start(bf16[8,64,512]{2,1,0:T(8,128)(2,1)} %get-tuple-element.39), calls=%async_computation.2 | async-start | bytes 1048576 | tf_op jit(solution)/shard_map/all_to_all | solution.py:484
  64.5 12.6 %collective-permute-start.2 = (bf16[8,64,512]{2,1,0:T(8,128)(2,1)S(1)}, bf16[8,64,512]{2,1,0:T(8,128)(2,1)S(1)}, u32[]{:S(2)}, u32[]{:S(2)}) collective-permute-start(bf16[8,64,512]{2,1,0:T(8,128)(2,1)S(1)} %get-tuple-element.38), channel_id=1, source_target_pairs={{0,2},{2,0},{4,6},{6,4},{8,10},{10,8},{12,14},{14,12},{16,18},{18,... | collective-permute-start | bytes 1572872 | tf_op jit(solution)/shard_map/ppermute | solution.py:557
  78.5 27.7 %all-to-all-start.3 = ((bf16[8,64,512]{2,1,0:T(8,128)(2,1)}), bf16[8,64,512]{2,1,0:T(8,128)(2,1)S(1)}, u32[]{:S(2)}, u32[]{:S(2)}) async-start(bf16[8,64,512]{2,1,0:T(8,128)(2,1)} %add_convert_fusion), calls=%async_computation.3 | async-start | bytes 1048576 | tf_op jit(solution)/shard_map/all_to_all | solution.py:484
  85.0 10.3 %collective-permute-start.3 = (bf16[2,64,512]{2,1,0:T(8,128)(2,1)S(1)}, bf16[2,64,512]{2,1,0:T(8,128)(2,1)S(1)}, u32[]{:S(2)}, u32[]{:S(2)}) collective-permute-start(bf16[2,64,512]{2,1,0:T(8,128)(2,1)S(1)} %get-tuple-element.43), channel_id=1, source_target_pairs={{0,32},{32,0},{64,96},{96,64},{128,160},{160,128},{192,224},{224,1... | collective-permute-start | bytes 393224 | tf_op jit(solution)/shard_map/ppermute | solution.py:570
  89.1 7.5 %collective-permute-start.4 = (bf16[2,64,512]{2,1,0:T(8,128)(2,1)S(1)}, bf16[2,64,512]{2,1,0:T(8,128)(2,1)S(1)}, u32[]{:S(2)}, u32[]{:S(2)}) collective-permute-start(bf16[2,64,512]{2,1,0:T(8,128)(2,1)S(1)} %get-tuple-element.44), channel_id=1, source_target_pairs={{0,64},{32,96},{64,128},{96,160},{128,192},{160,224},{192,0},{224,... | collective-permute-start | bytes 393224 | tf_op jit(solution)/shard_map/ppermute | solution.py:570
  90.4 8.3 %collective-permute-start.5 = (bf16[2,64,512]{2,1,0:T(8,128)(2,1)S(1)}, bf16[2,64,512]{2,1,0:T(8,128)(2,1)S(1)}, u32[]{:S(2)}, u32[]{:S(2)}) collective-permute-start(bf16[2,64,512]{2,1,0:T(8,128)(2,1)S(1)} %get-tuple-element.45), channel_id=1, source_target_pairs={{0,96},{32,64},{64,160},{96,128},{128,224},{160,192},{192,32},{224... | collective-permute-start | bytes 393224 | tf_op jit(solution)/shard_map/ppermute | solution.py:570
  91.9 10.3 %collective-permute-start.6 = (bf16[2,64,512]{2,1,0:T(8,128)(2,1)S(1)}, bf16[2,64,512]{2,1,0:T(8,128)(2,1)S(1)}, u32[]{:S(2)}, u32[]{:S(2)}) collective-permute-start(bf16[2,64,512]{2,1,0:T(8,128)(2,1)S(1)} %get-tuple-element.46), channel_id=1, source_target_pairs={{0,128},{32,160},{64,192},{96,224},{128,0},{160,32},{192,64},{224,... | collective-permute-start | bytes 393224 | tf_op jit(solution)/shard_map/ppermute | solution.py:570
  93.2 12.0 %collective-permute-start.7 = (bf16[2,64,512]{2,1,0:T(8,128)(2,1)S(1)}, bf16[2,64,512]{2,1,0:T(8,128)(2,1)S(1)}, u32[]{:S(2)}, u32[]{:S(2)}) collective-permute-start(bf16[2,64,512]{2,1,0:T(8,128)(2,1)S(1)} %get-tuple-element.47), channel_id=1, source_target_pairs={{0,160},{32,128},{64,224},{96,192},{128,32},{160,0},{192,96},{224,... | collective-permute-start | bytes 393224 | tf_op jit(solution)/shard_map/ppermute | solution.py:570
  95.3 10.0 %collective-permute-start.8 = (bf16[2,64,512]{2,1,0:T(8,128)(2,1)S(1)}, bf16[2,64,512]{2,1,0:T(8,128)(2,1)S(1)}, u32[]{:S(2)}, u32[]{:S(2)}) collective-permute-start(bf16[2,64,512]{2,1,0:T(8,128)(2,1)S(1)} %get-tuple-element.48), channel_id=1, source_target_pairs={{0,192},{32,224},{64,0},{96,32},{128,64},{160,96},{192,128},{224,1... | collective-permute-start | bytes 393224 | tf_op jit(solution)/shard_map/ppermute | solution.py:570
  96.6 9.5 %collective-permute-start.9 = (bf16[2,64,512]{2,1,0:T(8,128)(2,1)S(1)}, bf16[2,64,512]{2,1,0:T(8,128)(2,1)S(1)}, u32[]{:S(2)}, u32[]{:S(2)}) collective-permute-start(bf16[2,64,512]{2,1,0:T(8,128)(2,1)S(1)} %get-tuple-element.49), channel_id=1, source_target_pairs={{0,224},{32,192},{64,32},{96,0},{128,96},{160,64},{192,160},{224,1... | collective-permute-start | bytes 393224 | tf_op jit(solution)/shard_map/ppermute | solution.py:570
  107.6 19.6 %all-to-all-start.4 = ((bf16[8,2,64,512]{3,2,1,0:T(8,128)(2,1)}), bf16[8,2,64,512]{3,2,1,0:T(8,128)(2,1)S(1)}, u32[]{:S(2)}, u32[]{:S(2)}) async-start(bf16[8,2,64,512]{3,2,1,0:T(8,128)(2,1)} %pick_stacked.1), calls=%async_computation.4 | async-start | bytes 2097152 | tf_op jit(solution)/shard_map/all_to_all | solution.py:484

commit v6 on v5

--- a/solution.py
+++ b/solution.py
@@ -63,12 +63,15 @@
     out_ref,
     x_ref,
     part_ref,
+    turned_hbm,
     seg_ref,
     k_ref,
     v_ref,
     weight_ref,
+    turned_ref,
     sems,
     weight_sems,
+    turned_sems,
 ):
     rows, block, kv_width = k_ref.shape
     kv_heads = kv_width // HEAD
@@ -85,7 +88,21 @@
 
     @pl.when(on_core() == 0)
     def _():
-        own_half(lax.axis_index("tp"), x_ref, weight_hbm, part_ref, weight_ref, weight_sems)
+        tp = lax.axis_index("tp")
+        stores = []
+        for at in load_half(1 - tp, weight_hbm, weight_ref, weight_sems):
+            turned_ref[:, at] = weight_ref[at].T
+            stores.append(
+                pltpu.make_async_copy(
+                    turned_ref.at[:, at],
+                    turned_hbm.at[:, at],
+                    turned_sems.at[len(stores)],
+                )
+            )
+            stores[-1].start()
+        own_half(tp, x_ref, weight_hbm, part_ref, weight_ref, weight_sems)
+        for store in stores:
+            store.wait()
 
     copies[0].wait()
     place = lax.broadcasted_iota(jnp.int32, (TILE, block), 1)
@@ -126,18 +143,21 @@
     return pl.pallas_call(
         begin_kernel,
         in_specs=[ANY] * 5,
-        out_specs=[VMEM] * 3,
+        out_specs=[VMEM] * 3 + [ANY],
         out_shape=[
             pltpu.HBM((rows * kv_heads, TILE, lanes), BF16),
             jax.ShapeDtypeStruct(x.shape, BF16),
             jax.ShapeDtypeStruct((rows * block, width), F32),
+            pltpu.HBM((half, width), BF16),
         ],
         scratch_shapes=[
             pltpu.VMEM(seg.shape, jnp.int32),
             pltpu.VMEM(k.shape, BF16),
             pltpu.VMEM(v.shape, BF16),
             pltpu.VMEM((width, half), BF16),
+            pltpu.VMEM((half, width), BF16),
             pltpu.SemaphoreType.DMA((4,)),
+            pltpu.SemaphoreType.DMA((width // HEAD,)),
             pltpu.SemaphoreType.DMA((width // HEAD,)),
         ],
         compiler_params=pltpu.CompilerParams(vmem_limit_bytes=MEDIUM_VMEM),
@@ -146,22 +166,27 @@
 
 
 def project_own_kernel(
-    x_ref, weight_hbm, part_ref, turned_ref, weight_ref, sems
+    x_ref, weight_hbm, turned_hbm, part_ref, turned_ref, weight_ref, sems
 ):
-    for at in load_half(1 - lax.axis_index("tp"), weight_hbm, weight_ref, sems):
-        turned_ref[:, at] = weight_ref[at].T
+    tp = lax.axis_index("tp")
+
+    @pl.when(on_core() == 0)
+    def _():
+        run_copies([pltpu.make_async_copy(turned_hbm, turned_ref, sems.at[0])])
 
     @pl.when(on_core() != 0)
     def _():
-        own_half(lax.axis_index("tp"), x_ref, weight_hbm, part_ref, weight_ref, sems)
-
-
-def project_own(x, weight):
+        for at in load_half(1 - tp, weight_hbm, weight_ref, sems):
+            turned_ref[:, at] = weight_ref[at].T
+        own_half(tp, x_ref, weight_hbm, part_ref, weight_ref, sems)
+
+
+def project_own(x, weight, turned):
     rows, block, half = x.shape
     width = weight.shape[0]
     return pl.pallas_call(
         project_own_kernel,
-        in_specs=[VMEM, ANY],
+        in_specs=[VMEM, ANY, ANY],
         out_specs=[VMEM, VMEM],
         out_shape=[
             jax.ShapeDtypeStruct((rows * block, width), F32),
@@ -178,7 +203,7 @@
             transcendentals=0,
         ),
         name="project_own",
-    )(x, *in_hbm(weight))
+    )(x, *in_hbm(weight, turned))
 
 
 def other_half_kernel(x_ref, q_ref, part_0, part_1, turned_ref, out_ref):
@@ -501,7 +526,7 @@
     columns = [[z * pair + h for z in ORDER] for h in range(pair)]
     swap = [(z * pair + h, z * pair + 1 - h) for z in range(units) for h in range(pair)]
 
-    own, grad, part_0 = begin(
+    own, grad, part_0, turned = begin(
         segment_ids, key_states, value_state_rows, output_grad, out_weight
     )
     other_grad = lax.ppermute(grad, "tp", [(0, 1), (1, 0)])
@@ -545,7 +570,7 @@
     send_index = row_for(steps)
     send_step = row_for(partner(group, steps, 1))
 
-    part_1, turned = project_own(grad, out_weight)
+    part_1, turned = project_own(grad, out_weight, turned)
     q_and_grad = project_other(
         other_grad, queries, part_0, part_1, turned, kv_heads
     )

time: 129 us -> 126 us (0.977)
  waiting for transfers between devices: 56.2 us -> 54.3 us
  starting transfers between devices: 50.8 us -> 49.2 us
    all_to_all x5, starting transfers between devices: 30.1 us -> 27.7 us  [exchange(): lax.all_to_all(x, axis, split_axis=0, concat_axis=0, tiled=True, axis_ind...]
  transfers between devices with their start and end apart: 15 -> 15, of which waited for: 11 -> 10; matrix products, arithmetic and copies ran while one was open for 1% -> 1% of each run, Pallas kernels for 8% -> 8%
where the time goes in v6:
time: 126 us; the launch traced here: 125 us
  waiting for transfers between devices  54.3 us (43%)
  starting transfers between devices  49.2 us (39%)
  Pallas kernels  19.4 us (15%)
  other arithmetic  1.45 us (1%)
    all_to_all x5, waiting for transfers between devices, exchange(): lax.all_to_all(x, axis, split_axis=0, concat_axis=0, tiled=True, axis_ind...  30.3 us
    all_to_all x5, starting transfers between devices, exchange(): lax.all_to_all(x, axis, split_axis=0, concat_axis=0, tiled=True, axis_ind...  27.7 us
    ppermute x7, starting transfers between devices, on_device(): got.append(lax.ppermute(sent[i], 'dp', route))  13.7 us
    ppermute x1, waiting for transfers between devices, on_device(): dkv_back = lax.ppermute(dkv_theirs, 'ctx', swap)  8.83 us
    ppermute x7, waiting for transfers between devices, on_device(): got.append(lax.ppermute(sent[i], 'dp', route))  8.02 us
    ppermute x1, waiting for transfers between devices, on_device(): other = lax.ppermute(own, 'ctx', swap)  7.14 us
    pallas_call x1, Pallas kernels, project_own(): pl.pallas_call(project_own_kernel, in_specs=[VMEM, ANY, ANY], out_specs=[...  6.25 us
    pallas_call x1, Pallas kernels, attention(): pl.pallas_call(attention_kernel, in_specs=[VMEM] * 3, out_specs=[ANY, VME...  3.67 us
  transfers between devices with their start and end apart: 15, of which 10 were waited for; matrix products, arithmetic and copies ran while one was open for 1% of the time, Pallas kernels for 8%

profile of v6, /device:TPU:1, one launch (start us, length us, event | category | flops | bytes accessed | tf_op | source)
XLA Modules:
  0.0 125.3 jit_solution(15672828085875008487)
XLA Ops:
  0.6 2.4 %begin.1 = (bf16[8,16,2176]{2,1,0:T(8,128)(2,1)}, bf16[4,64,1792]{2,1,0:T(8,128)(2,1)S(1)}, f32[256,1024]{1,0:T(8,128)S(1)}, bf16[1792,1024]{1,0:T(8,128)(2,1)}) custom-call(s32[4,64]{1,0:T(4,128)} %seg_hbm.1, bf16[4,64,512]{2,1,0:T(8,128)(2,1)} %k_hbm.1, bf16[4,64,512]{2,1,0:T(8,128)(2,1)} %v_hbm.1, bf16[4,64,1792]{2,1,0:T(8,128)(2,1)} %x_hbm.1, ...), custom_call_target="tpu_custom_call" | custom-call | tf_op jit(solution)/shard_map/begin/pallas_call | solution.py:143
  3.1 2.1 %collective-permute-start.1 = (bf16[4,64,1792]{2,1,0:T(8,128)(2,1)S(1)}, bf16[4,64,1792]{2,1,0:T(8,128)(2,1)S(1)}, u32[]{:S(2)}, u32[]{:S(2)}) collective-permute-start(bf16[4,64,1792]{2,1,0:T(8,128)(2,1)S(1)} %get-tuple-element.34.x_ref), channel_id=1, source_target_pairs={{0,1},{1,0},{2,3},{3,2},{4,5},{5,4},{6,7},{7,6},{8,9},{9,8},{10,11... | collective-permute-start | bytes 2752520 | tf_op jit(solution)/shard_map/ppermute | solution.py:532
  5.2 8.2 %all-to-all-start = ((bf16[8,16,2176]{2,1,0:T(8,128)(2,1)}), bf16[8,16,2176]{2,1,0:T(8,128)(2,1)S(1)}, u32[]{:S(2)}, u32[]{:S(2)}) async-start(bf16[8,16,2176]{2,1,0:T(8,128)(2,1)} %get-tuple-element.33), calls=%async_computation | async-start | bytes 1114112 | tf_op jit(solution)/shard_map/all_to_all | solution.py:509
  13.4 0.0 copy-start
  13.4 6.2 %project_own.1 = (f32[256,1024]{1,0:T(8,128)S(1)}, bf16[1792,1024]{1,0:T(8,128)(2,1)S(1)}) custom-call(bf16[4,64,1792]{2,1,0:T(8,128)(2,1)S(1)} %get-tuple-element.34.x_ref, bf16[1024,3584]{1,0:T(8,128)(2,1)} %weight_hbm.3, bf16[1792,1024]{1,0:T(8,128)(2,1)} %get-tuple-element.36.turned_hbm), custom_call_target="tpu_custom_call" | custom-call | flops 939524096 | bytes 7340032 | tf_op jit(solution)/shard_map/project_own/pallas_call | solution.py:187
  19.6 0.0 collective-permute-done.1.x_ref
  19.6 0.0 copy-done
  19.7 2.1 %project_other.1 = bf16[4,2,64,1024]{3,2,1,0:T(8,128)(2,1)} custom-call(bf16[4,64,1792]{2,1,0:T(8,128)(2,1)S(1)} %collective-permute-done.1.x_ref, bf16[4,64,1024]{2,1,0:T(8,128)(2,1)S(1)} %copy-done, f32[256,1024]{1,0:T(8,128)S(1)} %get-tuple-element.35.part_0, f32[256,1024]{1,0:T(8,128)S(1)} %get-tuple-element.37.part_1, ...), custom_call_target="tpu_custom_call" | custom-call | flops 939524096 | bytes 3670016 | tf_op jit(solution)/shard_map/project_other/pallas_call | solution.py:225
  21.8 1.4 %all-to-all-done.own_ref = bf16[8,16,2176]{2,1,0:T(8,128)(2,1)S(1)} async-done(((bf16[8,16,2176]{2,1,0:T(8,128)(2,1)}), bf16[8,16,2176]{2,1,0:T(8,128)(2,1)S(1)}, u32[]{:S(2)}, u32[]{:S(2)}) %all-to-all-start) | async-done | bytes 557088 | tf_op jit(solution)/shard_map/all_to_all | solution.py:509
  23.2 5.7 %all-to-all-start.1 = ((bf16[8,64,1024]{2,1,0:T(8,128)(2,1)}), bf16[8,64,1024]{2,1,0:T(8,128)(2,1)S(1)}, u32[]{:S(2)}, u32[]{:S(2)}) async-start(bf16[8,64,1024]{2,1,0:T(8,128)(2,1)} %bitcast.7), calls=%async_computation.1 | async-start | bytes 2097152 | tf_op jit(solution)/shard_map/all_to_all | solution.py:509
  28.9 0.0 copy-start.1
  28.9 2.8 %collective-permute-start = (bf16[8,16,2176]{2,1,0:T(8,128)(2,1)S(1)}, bf16[8,16,2176]{2,1,0:T(8,128)(2,1)S(1)}, u32[]{:S(2)}, u32[]{:S(2)}) collective-permute-start(bf16[8,16,2176]{2,1,0:T(8,128)(2,1)S(1)} %all-to-all-done.own_ref), channel_id=1, source_target_pairs={{0,2},{2,0},{4,6},{6,4},{8,10},{10,8},{12,14},{14,12},{16,18},{18,... | collective-permute-start | bytes 1671176 | tf_op jit(solution)/shard_map/ppermute | solution.py:534
  31.7 7.1 %collective-permute-done.other_ref = bf16[8,16,2176]{2,1,0:T(8,128)(2,1)S(1)} collective-permute-done((bf16[8,16,2176]{2,1,0:T(8,128)(2,1)S(1)}, bf16[8,16,2176]{2,1,0:T(8,128)(2,1)S(1)}, u32[]{:S(2)}, u32[]{:S(2)}) %collective-permute-start) | collective-permute-done | bytes 557088 | tf_op jit(solution)/shard_map/ppermute | solution.py:534
  38.8 14.3 %all-to-all-done.1.qd_ref = bf16[8,64,1024]{2,1,0:T(8,128)(2,1)S(1)} async-done(((bf16[8,64,1024]{2,1,0:T(8,128)(2,1)}), bf16[8,64,1024]{2,1,0:T(8,128)(2,1)S(1)}, u32[]{:S(2)}, u32[]{:S(2)}) %all-to-all-start.1) | async-done | bytes 1048608 | tf_op jit(solution)/shard_map/all_to_all | solution.py:509
  53.2 3.7 %attend.1 = (bf16[8,64,512]{2,1,0:T(8,128)(2,1)}, bf16[8,64,512]{2,1,0:T(8,128)(2,1)S(1)}, bf16[8,64,512]{2,1,0:T(8,128)(2,1)S(1)}) custom-call(bf16[8,16,2176]{2,1,0:T(8,128)(2,1)S(1)} %all-to-all-done.own_ref, bf16[8,16,2176]{2,1,0:T(8,128)(2,1)S(1)} %collective-permute-done.other_ref, bf16[8,64,1024]{2,1,0:T(8,128)(2,1)S(1)} %all-to-all-done.1.qd_ref), custom_call_target="tpu_custom_call" | custom-call | flops 3000000000 | bytes 6291456 | tf_op jit(solution)/shard_map/attend/pallas_call | solution.py:365
  56.8 4.1 %all-to-all-start.2 = ((bf16[8,64,512]{2,1,0:T(8,128)(2,1)}), bf16[8,64,512]{2,1,0:T(8,128)(2,1)S(1)}, u32[]{:S(2)}, u32[]{:S(2)}) async-start(bf16[8,64,512]{2,1,0:T(8,128)(2,1)} %get-tuple-element.41), calls=%async_computation.2 | async-start | bytes 1048576 | tf_op jit(solution)/shard_map/all_to_all | solution.py:509
  61.0 2.9 %collective-permute-start.2 = (bf16[8,64,512]{2,1,0:T(8,128)(2,1)S(1)}, bf16[8,64,512]{2,1,0:T(8,128)(2,1)S(1)}, u32[]{:S(2)}, u32[]{:S(2)}) collective-permute-start(bf16[8,64,512]{2,1,0:T(8,128)(2,1)S(1)} %get-tuple-element.40), channel_id=1, source_target_pairs={{0,2},{2,0},{4,6},{6,4},{8,10},{10,8},{12,14},{14,12},{16,18},{18,... | collective-permute-start | bytes 1572872 | tf_op jit(solution)/shard_map/ppermute | solution.py:582
  63.9 0.0 copy-done.1
  63.9 0.1 reshape.149
  64.0 8.8 %collective-permute-done.2 = bf16[8,64,512]{2,1,0:T(8,128)(2,1)S(1)} collective-permute-done((bf16[8,64,512]{2,1,0:T(8,128)(2,1)S(1)}, bf16[8,64,512]{2,1,0:T(8,128)(2,1)S(1)}, u32[]{:S(2)}, u32[]{:S(2)}) %collective-permute-start.2) | collective-permute-done | bytes 524320 | tf_op jit(solution)/shard_map/ppermute | solution.py:582
  72.8 0.9 add_convert_fusion
  73.7 1.3 all-to-all-done.2
  75.0 5.1 %all-to-all-start.3 = ((bf16[8,64,512]{2,1,0:T(8,128)(2,1)}), bf16[8,64,512]{2,1,0:T(8,128)(2,1)S(1)}, u32[]{:S(2)}, u32[]{:S(2)}) async-start(bf16[8,64,512]{2,1,0:T(8,128)(2,1)} %add_convert_fusion), calls=%async_computation.3 | async-start | bytes 1048576 | tf_op jit(solution)/shard_map/all_to_all | solution.py:509
  80.1 0.1 select_reduce_fusion
  80.2 0.6 pick.1
  80.9 4.7 %collective-permute-start.3 = (bf16[2,64,512]{2,1,0:T(8,128)(2,1)S(1)}, bf16[2,64,512]{2,1,0:T(8,128)(2,1)S(1)}, u32[]{:S(2)}, u32[]{:S(2)}) collective-permute-start(bf16[2,64,512]{2,1,0:T(8,128)(2,1)S(1)} %get-tuple-element.45), channel_id=1, source_target_pairs={{0,32},{32,0},{64,96},{96,64},{128,160},{160,128},{192,224},{224,1... | collective-permute-start | bytes 393224 | tf_op jit(solution)/shard_map/ppermute | solution.py:595
  85.6 1.3 %collective-permute-start.4 = (bf16[2,64,512]{2,1,0:T(8,128)(2,1)S(1)}, bf16[2,64,512]{2,1,0:T(8,128)(2,1)S(1)}, u32[]{:S(2)}, u32[]{:S(2)}) collective-permute-start(bf16[2,64,512]{2,1,0:T(8,128)(2,1)S(1)} %get-tuple-element.46), channel_id=1, source_target_pairs={{0,64},{32,96},{64,128},{96,160},{128,192},{160,224},{192,0},{224,... | collective-permute-start | bytes 393224 | tf_op jit(solution)/shard_map/ppermute | solution.py:595
  86.9 1.5 %collective-permute-start.5 = (bf16[2,64,512]{2,1,0:T(8,128)(2,1)S(1)}, bf16[2,64,512]{2,1,0:T(8,128)(2,1)S(1)}, u32[]{:S(2)}, u32[]{:S(2)}) collective-permute-start(bf16[2,64,512]{2,1,0:T(8,128)(2,1)S(1)} %get-tuple-element.47), channel_id=1, source_target_pairs={{0,96},{32,64},{64,160},{96,128},{128,224},{160,192},{192,32},{224... | collective-permute-start | bytes 393224 | tf_op jit(solution)/shard_map/ppermute | solution.py:595
  88.4 1.3 %collective-permute-start.6 = (bf16[2,64,512]{2,1,0:T(8,128)(2,1)S(1)}, bf16[2,64,512]{2,1,0:T(8,128)(2,1)S(1)}, u32[]{:S(2)}, u32[]{:S(2)}) collective-permute-start(bf16[2,64,512]{2,1,0:T(8,128)(2,1)S(1)} %get-tuple-element.48), channel_id=1, source_target_pairs={{0,128},{32,160},{64,192},{96,224},{128,0},{160,32},{192,64},{224,... | collective-permute-start | bytes 393224 | tf_op jit(solution)/shard_map/ppermute | solution.py:595
  89.7 2.0 %collective-permute-start.7 = (bf16[2,64,512]{2,1,0:T(8,128)(2,1)S(1)}, bf16[2,64,512]{2,1,0:T(8,128)(2,1)S(1)}, u32[]{:S(2)}, u32[]{:S(2)}) collective-permute-start(bf16[2,64,512]{2,1,0:T(8,128)(2,1)S(1)} %get-tuple-element.49), channel_id=1, source_target_pairs={{0,160},{32,128},{64,224},{96,192},{128,32},{160,0},{192,96},{224,... | collective-permute-start | bytes 393224 | tf_op jit(solution)/shard_map/ppermute | solution.py:595
  91.7 0.0 collective-permute-done.3.refs_1_
  91.7 1.4 %collective-permute-start.8 = (bf16[2,64,512]{2,1,0:T(8,128)(2,1)S(1)}, bf16[2,64,512]{2,1,0:T(8,128)(2,1)S(1)}, u32[]{:S(2)}, u32[]{:S(2)}) collective-permute-start(bf16[2,64,512]{2,1,0:T(8,128)(2,1)S(1)} %get-tuple-element.50), channel_id=1, source_target_pairs={{0,192},{32,224},{64,0},{96,32},{128,64},{160,96},{192,128},{224,1... | collective-permute-start | bytes 393224 | tf_op jit(solution)/shard_map/ppermute | solution.py:595
  93.1 0.0 collective-permute-done.4.refs_2_
  93.1 1.5 %collective-permute-start.9 = (bf16[2,64,512]{2,1,0:T(8,128)(2,1)S(1)}, bf16[2,64,512]{2,1,0:T(8,128)(2,1)S(1)}, u32[]{:S(2)}, u32[]{:S(2)}) collective-permute-start(bf16[2,64,512]{2,1,0:T(8,128)(2,1)S(1)} %get-tuple-element.51), channel_id=1, source_target_pairs={{0,224},{32,192},{64,32},{96,0},{128,96},{160,64},{192,160},{224,1... | collective-permute-start | bytes 393224 | tf_op jit(solution)/shard_map/ppermute | solution.py:595
  94.6 0.6 collective-permute-done.5.refs_3_
  95.2 3.5 %collective-permute-done.6.refs_4_ = bf16[2,64,512]{2,1,0:T(8,128)(2,1)S(1)} collective-permute-done((bf16[2,64,512]{2,1,0:T(8,128)(2,1)S(1)}, bf16[2,64,512]{2,1,0:T(8,128)(2,1)S(1)}, u32[]{:S(2)}, u32[]{:S(2)}) %collective-permute-start.6) | collective-permute-done | bytes 131104 | tf_op jit(solution)/shard_map/ppermute | solution.py:595
  98.7 3.0 %collective-permute-done.7.refs_5_ = bf16[2,64,512]{2,1,0:T(8,128)(2,1)S(1)} collective-permute-done((bf16[2,64,512]{2,1,0:T(8,128)(2,1)S(1)}, bf16[2,64,512]{2,1,0:T(8,128)(2,1)S(1)}, u32[]{:S(2)}, u32[]{:S(2)}) %collective-permute-start.7) | collective-permute-done | bytes 131104 | tf_op jit(solution)/shard_map/ppermute | solution.py:595
  101.7 0.0 collective-permute-done.8.refs_6_
  101.7 0.9 collective-permute-done.9.refs_7_
  102.6 0.0 all-to-all-done.3
  102.6 1.4 %pick_stacked.1 = bf16[8,2,64,512]{3,2,1,0:T(8,128)(2,1)} custom-call(s32[8]{0:T(128)S(1)} %get-tuple-element.65.index_ref, bf16[4,2,64,512]{3,2,1,0:T(8,128)(2,1)S(1)} %bitcast.6), custom_call_target="tpu_custom_call" | custom-call | tf_op jit(solution)/shard_map/pick_stacked/pallas_call | solution.py:432
  104.0 4.5 %all-to-all-start.4 = ((bf16[8,2,64,512]{3,2,1,0:T(8,128)(2,1)}), bf16[8,2,64,512]{3,2,1,0:T(8,128)(2,1)S(1)}, u32[]{:S(2)}, u32[]{:S(2)}) async-start(bf16[8,2,64,512]{3,2,1,0:T(8,128)(2,1)} %pick_stacked.1), calls=%async_computation.4 | async-start | bytes 2097152 | tf_op jit(solution)/shard_map/all_to_all | solution.py:509
  108.6 0.2 select_reduce_fusion.3.index_ref
  108.8 0.2 select_reduce_fusion.2.index_ref
  109.0 1.4 %place_q.1 = bf16[4,64,1024]{2,1,0:T(8,128)(2,1)} custom-call(s32[4]{0:T(128)S(1)} %select_reduce_fusion.2.index_ref, bf16[2,64,512]{2,1,0:T(8,128)(2,1)S(1)} %get-tuple-element.52.refs_0_, bf16[2,64,512]{2,1,0:T(8,128)(2,1)S(1)} %collective-permute-done.3.refs_1_, bf16[2,64,512]{2,1,0:T(8,128)(2,1)S(1)} %collective-permute-done.4.refs_2_, ...), custom_call_target="tpu_custom_call" | custom-call | tf_op jit(solution)/shard_map/place_q/pallas_call | solution.py:468
  110.4 13.3 %all-to-all-done.4.in_ref = bf16[8,2,64,512]{3,2,1,0:T(8,128)(2,1)S(1)} async-done(((bf16[8,2,64,512]{3,2,1,0:T(8,128)(2,1)}), bf16[8,2,64,512]{3,2,1,0:T(8,128)(2,1)S(1)}, u32[]{:S(2)}, u32[]{:S(2)}) %all-to-all-start.4) | async-done | bytes 1048608 | tf_op jit(solution)/shard_map/all_to_all | solution.py:509
  123.7 1.5 %place_kv.1 = (bf16[4,64,512]{2,1,0:T(8,128)(2,1)}, bf16[4,64,512]{2,1,0:T(8,128)(2,1)}) custom-call(s32[4]{0:T(128)S(1)} %select_reduce_fusion.3.index_ref, bf16[8,2,64,512]{3,2,1,0:T(8,128)(2,1)S(1)} %all-to-all-done.4.in_ref), custom_call_target="tpu_custom_call" | custom-call | tf_op jit(solution)/shard_map/place_kv/pallas_call | solution.py:497
  (7 shorter events, 0.1 us)
Async XLA Ops:
  3.1 16.6 %collective-permute-start.1 = (bf16[4,64,1792]{2,1,0:T(8,128)(2,1)S(1)}, bf16[4,64,1792]{2,1,0:T(8,128)(2,1)S(1)}, u32[]{:S(2)}, u32[]{:S(2)}) collective-permute-start(bf16[4,64,1792]{2,1,0:T(8,128)(2,1)S(1)} %get-tuple-element.34.x_ref), channel_id=1, source_target_pairs={{0,1},{1,0},{2,3},{3,2},{4,5},{5,4},{6,7},{7,6},{8,9},{9,8},{10,11... | collective-permute-start | bytes 2752520 | tf_op jit(solution)/shard_map/ppermute | solution.py:532
  5.2 18.0 %all-to-all-start = ((bf16[8,16,2176]{2,1,0:T(8,128)(2,1)}), bf16[8,16,2176]{2,1,0:T(8,128)(2,1)S(1)}, u32[]{:S(2)}, u32[]{:S(2)}) async-start(bf16[8,16,2176]{2,1,0:T(8,128)(2,1)} %get-tuple-element.33), calls=%async_computation | async-start | bytes 1114112 | tf_op jit(solution)/shard_map/all_to_all | solution.py:509
  13.4 6.3 %copy-start = (bf16[4,64,1024]{2,1,0:T(8,128)(2,1)S(1)}, bf16[4,64,1024]{2,1,0:T(8,128)(2,1)}, u32[]{:S(2)}) copy-start(bf16[4,64,1024]{2,1,0:T(8,128)(2,1)} %q_ref.1) | copy-start | bytes 1572868
  23.2 30.0 %all-to-all-start.1 = ((bf16[8,64,1024]{2,1,0:T(8,128)(2,1)}), bf16[8,64,1024]{2,1,0:T(8,128)(2,1)S(1)}, u32[]{:S(2)}, u32[]{:S(2)}) async-start(bf16[8,64,1024]{2,1,0:T(8,128)(2,1)} %bitcast.7), calls=%async_computation.1 | async-start | bytes 2097152 | tf_op jit(solution)/shard_map/all_to_all | solution.py:509
  28.9 35.0 %copy-start.1 = (s32[32]{0:T(128)S(1)}, s32[32]{0:T(128)}, u32[]{:S(2)}) copy-start(s32[32]{0:T(128)} %param.13) | copy-start | bytes 388
  28.9 10.0 %collective-permute-start = (bf16[8,16,2176]{2,1,0:T(8,128)(2,1)S(1)}, bf16[8,16,2176]{2,1,0:T(8,128)(2,1)S(1)}, u32[]{:S(2)}, u32[]{:S(2)}) collective-permute-start(bf16[8,16,2176]{2,1,0:T(8,128)(2,1)S(1)} %all-to-all-done.own_ref), channel_id=1, source_target_pairs={{0,2},{2,0},{4,6},{6,4},{8,10},{10,8},{12,14},{14,12},{16,18},{18,... | collective-permute-start | bytes 1671176 | tf_op jit(solution)/shard_map/ppermute | solution.py:534
  56.8 18.1 %all-to-all-start.2 = ((bf16[8,64,512]{2,1,0:T(8,128)(2,1)}), bf16[8,64,512]{2,1,0:T(8,128)(2,1)S(1)}, u32[]{:S(2)}, u32[]{:S(2)}) async-start(bf16[8,64,512]{2,1,0:T(8,128)(2,1)} %get-tuple-element.41), calls=%async_computation.2 | async-start | bytes 1048576 | tf_op jit(solution)/shard_map/all_to_all | solution.py:509
  61.0 11.8 %collective-permute-start.2 = (bf16[8,64,512]{2,1,0:T(8,128)(2,1)S(1)}, bf16[8,64,512]{2,1,0:T(8,128)(2,1)S(1)}, u32[]{:S(2)}, u32[]{:S(2)}) collective-permute-start(bf16[8,64,512]{2,1,0:T(8,128)(2,1)S(1)} %get-tuple-element.40), channel_id=1, source_target_pairs={{0,2},{2,0},{4,6},{6,4},{8,10},{10,8},{12,14},{14,12},{16,18},{18,... | collective-permute-start | bytes 1572872 | tf_op jit(solution)/shard_map/ppermute | solution.py:582
  75.0 27.7 %all-to-all-start.3 = ((bf16[8,64,512]{2,1,0:T(8,128)(2,1)}), bf16[8,64,512]{2,1,0:T(8,128)(2,1)S(1)}, u32[]{:S(2)}, u32[]{:S(2)}) async-start(bf16[8,64,512]{2,1,0:T(8,128)(2,1)} %add_convert_fusion), calls=%async_computation.3 | async-start | bytes 1048576 | tf_op jit(solution)/shard_map/all_to_all | solution.py:509
  80.9 10.9 %collective-permute-start.3 = (bf16[2,64,512]{2,1,0:T(8,128)(2,1)S(1)}, bf16[2,64,512]{2,1,0:T(8,128)(2,1)S(1)}, u32[]{:S(2)}, u32[]{:S(2)}) collective-permute-start(bf16[2,64,512]{2,1,0:T(8,128)(2,1)S(1)} %get-tuple-element.45), channel_id=1, source_target_pairs={{0,32},{32,0},{64,96},{96,64},{128,160},{160,128},{192,224},{224,1... | collective-permute-start | bytes 393224 | tf_op jit(solution)/shard_map/ppermute | solution.py:595
  85.6 7.5 %collective-permute-start.4 = (bf16[2,64,512]{2,1,0:T(8,128)(2,1)S(1)}, bf16[2,64,512]{2,1,0:T(8,128)(2,1)S(1)}, u32[]{:S(2)}, u32[]{:S(2)}) collective-permute-start(bf16[2,64,512]{2,1,0:T(8,128)(2,1)S(1)} %get-tuple-element.46), channel_id=1, source_target_pairs={{0,64},{32,96},{64,128},{96,160},{128,192},{160,224},{192,0},{224,... | collective-permute-start | bytes 393224 | tf_op jit(solution)/shard_map/ppermute | solution.py:595
  86.9 8.3 %collective-permute-start.5 = (bf16[2,64,512]{2,1,0:T(8,128)(2,1)S(1)}, bf16[2,64,512]{2,1,0:T(8,128)(2,1)S(1)}, u32[]{:S(2)}, u32[]{:S(2)}) collective-permute-start(bf16[2,64,512]{2,1,0:T(8,128)(2,1)S(1)} %get-tuple-element.47), channel_id=1, source_target_pairs={{0,96},{32,64},{64,160},{96,128},{128,224},{160,192},{192,32},{224... | collective-permute-start | bytes 393224 | tf_op jit(solution)/shard_map/ppermute | solution.py:595
  88.4 10.3 %collective-permute-start.6 = (bf16[2,64,512]{2,1,0:T(8,128)(2,1)S(1)}, bf16[2,64,512]{2,1,0:T(8,128)(2,1)S(1)}, u32[]{:S(2)}, u32[]{:S(2)}) collective-permute-start(bf16[2,64,512]{2,1,0:T(8,128)(2,1)S(1)} %get-tuple-element.48), channel_id=1, source_target_pairs={{0,128},{32,160},{64,192},{96,224},{128,0},{160,32},{192,64},{224,... | collective-permute-start | bytes 393224 | tf_op jit(solution)/shard_map/ppermute | solution.py:595
  89.7 11.9 %collective-permute-start.7 = (bf16[2,64,512]{2,1,0:T(8,128)(2,1)S(1)}, bf16[2,64,512]{2,1,0:T(8,128)(2,1)S(1)}, u32[]{:S(2)}, u32[]{:S(2)}) collective-permute-start(bf16[2,64,512]{2,1,0:T(8,128)(2,1)S(1)} %get-tuple-element.49), channel_id=1, source_target_pairs={{0,160},{32,128},{64,224},{96,192},{128,32},{160,0},{192,96},{224,... | collective-permute-start | bytes 393224 | tf_op jit(solution)/shard_map/ppermute | solution.py:595
  91.7 10.0 %collective-permute-start.8 = (bf16[2,64,512]{2,1,0:T(8,128)(2,1)S(1)}, bf16[2,64,512]{2,1,0:T(8,128)(2,1)S(1)}, u32[]{:S(2)}, u32[]{:S(2)}) collective-permute-start(bf16[2,64,512]{2,1,0:T(8,128)(2,1)S(1)} %get-tuple-element.50), channel_id=1, source_target_pairs={{0,192},{32,224},{64,0},{96,32},{128,64},{160,96},{192,128},{224,1... | collective-permute-start | bytes 393224 | tf_op jit(solution)/shard_map/ppermute | solution.py:595
  93.1 9.5 %collective-permute-start.9 = (bf16[2,64,512]{2,1,0:T(8,128)(2,1)S(1)}, bf16[2,64,512]{2,1,0:T(8,128)(2,1)S(1)}, u32[]{:S(2)}, u32[]{:S(2)}) collective-permute-start(bf16[2,64,512]{2,1,0:T(8,128)(2,1)S(1)} %get-tuple-element.51), channel_id=1, source_target_pairs={{0,224},{32,192},{64,32},{96,0},{128,96},{160,64},{192,160},{224,1... | collective-permute-start | bytes 393224 | tf_op jit(solution)/shard_map/ppermute | solution.py:595
  104.0 19.6 %all-to-all-start.4 = ((bf16[8,2,64,512]{3,2,1,0:T(8,128)(2,1)}), bf16[8,2,64,512]{3,2,1,0:T(8,128)(2,1)S(1)}, u32[]{:S(2)}, u32[]{:S(2)}) async-start(bf16[8,2,64,512]{3,2,1,0:T(8,128)(2,1)} %pick_stacked.1), calls=%async_computation.4 | async-start | bytes 2097152 | tf_op jit(solution)/shard_map/all_to_all | solution.py:509

commit v7 on v6

--- a/solution.py
+++ b/solution.py
@@ -12,7 +12,7 @@
 F32 = jnp.float32
 BF16 = jnp.bfloat16
 TILE = 16
-ORDER = (0, 2, 4, 6, 1, 3, 5, 7)
+ORDER = (0, 4, 1, 5, 2, 6, 3, 7)
 SLOT = tuple(ORDER.index(z) for z in range(len(ORDER)))
 SMALL_VMEM = 8 * 1024 * 1024
 MEDIUM_VMEM = 14 * 1024 * 1024
@@ -89,6 +89,7 @@
     @pl.when(on_core() == 0)
     def _():
         tp = lax.axis_index("tp")
+        own_half(tp, x_ref, weight_hbm, part_ref, weight_ref, weight_sems)
         stores = []
         for at in load_half(1 - tp, weight_hbm, weight_ref, weight_sems):
             turned_ref[:, at] = weight_ref[at].T
@@ -100,7 +101,6 @@
                 )
             )
             stores[-1].start()
-        own_half(tp, x_ref, weight_hbm, part_ref, weight_ref, weight_sems)
         for store in stores:
             store.wait()
 
@@ -567,7 +567,11 @@
         jnp.where(recv_index[:, None] == partner(group, steps, -1)[None, :], steps, 0),
         axis=1,
     )
-    send_index = row_for(steps)
+    order = jnp.array(ORDER, jnp.int32)
+    send_index = row_for(order)
+    recv_index = jnp.sum(
+        jnp.where(recv_index[:, None] == order[None, :], steps[None, :], 0), axis=1
+    )
     send_step = row_for(partner(group, steps, 1))
 
     part_1, turned = project_own(grad, out_weight, turned)
@@ -595,7 +599,7 @@
         got.append(lax.ppermute(sent[i], "dp", route))
     dkv, *got = lax.optimization_barrier((dkv, *got))
     query_out = place_q(recv_step, got)
-    dkv = exchange(pick_stacked(send_index, by_row(dkv)), "dp")
+    dkv = exchange(pick_stacked(send_index, by_row(dkv)), "dp", [list(ORDER)])
     key_out, value_out = place_kv(recv_index, dkv)
     return query_out, key_out, value_out
 

time: 126 us -> 124 us (0.984)
  waiting for transfers between devices: 54.3 us -> 47.2 us
  starting transfers between devices: 49.2 us -> 54.1 us
    all_to_all x5, waiting for transfers between devices: 30.3 us -> 25.5 us  [exchange(): lax.all_to_all(x, axis, split_axis=0, concat_axis=0, tiled=True, axis_ind...]
    ppermute x7, starting transfers between devices: 13.7 us -> 17 us  [on_device(): got.append(lax.ppermute(sent[i], 'dp', route))]
    ppermute x1, waiting for transfers between devices: 8.83 us -> 6.55 us  [on_device(): dkv_back = lax.ppermute(dkv_theirs, 'ctx', swap)]
    all_to_all x5, starting transfers between devices: 27.7 us -> 29.2 us  [exchange(): lax.all_to_all(x, axis, split_axis=0, concat_axis=0, tiled=True, axis_ind...]
  transfers between devices with their start and end apart: 15 -> 15, of which waited for: 10 -> 9; matrix products, arithmetic and copies ran while one was open for 1% -> 1% of each run, Pallas kernels for 8% -> 8%
where the time goes in v7:
time: 124 us; the launch traced here: 123 us
  starting transfers between devices  54.1 us (44%)
  waiting for transfers between devices  47.2 us (38%)
  Pallas kernels  19.4 us (16%)
  other arithmetic  1.44 us (1%)
    all_to_all x5, starting transfers between devices, exchange(): lax.all_to_all(x, axis, split_axis=0, concat_axis=0, tiled=True, axis_ind...  29.2 us
    all_to_all x5, waiting for transfers between devices, exchange(): lax.all_to_all(x, axis, split_axis=0, concat_axis=0, tiled=True, axis_ind...  25.5 us
    ppermute x7, starting transfers between devices, on_device(): got.append(lax.ppermute(sent[i], 'dp', route))  17 us
    ppermute x7, waiting for transfers between devices, on_device(): got.append(lax.ppermute(sent[i], 'dp', route))  8.03 us
    ppermute x1, waiting for transfers between devices, on_device(): other = lax.ppermute(own, 'ctx', swap)  7.14 us
    ppermute x1, waiting for transfers between devices, on_device(): dkv_back = lax.ppermute(dkv_theirs, 'ctx', swap)  6.55 us
    pallas_call x1, Pallas kernels, project_own(): pl.pallas_call(project_own_kernel, in_specs=[VMEM, ANY, ANY], out_specs=[...  6.25 us
    pallas_call x1, Pallas kernels, attention(): pl.pallas_call(attention_kernel, in_specs=[VMEM] * 3, out_specs=[ANY, VME...  3.68 us
  transfers between devices with their start and end apart: 15, of which 9 were waited for; matrix products, arithmetic and copies ran while one was open for 1% of the time, Pallas kernels for 8%

profile of v7, /device:TPU:1, one launch (start us, length us, event | category | flops | bytes accessed | tf_op | source)
XLA Modules:
  0.0 123.1 jit_solution(3207277232560984847)
XLA Ops:
  0.6 2.4 %begin.1 = (bf16[8,16,2176]{2,1,0:T(8,128)(2,1)}, bf16[4,64,1792]{2,1,0:T(8,128)(2,1)S(1)}, f32[256,1024]{1,0:T(8,128)S(1)}, bf16[1792,1024]{1,0:T(8,128)(2,1)}) custom-call(s32[4,64]{1,0:T(4,128)} %seg_hbm.1, bf16[4,64,512]{2,1,0:T(8,128)(2,1)} %k_hbm.1, bf16[4,64,512]{2,1,0:T(8,128)(2,1)} %v_hbm.1, bf16[4,64,1792]{2,1,0:T(8,128)(2,1)} %x_hbm.1, ...), custom_call_target="tpu_custom_call" | custom-call | tf_op jit(solution)/shard_map/begin/pallas_call | solution.py:143
  3.1 2.1 %collective-permute-start.1 = (bf16[4,64,1792]{2,1,0:T(8,128)(2,1)S(1)}, bf16[4,64,1792]{2,1,0:T(8,128)(2,1)S(1)}, u32[]{:S(2)}, u32[]{:S(2)}) collective-permute-start(bf16[4,64,1792]{2,1,0:T(8,128)(2,1)S(1)} %get-tuple-element.34.x_ref), channel_id=1, source_target_pairs={{0,1},{1,0},{2,3},{3,2},{4,5},{5,4},{6,7},{7,6},{8,9},{9,8},{10,11... | collective-permute-start | bytes 2752520 | tf_op jit(solution)/shard_map/ppermute | solution.py:532
  5.2 8.2 %all-to-all-start = ((bf16[8,16,2176]{2,1,0:T(8,128)(2,1)}), bf16[8,16,2176]{2,1,0:T(8,128)(2,1)S(1)}, u32[]{:S(2)}, u32[]{:S(2)}) async-start(bf16[8,16,2176]{2,1,0:T(8,128)(2,1)} %get-tuple-element.33), calls=%async_computation | async-start | bytes 1114112 | tf_op jit(solution)/shard_map/all_to_all | solution.py:509
  13.4 0.0 copy-start
  13.4 6.2 %project_own.1 = (f32[256,1024]{1,0:T(8,128)S(1)}, bf16[1792,1024]{1,0:T(8,128)(2,1)S(1)}) custom-call(bf16[4,64,1792]{2,1,0:T(8,128)(2,1)S(1)} %get-tuple-element.34.x_ref, bf16[1024,3584]{1,0:T(8,128)(2,1)} %weight_hbm.3, bf16[1792,1024]{1,0:T(8,128)(2,1)} %get-tuple-element.36.turned_hbm), custom_call_target="tpu_custom_call" | custom-call | flops 939524096 | bytes 7340032 | tf_op jit(solution)/shard_map/project_own/pallas_call | solution.py:187
  19.6 0.0 collective-permute-done.1.x_ref
  19.6 0.0 copy-done
  19.7 2.1 %project_other.1 = bf16[4,2,64,1024]{3,2,1,0:T(8,128)(2,1)} custom-call(bf16[4,64,1792]{2,1,0:T(8,128)(2,1)S(1)} %collective-permute-done.1.x_ref, bf16[4,64,1024]{2,1,0:T(8,128)(2,1)S(1)} %copy-done, f32[256,1024]{1,0:T(8,128)S(1)} %get-tuple-element.35.part_0, f32[256,1024]{1,0:T(8,128)S(1)} %get-tuple-element.37.part_1, ...), custom_call_target="tpu_custom_call" | custom-call | flops 939524096 | bytes 3670016 | tf_op jit(solution)/shard_map/project_other/pallas_call | solution.py:225
  21.8 0.8 all-to-all-done.own_ref
  22.5 5.9 %all-to-all-start.1 = ((bf16[8,64,1024]{2,1,0:T(8,128)(2,1)}), bf16[8,64,1024]{2,1,0:T(8,128)(2,1)S(1)}, u32[]{:S(2)}, u32[]{:S(2)}) async-start(bf16[8,64,1024]{2,1,0:T(8,128)(2,1)} %bitcast.7), calls=%async_computation.1 | async-start | bytes 2097152 | tf_op jit(solution)/shard_map/all_to_all | solution.py:509
  28.4 0.0 copy-start.1
  28.4 2.8 %collective-permute-start = (bf16[8,16,2176]{2,1,0:T(8,128)(2,1)S(1)}, bf16[8,16,2176]{2,1,0:T(8,128)(2,1)S(1)}, u32[]{:S(2)}, u32[]{:S(2)}) collective-permute-start(bf16[8,16,2176]{2,1,0:T(8,128)(2,1)S(1)} %all-to-all-done.own_ref), channel_id=1, source_target_pairs={{0,2},{2,0},{4,6},{6,4},{8,10},{10,8},{12,14},{14,12},{16,18},{18,... | collective-permute-start | bytes 1671176 | tf_op jit(solution)/shard_map/ppermute | solution.py:534
  31.3 7.1 %collective-permute-done.other_ref = bf16[8,16,2176]{2,1,0:T(8,128)(2,1)S(1)} collective-permute-done((bf16[8,16,2176]{2,1,0:T(8,128)(2,1)S(1)}, bf16[8,16,2176]{2,1,0:T(8,128)(2,1)S(1)}, u32[]{:S(2)}, u32[]{:S(2)}) %collective-permute-start) | collective-permute-done | bytes 557088 | tf_op jit(solution)/shard_map/ppermute | solution.py:534
  38.4 11.6 %all-to-all-done.1.qd_ref = bf16[8,64,1024]{2,1,0:T(8,128)(2,1)S(1)} async-done(((bf16[8,64,1024]{2,1,0:T(8,128)(2,1)}), bf16[8,64,1024]{2,1,0:T(8,128)(2,1)S(1)}, u32[]{:S(2)}, u32[]{:S(2)}) %all-to-all-start.1) | async-done | bytes 1048608 | tf_op jit(solution)/shard_map/all_to_all | solution.py:509
  49.9 3.7 %attend.1 = (bf16[8,64,512]{2,1,0:T(8,128)(2,1)}, bf16[8,64,512]{2,1,0:T(8,128)(2,1)S(1)}, bf16[8,64,512]{2,1,0:T(8,128)(2,1)S(1)}) custom-call(bf16[8,16,2176]{2,1,0:T(8,128)(2,1)S(1)} %all-to-all-done.own_ref, bf16[8,16,2176]{2,1,0:T(8,128)(2,1)S(1)} %collective-permute-done.other_ref, bf16[8,64,1024]{2,1,0:T(8,128)(2,1)S(1)} %all-to-all-done.1.qd_ref), custom_call_target="tpu_custom_call" | custom-call | flops 3000000000 | bytes 6291456 | tf_op jit(solution)/shard_map/attend/pallas_call | solution.py:365
  53.6 0.0 copy-start.2
  53.6 3.7 %all-to-all-start.2 = ((bf16[8,64,512]{2,1,0:T(8,128)(2,1)}), bf16[8,64,512]{2,1,0:T(8,128)(2,1)S(1)}, u32[]{:S(2)}, u32[]{:S(2)}) async-start(bf16[8,64,512]{2,1,0:T(8,128)(2,1)} %get-tuple-element.41), calls=%async_computation.2 | async-start | bytes 1048576 | tf_op jit(solution)/shard_map/all_to_all | solution.py:509
  57.3 2.9 %collective-permute-start.2 = (bf16[8,64,512]{2,1,0:T(8,128)(2,1)S(1)}, bf16[8,64,512]{2,1,0:T(8,128)(2,1)S(1)}, u32[]{:S(2)}, u32[]{:S(2)}) collective-permute-start(bf16[8,64,512]{2,1,0:T(8,128)(2,1)S(1)} %get-tuple-element.40), channel_id=1, source_target_pairs={{0,2},{2,0},{4,6},{6,4},{8,10},{10,8},{12,14},{14,12},{16,18},{18,... | collective-permute-start | bytes 1572872 | tf_op jit(solution)/shard_map/ppermute | solution.py:586
  60.2 0.0 copy-done.1
  60.2 0.1 reshape.151
  60.3 6.5 %collective-permute-done.2 = bf16[8,64,512]{2,1,0:T(8,128)(2,1)S(1)} collective-permute-done((bf16[8,64,512]{2,1,0:T(8,128)(2,1)S(1)}, bf16[8,64,512]{2,1,0:T(8,128)(2,1)S(1)}, u32[]{:S(2)}, u32[]{:S(2)}) %collective-permute-start.2) | collective-permute-done | bytes 524320 | tf_op jit(solution)/shard_map/ppermute | solution.py:586
  66.9 0.9 add_convert_fusion
  67.8 0.0 all-to-all-done.2
  67.8 6.9 %all-to-all-start.3 = ((bf16[8,64,512]{2,1,0:T(8,128)(2,1)}), bf16[8,64,512]{2,1,0:T(8,128)(2,1)S(1)}, u32[]{:S(2)}, u32[]{:S(2)}) async-start(bf16[8,64,512]{2,1,0:T(8,128)(2,1)} %add_convert_fusion), calls=%async_computation.3 | async-start | bytes 1048576 | tf_op jit(solution)/shard_map/all_to_all | solution.py:509
  74.8 0.0 copy-done.2
  74.8 0.1 select_reduce_fusion
  74.9 0.6 pick.1
  75.5 8.0 %collective-permute-start.3 = (bf16[2,64,512]{2,1,0:T(8,128)(2,1)S(1)}, bf16[2,64,512]{2,1,0:T(8,128)(2,1)S(1)}, u32[]{:S(2)}, u32[]{:S(2)}) collective-permute-start(bf16[2,64,512]{2,1,0:T(8,128)(2,1)S(1)} %get-tuple-element.45), channel_id=1, source_target_pairs={{0,32},{32,0},{64,96},{96,64},{128,160},{160,128},{192,224},{224,1... | collective-permute-start | bytes 393224 | tf_op jit(solution)/shard_map/ppermute | solution.py:599
  83.5 1.3 %collective-permute-start.4 = (bf16[2,64,512]{2,1,0:T(8,128)(2,1)S(1)}, bf16[2,64,512]{2,1,0:T(8,128)(2,1)S(1)}, u32[]{:S(2)}, u32[]{:S(2)}) collective-permute-start(bf16[2,64,512]{2,1,0:T(8,128)(2,1)S(1)} %get-tuple-element.46), channel_id=1, source_target_pairs={{0,64},{32,96},{64,128},{96,160},{128,192},{160,224},{192,0},{224,... | collective-permute-start | bytes 393224 | tf_op jit(solution)/shard_map/ppermute | solution.py:599
  84.8 1.5 %collective-permute-start.5 = (bf16[2,64,512]{2,1,0:T(8,128)(2,1)S(1)}, bf16[2,64,512]{2,1,0:T(8,128)(2,1)S(1)}, u32[]{:S(2)}, u32[]{:S(2)}) collective-permute-start(bf16[2,64,512]{2,1,0:T(8,128)(2,1)S(1)} %get-tuple-element.47), channel_id=1, source_target_pairs={{0,96},{32,64},{64,160},{96,128},{128,224},{160,192},{192,32},{224... | collective-permute-start | bytes 393224 | tf_op jit(solution)/shard_map/ppermute | solution.py:599
  86.3 1.3 %collective-permute-start.6 = (bf16[2,64,512]{2,1,0:T(8,128)(2,1)S(1)}, bf16[2,64,512]{2,1,0:T(8,128)(2,1)S(1)}, u32[]{:S(2)}, u32[]{:S(2)}) collective-permute-start(bf16[2,64,512]{2,1,0:T(8,128)(2,1)S(1)} %get-tuple-element.48), channel_id=1, source_target_pairs={{0,128},{32,160},{64,192},{96,224},{128,0},{160,32},{192,64},{224,... | collective-permute-start | bytes 393224 | tf_op jit(solution)/shard_map/ppermute | solution.py:599
  87.6 2.0 %collective-permute-start.7 = (bf16[2,64,512]{2,1,0:T(8,128)(2,1)S(1)}, bf16[2,64,512]{2,1,0:T(8,128)(2,1)S(1)}, u32[]{:S(2)}, u32[]{:S(2)}) collective-permute-start(bf16[2,64,512]{2,1,0:T(8,128)(2,1)S(1)} %get-tuple-element.49), channel_id=1, source_target_pairs={{0,160},{32,128},{64,224},{96,192},{128,32},{160,0},{192,96},{224,... | collective-permute-start | bytes 393224 | tf_op jit(solution)/shard_map/ppermute | solution.py:599
  89.6 0.0 collective-permute-done.3.refs_1_
  89.6 1.4 %collective-permute-start.8 = (bf16[2,64,512]{2,1,0:T(8,128)(2,1)S(1)}, bf16[2,64,512]{2,1,0:T(8,128)(2,1)S(1)}, u32[]{:S(2)}, u32[]{:S(2)}) collective-permute-start(bf16[2,64,512]{2,1,0:T(8,128)(2,1)S(1)} %get-tuple-element.50), channel_id=1, source_target_pairs={{0,192},{32,224},{64,0},{96,32},{128,64},{160,96},{192,128},{224,1... | collective-permute-start | bytes 393224 | tf_op jit(solution)/shard_map/ppermute | solution.py:599
  91.0 0.0 collective-permute-done.4.refs_2_
  91.0 1.5 %collective-permute-start.9 = (bf16[2,64,512]{2,1,0:T(8,128)(2,1)S(1)}, bf16[2,64,512]{2,1,0:T(8,128)(2,1)S(1)}, u32[]{:S(2)}, u32[]{:S(2)}) collective-permute-start(bf16[2,64,512]{2,1,0:T(8,128)(2,1)S(1)} %get-tuple-element.51), channel_id=1, source_target_pairs={{0,224},{32,192},{64,32},{96,0},{128,96},{160,64},{192,160},{224,1... | collective-permute-start | bytes 393224 | tf_op jit(solution)/shard_map/ppermute | solution.py:599
  92.5 0.3 collective-permute-done.5.refs_3_
  92.8 3.8 %collective-permute-done.6.refs_4_ = bf16[2,64,512]{2,1,0:T(8,128)(2,1)S(1)} collective-permute-done((bf16[2,64,512]{2,1,0:T(8,128)(2,1)S(1)}, bf16[2,64,512]{2,1,0:T(8,128)(2,1)S(1)}, u32[]{:S(2)}, u32[]{:S(2)}) %collective-permute-start.6) | collective-permute-done | bytes 131104 | tf_op jit(solution)/shard_map/ppermute | solution.py:599
  96.6 3.0 %collective-permute-done.7.refs_5_ = bf16[2,64,512]{2,1,0:T(8,128)(2,1)S(1)} collective-permute-done((bf16[2,64,512]{2,1,0:T(8,128)(2,1)S(1)}, bf16[2,64,512]{2,1,0:T(8,128)(2,1)S(1)}, u32[]{:S(2)}, u32[]{:S(2)}) %collective-permute-start.7) | collective-permute-done | bytes 131104 | tf_op jit(solution)/shard_map/ppermute | solution.py:599
  99.6 0.0 collective-permute-done.8.refs_6_
  99.6 0.9 collective-permute-done.9.refs_7_
  100.5 0.0 all-to-all-done.3
  100.5 1.4 %pick_stacked.1 = bf16[8,2,64,512]{3,2,1,0:T(8,128)(2,1)} custom-call(s32[8]{0:T(128)S(1)} %broadcast_add_fusion.index_ref, bf16[4,2,64,512]{3,2,1,0:T(8,128)(2,1)S(1)} %bitcast.6), custom_call_target="tpu_custom_call" | custom-call | tf_op jit(solution)/shard_map/pick_stacked/pallas_call | solution.py:432
  102.0 4.5 %all-to-all-start.4 = ((bf16[8,2,64,512]{3,2,1,0:T(8,128)(2,1)}), bf16[8,2,64,512]{3,2,1,0:T(8,128)(2,1)S(1)}, u32[]{:S(2)}, u32[]{:S(2)}) async-start(bf16[8,2,64,512]{3,2,1,0:T(8,128)(2,1)} %pick_stacked.1), calls=%async_computation.4 | async-start | bytes 2097152 | tf_op jit(solution)/shard_map/all_to_all | solution.py:509
  106.5 0.2 select_reduce_fusion.4
  106.7 0.2 select_reduce_fusion.1
  106.9 1.4 %place_q.1 = bf16[4,64,1024]{2,1,0:T(8,128)(2,1)} custom-call(s32[4]{0:T(128)S(1)} %get-tuple-element.66.index_ref, bf16[2,64,512]{2,1,0:T(8,128)(2,1)S(1)} %get-tuple-element.52.refs_0_, bf16[2,64,512]{2,1,0:T(8,128)(2,1)S(1)} %collective-permute-done.3.refs_1_, bf16[2,64,512]{2,1,0:T(8,128)(2,1)S(1)} %collective-permute-done.4.refs_2_, ...), custom_call_target="tpu_custom_call" | custom-call | tf_op jit(solution)/shard_map/place_q/pallas_call | solution.py:468
  108.3 13.2 %all-to-all-done.4.in_ref = bf16[8,2,64,512]{3,2,1,0:T(8,128)(2,1)S(1)} async-done(((bf16[8,2,64,512]{3,2,1,0:T(8,128)(2,1)}), bf16[8,2,64,512]{3,2,1,0:T(8,128)(2,1)S(1)}, u32[]{:S(2)}, u32[]{:S(2)}) %all-to-all-start.4) | async-done | bytes 1048608 | tf_op jit(solution)/shard_map/all_to_all | solution.py:509
  121.5 1.5 %place_kv.1 = (bf16[4,64,512]{2,1,0:T(8,128)(2,1)}, bf16[4,64,512]{2,1,0:T(8,128)(2,1)}) custom-call(s32[4]{0:T(128)S(1)} %get-tuple-element.65.index_ref, bf16[8,2,64,512]{3,2,1,0:T(8,128)(2,1)S(1)} %all-to-all-done.4.in_ref), custom_call_target="tpu_custom_call" | custom-call | tf_op jit(solution)/shard_map/place_kv/pallas_call | solution.py:497
  (7 shorter events, 0.0 us)
Async XLA Ops:
  3.1 16.6 %collective-permute-start.1 = (bf16[4,64,1792]{2,1,0:T(8,128)(2,1)S(1)}, bf16[4,64,1792]{2,1,0:T(8,128)(2,1)S(1)}, u32[]{:S(2)}, u32[]{:S(2)}) collective-permute-start(bf16[4,64,1792]{2,1,0:T(8,128)(2,1)S(1)} %get-tuple-element.34.x_ref), channel_id=1, source_target_pairs={{0,1},{1,0},{2,3},{3,2},{4,5},{5,4},{6,7},{7,6},{8,9},{9,8},{10,11... | collective-permute-start | bytes 2752520 | tf_op jit(solution)/shard_map/ppermute | solution.py:532
  5.2 17.3 %all-to-all-start = ((bf16[8,16,2176]{2,1,0:T(8,128)(2,1)}), bf16[8,16,2176]{2,1,0:T(8,128)(2,1)S(1)}, u32[]{:S(2)}, u32[]{:S(2)}) async-start(bf16[8,16,2176]{2,1,0:T(8,128)(2,1)} %get-tuple-element.33), calls=%async_computation | async-start | bytes 1114112 | tf_op jit(solution)/shard_map/all_to_all | solution.py:509
  13.4 6.3 %copy-start = (bf16[4,64,1024]{2,1,0:T(8,128)(2,1)S(1)}, bf16[4,64,1024]{2,1,0:T(8,128)(2,1)}, u32[]{:S(2)}) copy-start(bf16[4,64,1024]{2,1,0:T(8,128)(2,1)} %q_ref.1) | copy-start | bytes 1572868
  22.5 27.4 %all-to-all-start.1 = ((bf16[8,64,1024]{2,1,0:T(8,128)(2,1)}), bf16[8,64,1024]{2,1,0:T(8,128)(2,1)S(1)}, u32[]{:S(2)}, u32[]{:S(2)}) async-start(bf16[8,64,1024]{2,1,0:T(8,128)(2,1)} %bitcast.7), calls=%async_computation.1 | async-start | bytes 2097152 | tf_op jit(solution)/shard_map/all_to_all | solution.py:509
  28.4 31.8 %copy-start.1 = (s32[32]{0:T(128)S(1)}, s32[32]{0:T(128)}, u32[]{:S(2)}) copy-start(s32[32]{0:T(128)} %param.14) | copy-start | bytes 388
  28.4 10.0 %collective-permute-start = (bf16[8,16,2176]{2,1,0:T(8,128)(2,1)S(1)}, bf16[8,16,2176]{2,1,0:T(8,128)(2,1)S(1)}, u32[]{:S(2)}, u32[]{:S(2)}) collective-permute-start(bf16[8,16,2176]{2,1,0:T(8,128)(2,1)S(1)} %all-to-all-done.own_ref), channel_id=1, source_target_pairs={{0,2},{2,0},{4,6},{6,4},{8,10},{10,8},{12,14},{14,12},{16,18},{18,... | collective-permute-start | bytes 1671176 | tf_op jit(solution)/shard_map/ppermute | solution.py:534
  53.6 21.1 %copy-start.2 = (s32[8]{0:T(128)S(1)}, s32[8]{0:T(128)}, u32[]{:S(2)}) copy-start(s32[8]{0:T(128)} %constant.111.clone) | copy-start | bytes 100
  53.6 14.1 %all-to-all-start.2 = ((bf16[8,64,512]{2,1,0:T(8,128)(2,1)}), bf16[8,64,512]{2,1,0:T(8,128)(2,1)S(1)}, u32[]{:S(2)}, u32[]{:S(2)}) async-start(bf16[8,64,512]{2,1,0:T(8,128)(2,1)} %get-tuple-element.41), calls=%async_computation.2 | async-start | bytes 1048576 | tf_op jit(solution)/shard_map/all_to_all | solution.py:509
  57.3 9.5 %collective-permute-start.2 = (bf16[8,64,512]{2,1,0:T(8,128)(2,1)S(1)}, bf16[8,64,512]{2,1,0:T(8,128)(2,1)S(1)}, u32[]{:S(2)}, u32[]{:S(2)}) collective-permute-start(bf16[8,64,512]{2,1,0:T(8,128)(2,1)S(1)} %get-tuple-element.40), channel_id=1, source_target_pairs={{0,2},{2,0},{4,6},{6,4},{8,10},{10,8},{12,14},{14,12},{16,18},{18,... | collective-permute-start | bytes 1572872 | tf_op jit(solution)/shard_map/ppermute | solution.py:586
  67.8 32.7 %all-to-all-start.3 = ((bf16[8,64,512]{2,1,0:T(8,128)(2,1)}), bf16[8,64,512]{2,1,0:T(8,128)(2,1)S(1)}, u32[]{:S(2)}, u32[]{:S(2)}) async-start(bf16[8,64,512]{2,1,0:T(8,128)(2,1)} %add_convert_fusion), calls=%async_computation.3 | async-start | bytes 1048576 | tf_op jit(solution)/shard_map/all_to_all | solution.py:509
  75.5 14.1 %collective-permute-start.3 = (bf16[2,64,512]{2,1,0:T(8,128)(2,1)S(1)}, bf16[2,64,512]{2,1,0:T(8,128)(2,1)S(1)}, u32[]{:S(2)}, u32[]{:S(2)}) collective-permute-start(bf16[2,64,512]{2,1,0:T(8,128)(2,1)S(1)} %get-tuple-element.45), channel_id=1, source_target_pairs={{0,32},{32,0},{64,96},{96,64},{128,160},{160,128},{192,224},{224,1... | collective-permute-start | bytes 393224 | tf_op jit(solution)/shard_map/ppermute | solution.py:599
  83.5 7.5 %collective-permute-start.4 = (bf16[2,64,512]{2,1,0:T(8,128)(2,1)S(1)}, bf16[2,64,512]{2,1,0:T(8,128)(2,1)S(1)}, u32[]{:S(2)}, u32[]{:S(2)}) collective-permute-start(bf16[2,64,512]{2,1,0:T(8,128)(2,1)S(1)} %get-tuple-element.46), channel_id=1, source_target_pairs={{0,64},{32,96},{64,128},{96,160},{128,192},{160,224},{192,0},{224,... | collective-permute-start | bytes 393224 | tf_op jit(solution)/shard_map/ppermute | solution.py:599
  84.8 8.0 %collective-permute-start.5 = (bf16[2,64,512]{2,1,0:T(8,128)(2,1)S(1)}, bf16[2,64,512]{2,1,0:T(8,128)(2,1)S(1)}, u32[]{:S(2)}, u32[]{:S(2)}) collective-permute-start(bf16[2,64,512]{2,1,0:T(8,128)(2,1)S(1)} %get-tuple-element.47), channel_id=1, source_target_pairs={{0,96},{32,64},{64,160},{96,128},{128,224},{160,192},{192,32},{224... | collective-permute-start | bytes 393224 | tf_op jit(solution)/shard_map/ppermute | solution.py:599
  86.3 10.3 %collective-permute-start.6 = (bf16[2,64,512]{2,1,0:T(8,128)(2,1)S(1)}, bf16[2,64,512]{2,1,0:T(8,128)(2,1)S(1)}, u32[]{:S(2)}, u32[]{:S(2)}) collective-permute-start(bf16[2,64,512]{2,1,0:T(8,128)(2,1)S(1)} %get-tuple-element.48), channel_id=1, source_target_pairs={{0,128},{32,160},{64,192},{96,224},{128,0},{160,32},{192,64},{224,... | collective-permute-start | bytes 393224 | tf_op jit(solution)/shard_map/ppermute | solution.py:599
  87.6 11.9 %collective-permute-start.7 = (bf16[2,64,512]{2,1,0:T(8,128)(2,1)S(1)}, bf16[2,64,512]{2,1,0:T(8,128)(2,1)S(1)}, u32[]{:S(2)}, u32[]{:S(2)}) collective-permute-start(bf16[2,64,512]{2,1,0:T(8,128)(2,1)S(1)} %get-tuple-element.49), channel_id=1, source_target_pairs={{0,160},{32,128},{64,224},{96,192},{128,32},{160,0},{192,96},{224,... | collective-permute-start | bytes 393224 | tf_op jit(solution)/shard_map/ppermute | solution.py:599
  89.6 10.0 %collective-permute-start.8 = (bf16[2,64,512]{2,1,0:T(8,128)(2,1)S(1)}, bf16[2,64,512]{2,1,0:T(8,128)(2,1)S(1)}, u32[]{:S(2)}, u32[]{:S(2)}) collective-permute-start(bf16[2,64,512]{2,1,0:T(8,128)(2,1)S(1)} %get-tuple-element.50), channel_id=1, source_target_pairs={{0,192},{32,224},{64,0},{96,32},{128,64},{160,96},{192,128},{224,1... | collective-permute-start | bytes 393224 | tf_op jit(solution)/shard_map/ppermute | solution.py:599
  91.0 9.5 %collective-permute-start.9 = (bf16[2,64,512]{2,1,0:T(8,128)(2,1)S(1)}, bf16[2,64,512]{2,1,0:T(8,128)(2,1)S(1)}, u32[]{:S(2)}, u32[]{:S(2)}) collective-permute-start(bf16[2,64,512]{2,1,0:T(8,128)(2,1)S(1)} %get-tuple-element.51), channel_id=1, source_target_pairs={{0,224},{32,192},{64,32},{96,0},{128,96},{160,64},{192,160},{224,1... | collective-permute-start | bytes 393224 | tf_op jit(solution)/shard_map/ppermute | solution.py:599
  102.0 19.5 %all-to-all-start.4 = ((bf16[8,2,64,512]{3,2,1,0:T(8,128)(2,1)}), bf16[8,2,64,512]{3,2,1,0:T(8,128)(2,1)S(1)}, u32[]{:S(2)}, u32[]{:S(2)}) async-start(bf16[8,2,64,512]{3,2,1,0:T(8,128)(2,1)} %pick_stacked.1), calls=%async_computation.4 | async-start | bytes 2097152 | tf_op jit(solution)/shard_map/all_to_all | solution.py:509
